TPU v7x, 32 devices: a whole 2x2x4 slice. The times are simulated.
32 devices in a mesh: front: 4 (over y, x), row: 2 (over core), col: 4 (over z).
Axes of the slice: x: 2, y: 2, z: 4, core: 2. Of those that a mesh axis runs over, the one named last changes fastest.
Arguments:
- front: bfloat16 [4, 12288, 12288], P('front', 'row', 'col'), may hold values from -6 to 6
- panel: bfloat16 [4, 12288, 512], P('front', ('row', 'col')), may hold values from -8 to 8
- inverse: bfloat16 [4, 512, 512], P('front'), may hold values from -0.0046 to 0.056
- fill: int32 [4, 48], P('front'), may hold values 0 or 1
- block_map: int32 [4, 48], P('front'), may hold values from 0 to 47, as said below
- parent_front: bfloat16 [4, 6144, 12288], P('front', 'row', 'col'), may hold values from -6 to 6
Outputs:
- factor_rows: bfloat16 [4, 12288, 512], P('front', ('row', 'col'))
- parent: float32 [4, 6144, 12288], P('front', 'row', 'col')
Inputs may be any that keep to these rules, and one draw needn't show every extreme that they name: `block_map`: each front's map is a permutation of its blocks that keeps every aligned group of 12 blocks in place as a group.
All inputs are finite; a program needn't handle non-finite values. No bound on the sum of `fill` on one device may be relied on, other than what follows from the above.
Results may differ from a plain program's by a relative error of at most 0.0025.
Values may be sent and summed in bfloat16 or wider, within the bound.
No kernel may reach another device: no remote copies, remote signals or barrier semaphores. Data moves between devices by JAX's collectives and lax.ppermute only.
A program may use at most 320 MiB of HBM per device.

v0:
```python
import jax
import jax.numpy as jnp
from jax import lax
from jax.sharding import PartitionSpec as P

BLK = 256


def from_partner(block, axis, distance):
    count = lax.axis_size(axis)
    route = []
    for low in range(count):
        high = low | 1 << distance
        if high != low and high < count:
            route += [(low, high), (high, low)]
    return lax.ppermute(block, axis, route)


def block_inverse(mapping, block_total):
    target = jnp.arange(block_total, dtype=jnp.int32)
    matches = (mapping[:, None] == target[None, :]).astype(jnp.int32)
    return jnp.sum(matches * target[:, None], axis=0)


def shards(front, panel, inverse, fill, block_map, parent_front):
    col_count = lax.axis_size("col")
    row_index = lax.axis_index("row")
    col_index = lax.axis_index("col")
    local_rows = panel.shape[1]
    tile_rows = front.shape[1]
    tile_cols = front.shape[2]
    block_total = fill.shape[1]
    first_row = (row_index * col_count + col_index) * local_rows
    positions = (first_row + jnp.arange(local_rows, dtype=jnp.int32)) // BLK
    blocks = jnp.arange(block_total, dtype=jnp.int32)
    row_fill = jnp.sum(
        (positions[:, None] == blocks[None, :]).astype(jnp.int32) * fill[0][None, :], axis=1
    )
    masked = panel[0] * row_fill[:, None].astype(jnp.bfloat16)
    factor = jnp.dot(masked, jnp.triu(inverse[0]), preferred_element_type=jnp.float32).astype(
        jnp.bfloat16
    )
    all_rows = lax.all_gather(factor, ("row", "col"), axis=0, tiled=True)
    row_side = lax.dynamic_slice_in_dim(all_rows, row_index * tile_rows, tile_rows, 0)
    col_side = lax.dynamic_slice_in_dim(all_rows, col_index * tile_cols, tile_cols, 0)
    contract = (((1,), (1,)), ((), ()))
    initial = front[0].astype(jnp.float32)
    row_blocks = tile_rows // BLK
    col_blocks = tile_cols // BLK
    update = lax.dot_general(row_side, col_side, contract, preferred_element_type=jnp.float32)
    schur = initial - update
    source = block_inverse(block_map[0], block_total)
    row_source = (
        lax.dynamic_slice_in_dim(source, row_index * row_blocks, row_blocks, 0)
        - row_index * row_blocks
    )
    col_source = (
        lax.dynamic_slice_in_dim(source, col_index * col_blocks, col_blocks, 0)
        - col_index * col_blocks
    )
    shaped = jnp.take(schur.reshape(row_blocks, BLK, tile_cols), row_source, axis=0)
    shaped = jnp.take(shaped.reshape(tile_rows, col_blocks, BLK), col_source, axis=1)
    contribution = shaped.reshape(tile_rows, tile_cols).astype(jnp.bfloat16)
    half_rows = tile_rows // 2
    parity = lax.axis_index("front") % 2
    kept_half = lax.dynamic_slice_in_dim(contribution, parity * half_rows, half_rows, 0)
    sent_half = lax.dynamic_slice_in_dim(contribution, (1 - parity) * half_rows, half_rows, 0)
    arrived = from_partner(sent_half, "front", 0)
    parent = (
        parent_front[0].astype(jnp.float32)
        + kept_half.astype(jnp.float32)
        + arrived.astype(jnp.float32)
    )
    return (factor[None], parent[None])


def solution(mesh):
    placed = (
        P("front", "row", "col"),
        P("front", ("row", "col"), None),
        P("front", None, None),
        P("front", None),
        P("front", None),
        P("front", "row", "col"),
    )
    return jax.shard_map(
        shards,
        mesh=mesh,
        in_specs=placed,
        out_specs=(P("front", ("row", "col"), None), P("front", "row", "col")),
        check_vma=False,
    )
```

profile of v0, /device:TPU:0, one launch (start us, length us, event | category | flops | bytes accessed | tf_op | source)
XLA Modules:
  0.0 930.2 jit_solution(10558905328028933205)
XLA Ops:
  7.2 0.0 all-gather.2.cloned.1.call-start
  7.3 0.8 select_reduce_fusion
  8.0 3.7 convolution_convert_fusion
  11.8 0.0 all-gather.2.cloned.1.call-update
  11.8 0.7 select_reduce_fusion.1
  12.6 0.1 compare_and_fusion.1
  12.6 0.1 broadcast_in_dim.49
  12.7 0.6 broadcast_in_dim.50
  13.3 0.1 compare_and_fusion
  13.4 0.1 broadcast_in_dim.52
  13.5 117.8 %all-gather.2.cloned.1.call-done = bf16[12288,512]{1,0:T(8,128)(2,1)} async-done(((bf16[1536,512]{1,0:T(8,128)(2,1)}), bf16[12288,512]{1,0:T(8,128)(2,1)}) %all-gather.2.cloned.1.call-update) | async-done | bytes 12582928 | tf_op jit(solution)/shard_map/all_gather | solution.py:43
  131.4 40.2 %convert_subtract_fusion = bf16[6144,3072]{1,0:T(8,128)(2,1)} fusion(bf16[1,6144,3072]{2,1,0:T(8,128)(2,1)} %param.6, bf16[12288,512]{1,0:T(8,128)(2,1)} %all-gather.2.cloned.1.call-done, s32[]{:T(128)S(6)} %select_n.68, s32[]{:T(128)S(6)} %select_n.69), kind=kOutput, calls=%fused_computation.4 | convolution fusion | flops 19383975936 | bytes 84934664 | tf_op jit(solution)/shard_map/dot_general | solution.py:50
  171.6 25.0 %gather_fusion = bf16[24,256,3072]{2,1,0:T(8,128)(2,1)} fusion(bf16[24,256,3072]{2,1,0:T(8,128)(2,1)} %bitcast.30, s32[1024]{0:T(1024)S(1)} %pad_clamp_fusion.1), kind=kCustom, calls=%fused_computation | custom fusion | bytes 75497568 | tf_op jit(solution)/shard_map/jit(_take)/gather | solution.py:61
  196.6 51.3 %copy.14 = bf16[24,256,3072]{1,0,2:T(8,128)(2,1)} copy(bf16[24,256,3072]{2,1,0:T(8,128)(2,1)} %gather_fusion) | data formatting | bytes 75497472 | tf_op jit(solution)/shard_map/jit(_take)/gather | solution.py:61
  247.8 52.6 %gather.13 = bf16[6144,12,256]{0,2,1:T(8,128)(2,1)} reshape(bf16[24,256,3072]{1,0,2:T(8,128)(2,1)} %copy.14) | data formatting | bytes 75497472 | tf_op jit(solution)/shard_map/jit(_take)/gather | solution.py:61
  300.4 25.8 %broadcast_select_fusion = bf16[6144,12,256]{0,2,1:T(8,128)(2,1)} fusion(bf16[6144,12,256]{0,2,1:T(8,128)(2,1)} %gather.13, pred[6144]{0:T(1024)(128)(4,1)S(1)} %broadcast_in_dim.53), kind=kLoop, calls=%fused_computation.10 | loop fusion | flops 18874368 | bytes 75503616 | tf_op jit(solution)/shard_map/jit(_take)/select_n | solution.py:61
  326.3 25.1 %fusion.18 = (bf16[3072,12,256]{0,2,1:T(8,128)(2,1)}, bf16[3072,12,256]{0,2,1:T(8,128)(2,1)}) fusion(bf16[6144,12,256]{0,2,1:T(8,128)(2,1)} %broadcast_select_fusion), kind=kLoop, calls=%fused_computation.45 | loop fusion | bytes 75497472 | tf_op jit(solution)/shard_map/jit(_take)/gather | solution.py:62
  351.4 14.7 %gather_fusion.1 = bf16[12,3072,256]{1,2,0:T(8,128)(2,1)} fusion(bf16[3072,12,256]{0,2,1:T(8,128)(2,1)} %get-tuple-element.12, s32[1024]{0:T(1024)S(1)} %pad_clamp_fusion), kind=kCustom, calls=%fused_computation.1 | custom fusion | bytes 37748784 | tf_op jit(solution)/shard_map/jit(_take)/gather | solution.py:62
  366.1 14.6 %gather_fusion.2 = bf16[12,3072,256]{1,2,0:T(8,128)(2,1)} fusion(bf16[3072,12,256]{0,2,1:T(8,128)(2,1)} %get-tuple-element.13, s32[1024]{0:T(1024)S(1)} %pad_clamp_fusion), kind=kCustom, calls=%fused_computation.2 | custom fusion | bytes 37748784 | tf_op jit(solution)/shard_map/jit(_take)/gather | solution.py:62
  380.7 0.0 copy-start
  380.7 25.7 %pad_maximum_fusion = bf16[6144,12,256]{0,2,1:T(8,128)(2,1)} fusion(bf16[3072,12,256]{0,2,1:T(8,128)(2,1)} %bitcast.29, bf16[3072,12,256]{0,2,1:T(8,128)(2,1)} %bitcast.28), kind=kLoop, calls=%fused_computation.3 | loop fusion | flops 75497472 | bytes 75497472
  406.4 0.0 copy-done
  406.4 25.4 %fusion = bf16[6144,3072]{0,1:T(8,128)(2,1)} fusion(bf16[6144,12,256]{0,2,1:T(8,128)(2,1)} %pad_maximum_fusion, pred[3072]{0:T(1024)(128)(4,1)S(1)} %copy-done), kind=kLoop, calls=%fused_computation.6 | loop fusion | flops 18874368 | bytes 75500544 | tf_op jit(solution)/shard_map/convert_element_type | solution.py:63
  431.8 16.6 %constant_dynamic-slice_fusion = bf16[3072,3072]{0,1:T(8,128)(2,1)} fusion(bf16[6144,3072]{0,1:T(8,128)(2,1)} %fusion, s32[]{:T(128)S(6)} %select_n.74), kind=kLoop, calls=%fused_computation.42 | loop fusion | bytes 37748740 | tf_op jit(solution)/shard_map/dynamic_slice | solution.py:67
  448.4 1.5 collective-permute-start
  449.9 24.7 %copy.13 = bf16[1,3072,3072]{1,2,0:T(8,128)(2,1)} copy(bf16[1,3072,3072]{2,1,0:T(8,128)(2,1)} %param.11) | data formatting | bytes 37748736 | tf_op args[5]
  474.6 379.1 %collective-permute-done = bf16[3072,3072]{0,1:T(8,128)(2,1)} collective-permute-done((bf16[3072,3072]{0,1:T(8,128)(2,1)}, bf16[3072,3072]{0,1:T(8,128)(2,1)}, u32[]{:S(2)}, u32[]{:S(2)}) %collective-permute-start) | collective-permute-done | bytes 18874400 | tf_op jit(solution)/shard_map/ppermute | solution.py:16
  853.7 32.9 %fusion.2 = f32[1,3072,3072]{1,2,0:T(8,128)} fusion(bf16[3072,3072]{0,1:T(8,128)(2,1)} %collective-permute-done, bf16[1,3072,3072]{1,2,0:T(8,128)(2,1)} %copy.13, bf16[6144,3072]{0,1:T(8,128)(2,1)} %fusion, s32[]{:T(128)S(6)} %select_n.73), kind=kLoop, calls=%fused_computation.9 | loop fusion | flops 47185920 | bytes 94371840 | tf_op jit(solution)/shard_map/broadcast_in_dim | solution.py:74
  886.6 36.8 %copy.15 = f32[1,3072,3072]{2,1,0:T(8,128)} copy(f32[1,3072,3072]{1,2,0:T(8,128)} %fusion.2) | data formatting | bytes 75497472
  (6 shorter events, 0.0 us)
Async XLA Ops:
  7.2 124.2 %all-gather.2.cloned.1.call-start = ((), (), s32[]{:S(2)}) async-start(), calls=%async_computation | async-start | bytes 14155776 | tf_op jit(solution)/shard_map/all_gather | solution.py:43
  380.7 25.7 %copy-start = (pred[3072]{0:T(1024)(128)(4,1)S(1)}, pred[3072]{0:T(1024)(128)(4,1)}, u32[]{:S(2)}) copy-start(pred[3072]{0:T(1024)(128)(4,1)} %broadcast_in_dim.50) | copy-start | bytes 9220
  448.4 405.3 %collective-permute-start = (bf16[3072,3072]{0,1:T(8,128)(2,1)}, bf16[3072,3072]{0,1:T(8,128)(2,1)}, u32[]{:S(2)}, u32[]{:S(2)}) collective-permute-start(bf16[3072,3072]{0,1:T(8,128)(2,1)} %constant_dynamic-slice_fusion), channel_id=1, source_target_pairs={{0,8},{8,0},{16,24},{24,16},{1,9},{9,1},{17,25},{25,17},{2,10},{10... | collective-permute-start | bytes 56623112 | tf_op jit(solution)/shard_map/ppermute | solution.py:16
Sparse Core Ops, SparseCore 0:
  11.9 119.4 all-gather.1
where the time goes:
time: 934 us; the launch traced here: 930 us
  waiting for transfers between devices  497 us (53%)
  local copies, waits for them, and re-layouts  262 us (28%)
  other arithmetic  112 us (12%)
  matrix products  43.9 us (5%)
  between operations  14.1 us (2%)
    ppermute x1, waiting for transfers between devices, from_partner(): return lax.ppermute(block, axis, route)  379 us
    gather x3, local copies, waits for them, and re-layouts, shards(): jnp.take(schur.reshape(row_blocks, BLK, tile_cols), row_source, axis=0)  129 us
    all_gather x1, waiting for transfers between devices, shards(): all_rows = lax.all_gather(factor, ('row', 'col'), axis=0, tiled=True)  118 us
    unnamed x4, local copies, waits for them, and re-layouts  61.4 us
    gather x3, local copies, waits for them, and re-layouts, shards(): jnp.take(shaped.reshape(tile_rows, col_blocks, BLK), col_source, axis=1)  54.4 us
    dot_general x1, matrix products, shards(): lax.dot_general(row_side, col_side, contract, preferred_element_type=jnp....  40.2 us
    broadcast_in_dim x1, other arithmetic, shards(): return (factor[None], parent[None])  32.9 us
    select_n x1, other arithmetic, shards(): jnp.take(schur.reshape(row_blocks, BLK, tile_cols), row_source, axis=0)  25.8 us
  transfers between devices with their start and end apart: 2, of which 2 were waited for; matrix products, arithmetic and copies ran while one was open for 3% of the time, Pallas kernels for 0%

commit v1 on v0

v1 whole, which is shorter than its diff:
```python
import functools

import jax
import jax.numpy as jnp
from jax import lax
from jax.experimental import pallas as pl
from jax.experimental.pallas import tpu as pltpu
from jax.sharding import PartitionSpec as P

BLK = 256
NT = (((1,), (1,)), ((), ()))
VMEM_LIMIT = 48 * 1024 * 1024


def block_inverse(mapping):
    block_total = mapping.shape[0]
    target = jnp.arange(block_total, dtype=jnp.int32)
    matches = (mapping[:, None] == target[None, :]).astype(jnp.int32)
    return jnp.sum(matches * target[:, None], axis=0)


def cost(flops, moved):
    return pl.CostEstimate(flops=int(flops), bytes_accessed=int(moved), transcendentals=0)


def update_kernel(unit, stride, offset, rows_ref, fac_ref, front_ref, factor_ref, col_ref, out_ref):
    first = (pl.program_id(1) * stride + offset) * unit
    col = col_ref[pl.ds(pl.multiple_of(first, unit), unit), :]
    product = lax.dot_general(factor_ref[...], col, NT, preferred_element_type=jnp.float32)
    out_ref[...] = (front_ref[...].astype(jnp.float32) - product).astype(jnp.bfloat16)


def updated_blocks(front, rows, factor, factor_rows, col_side, unit, stride, offset, units):
    count = rows.shape[0]
    pivots = factor.shape[1]
    grid_spec = pltpu.PrefetchScalarGridSpec(
        num_scalar_prefetch=2,
        grid=(count, units),
        in_specs=[
            pl.BlockSpec((BLK, unit), lambda i, j, rows, fac: (rows[i], j * stride + offset)),
            pl.BlockSpec((BLK, pivots), lambda i, j, rows, fac: (fac[i], 0)),
            pl.BlockSpec(col_side.shape, lambda i, j, rows, fac: (0, 0)),
        ],
        out_specs=pl.BlockSpec((BLK, unit), lambda i, j, rows, fac: (i, j)),
    )
    return pl.pallas_call(
        functools.partial(update_kernel, unit, stride, offset),
        grid_spec=grid_spec,
        out_shape=jax.ShapeDtypeStruct((count * BLK, units * unit), jnp.bfloat16),
        compiler_params=pltpu.CompilerParams(vmem_limit_bytes=VMEM_LIMIT),
        cost_estimate=cost(
            2 * count * BLK * units * unit * pivots, 4 * count * BLK * units * unit + 2 * col_side.size
        ),
    )(rows, factor_rows, front, factor, col_side)


def pick_kernel(rows_ref, front_ref, out_ref):
    out_ref[...] = front_ref[...]


def picked_blocks(front, rows, unit, stride, offset, units):
    count = rows.shape[0]
    grid_spec = pltpu.PrefetchScalarGridSpec(
        num_scalar_prefetch=1,
        grid=(count, units),
        in_specs=[pl.BlockSpec((BLK, unit), lambda i, j, rows: (rows[i], j * stride + offset))],
        out_specs=pl.BlockSpec((BLK, unit), lambda i, j, rows: (i, j)),
    )
    return pl.pallas_call(
        pick_kernel,
        grid_spec=grid_spec,
        out_shape=jax.ShapeDtypeStruct((count * BLK, units * unit), jnp.bfloat16),
        compiler_params=pltpu.CompilerParams(vmem_limit_bytes=VMEM_LIMIT),
        cost_estimate=cost(0, 4 * count * BLK * units * unit),
    )(rows, front)


def add_kernel(
    blocks, pieces, target_ref, own_ref, place_ref, front_ref, factor_ref, col_ref, given_ref, *refs
):
    piece_refs, out_ref = refs[:pieces], refs[-1]
    factor = factor_ref[...]
    for block in range(blocks):
        here = pl.ds(block * BLK, BLK)
        own = pl.ds(pl.multiple_of(place_ref[0, block] * BLK, BLK), BLK)
        product = lax.dot_general(factor, col_ref[own, :], NT, preferred_element_type=jnp.float32)
        kept = (front_ref[:, own].astype(jnp.float32) - product).astype(jnp.bfloat16)
        arrived = piece_refs[0][:, pl.ds(pl.multiple_of(place_ref[1, block] * BLK, BLK), BLK)]
        if pieces == 2:
            other = piece_refs[1][:, pl.ds(pl.multiple_of(place_ref[2, block] * BLK, BLK), BLK)]
            arrived = jnp.where(place_ref[3, block] == 0, arrived, other)
        out_ref[:, here] = (
            given_ref[:, here].astype(jnp.float32)
            + kept.astype(jnp.float32)
            + arrived.astype(jnp.float32)
        )


def add_rows(out, targets, owns, places, front, factor, col_side, given, pieces):
    count = targets.shape[0]
    cols = front.shape[1]
    pivots = factor.shape[1]
    blocks = cols // BLK
    in_specs = [
        pl.BlockSpec((BLK, cols), lambda i, targets, owns, places: (owns[i], 0)),
        pl.BlockSpec((BLK, pivots), lambda i, targets, owns, places: (owns[i], 0)),
        pl.BlockSpec(col_side.shape, lambda i, targets, owns, places: (0, 0)),
        pl.BlockSpec((BLK, cols), lambda i, targets, owns, places: (targets[i], 0)),
    ] + [
        pl.BlockSpec((BLK, piece.shape[1]), lambda i, targets, owns, places: (i, 0))
        for piece in pieces
    ]
    operands = [targets, owns, places, front, factor, col_side, given, *pieces]
    aliases = {}
    if out is not None:
        aliases = {len(operands): 0}
        operands.append(out)
        in_specs.append(pl.BlockSpec(memory_space=pl.ANY))
    return pl.pallas_call(
        functools.partial(add_kernel, blocks, len(pieces)),
        grid_spec=pltpu.PrefetchScalarGridSpec(
            num_scalar_prefetch=3,
            grid=(count,),
            in_specs=in_specs,
            out_specs=pl.BlockSpec((BLK, cols), lambda i, targets, owns, places: (targets[i], 0)),
        ),
        out_shape=jax.ShapeDtypeStruct(given.shape, jnp.float32),
        input_output_aliases=aliases,
        compiler_params=pltpu.CompilerParams(vmem_limit_bytes=VMEM_LIMIT),
        cost_estimate=cost(2 * count * BLK * cols * pivots, 10 * count * BLK * cols + 2 * col_side.size),
    )(*operands)


def take_block(table, first, count):
    return lax.dynamic_slice_in_dim(table, first, count, 0)


def line_gather(mine, place, between):
    up = [(0, 1), (1, 2), (2, 3)]
    down = [(1, 0), (2, 1), (3, 2)]
    below = lax.ppermute(mine, "col", up)
    above = lax.ppermute(mine, "col", down)
    below2 = lax.ppermute(below, "col", up[1:])
    above2 = lax.ppermute(above, "col", down[:2])
    far = lax.ppermute(jnp.where(place == 2, below2, above2), "col", [(2, 3), (1, 0)])

    def choose(*options):
        picked = options[-1]
        for index in range(len(options) - 2, -1, -1):
            picked = jnp.where(place == index, options[index], picked)
        return picked

    segments = [
        choose(mine, below, below2, far),
        choose(above, mine, below, below2),
        choose(above2, above, mine, below),
        choose(far, above2, above, mine),
    ]
    low = choose(mine, above, below2, below)
    high = choose(above, above2, below, mine)
    return segments, low, high


def col_rows(low, high, place, core):
    both = jnp.concatenate([low, high], axis=0)
    swapped = lax.ppermute(both, "row", [(0, 1), (1, 0)])
    return jnp.where(core == place // 2, both, swapped)


def factor_of(panel, inverse, fill, first_row):
    local_rows = panel.shape[0]
    positions = (first_row + jnp.arange(local_rows, dtype=jnp.int32)) // BLK
    blocks = jnp.arange(fill.shape[0], dtype=jnp.int32)
    row_fill = jnp.sum(
        (positions[:, None] == blocks[None, :]).astype(jnp.int32) * fill[None, :], axis=1
    )
    masked = panel * row_fill[:, None].astype(jnp.bfloat16)
    return jnp.dot(masked, jnp.triu(inverse), preferred_element_type=jnp.float32).astype(jnp.bfloat16)


def from_sibling(block):
    route = []
    for low in range(0, lax.axis_size("front"), 2):
        route += [(low, low + 1), (low + 1, low)]
    return lax.ppermute(block, "front", route)


def shards(front, panel, inverse, fill, block_map, parent_front):
    front, panel, given = front[0], panel[0], parent_front[0]
    col_count = lax.axis_size("col")
    row_count = lax.axis_size("row")
    core = lax.axis_index("row")
    place = lax.axis_index("col")
    parity = lax.axis_index("front") % 2
    local_rows = panel.shape[0]
    tile_rows, tile_cols = front.shape
    half_blocks = tile_rows // 2 // BLK
    col_blocks = tile_cols // BLK
    seg = local_rows // BLK
    row_base = core * (tile_rows // BLK)
    sibling_map = from_sibling(block_map[0])
    source = block_inverse(block_map[0])
    sibling_source = block_inverse(sibling_map)
    col_source = take_block(source, place * col_blocks, col_blocks) - place * col_blocks
    sibling_cols = take_block(sibling_source, place * col_blocks, col_blocks) - place * col_blocks
    first_row = (core * col_count + place) * local_rows

    closed = half_blocks % col_blocks == 0
    line = (
        row_count == 2 and col_count == 4 and closed and tile_rows == 2 * tile_cols
        and local_rows % (2 * BLK) == 0 and 2 * local_rows == tile_cols
    )
    if not line:
        factor = factor_of(panel, inverse[0], fill[0], first_row)
        all_rows = lax.all_gather(factor, ("row", "col"), axis=0, tiled=True)
        row_side = take_block(all_rows, core * tile_rows, tile_rows)
        col_side = take_block(all_rows, place * tile_cols, tile_cols)
        sent = take_block(source, row_base + (1 - parity) * half_blocks, half_blocks) - row_base
        owns = take_block(source, row_base + parity * half_blocks, half_blocks) - row_base
        targets = jnp.arange(half_blocks, dtype=jnp.int32)
        arrived = from_sibling(
            updated_blocks(front, sent, row_side, sent, col_side, tile_cols, 1, 0, 1)
        )
        places = jnp.stack([col_source, sibling_cols])
        out = add_rows(None, targets, owns, places, front, row_side, col_side, given, [arrived])
        return factor[None], out[None]

    cut = seg // 2
    unit = cut * BLK
    steps = jnp.arange(cut, dtype=jnp.int32)
    sent_half = 1 - parity
    inner = parity * seg
    outer = seg - inner
    starts = [inner, inner + cut, outer, outer + cut]
    sent_base = sent_half * half_blocks
    raw = []
    for start in (starts[0], starts[2]):
        raw.append(from_sibling(picked_blocks(front, sent_base + start + steps, unit, 2, 0, 2)))
    factor = factor_of(panel, inverse[0], fill[0], first_row)
    segments, low, high = line_gather(factor, place, None)
    sibling_part = from_sibling(factor[:unit])
    col_side = col_rows(low, high, place, core)
    inner_rows = jnp.where(parity == 1, segments[1], segments[2])
    outer_rows = jnp.where(parity == 1, segments[0], segments[3])
    arrived = []
    for kind, (start, rows) in enumerate(zip(starts, (inner_rows, inner_rows, outer_rows, outer_rows))):
        fronts = sent_base + start + steps
        if kind % 2 == 0:
            piece = updated_blocks(front, fronts, rows, steps, col_side, unit, 2, 1, 2)
            arrived.append(from_sibling(piece))
        elif kind == 1:
            piece = updated_blocks(front, fronts, rows, steps + cut, col_side, unit, 1, 0, 4)
            arrived.append(from_sibling(piece))
        else:
            arrived.append([
                from_sibling(
                    updated_blocks(front, fronts[i:i + 1], rows, steps[i:i + 1] + cut, col_side, unit, 1, 0, 4)
                )
                for i in range(cut)
            ])

    row_side = jnp.concatenate(segments, axis=0)
    parts, part_low, part_high = line_gather(sibling_part, place, None)
    sibling_col = col_rows(part_low, part_high, place, core)
    kept_inner = jnp.where(parity == 0, parts[1], parts[2])
    kept_outer = jnp.where(parity == 0, parts[0], parts[3])
    finished = [
        updated_blocks(piece, steps, rows, steps, sibling_col, unit, 1, 0, 2)
        for piece, rows in zip(raw, (kept_inner, kept_outer))
    ]
    in_x = sibling_cols % seg < cut
    seg_at = sibling_cols // seg * cut
    places_x = jnp.stack([
        col_source,
        seg_at + jnp.minimum(sibling_cols % seg, cut - 1),
        seg_at + jnp.maximum(sibling_cols % seg - cut, 0),
        jnp.where(in_x, 0, 1),
    ])
    places_y = jnp.stack([col_source, sibling_cols])
    kept_base = row_base + parity * half_blocks
    kept_inner_at = (1 - parity) * seg
    kept_starts = [kept_inner_at, kept_inner_at + cut, seg - kept_inner_at, seg - kept_inner_at + cut]
    out = None
    for kind, start in enumerate(kept_starts):
        landed = take_block(sibling_map, kept_base + start, cut)
        owns = jnp.sum(
            jnp.where(landed[:, None] == jnp.arange(source.shape[0])[None, :], source[None, :], 0), axis=1
        ) - row_base
        targets = landed - kept_base
        if kind % 2 == 0:
            pieces = [finished[kind // 2], arrived[kind]]
            out = add_rows(out, targets, owns, places_x, front, row_side, col_side, given, pieces)
        elif kind == 1:
            out = add_rows(out, targets, owns, places_y, front, row_side, col_side, given, [arrived[kind]])
        else:
            for i in range(cut):
                out = add_rows(
                    out, targets[i:i + 1], owns[i:i + 1], places_y, front, row_side, col_side, given,
                    [arrived[kind][i]],
                )
    return factor[None], out[None]


def solution(mesh):
    placed = (
        P("front", "row", "col"),
        P("front", ("row", "col"), None),
        P("front", None, None),
        P("front", None),
        P("front", None),
        P("front", "row", "col"),
    )
    return jax.shard_map(
        shards,
        mesh=mesh,
        in_specs=placed,
        out_specs=(P("front", ("row", "col"), None), P("front", "row", "col")),
        check_vma=False,
    )
```

time: 934 us -> 577 us (0.62)
  local copies, waits for them, and re-layouts: 262 us -> 6.54 us
  Pallas kernels: 0 us -> 127 us
  waiting for transfers between devices: 497 us -> 385 us
  other arithmetic: 112 us -> 22.6 us
  matrix products: 43.9 us -> 2.58 us
  starting transfers between devices: 1.5 us -> 29.8 us
  between operations: 14.1 us -> 2.39 us
    gather x6 -> x0, local copies, waits for them, and re-layouts: 183 us -> none  [the longest x3 129 us: shards(): jnp.take(schur.reshape(row_blocks, BLK, tile_cols), row_source, axis=0)]
    pallas_call x0 -> x16, Pallas kernels: none -> 127 us  [the longest x6 61.2 us: add_rows(): pl.pallas_call(functools.partial(add_kernel, blocks, len(pieces)), grid_s...]
    all_gather x1 -> x0, waiting for transfers between devices: 118 us -> none  [shards(): all_rows = lax.all_gather(factor, ('row', 'col'), axis=0, tiled=True)]
    unnamed x4 -> x30, local copies, waits for them, and re-layouts: 61.4 us -> 3.97 us
    dot_general x2 -> x1, matrix products: 43.9 us -> 2.58 us  [factor_of(): jnp.dot(masked, jnp.triu(inverse), preferred_element_type=jnp.float32)]
    broadcast_in_dim x1 -> x0, other arithmetic: 32.9 us -> none  [shards(): return (factor[None], parent[None])]
    ppermute x1 -> x22, starting transfers between devices: 1.46 us -> 29.8 us  [the longest x10 11.1 us: from_sibling(): return lax.ppermute(block, 'front', route)]
    unnamed x1 -> x0, other arithmetic: 25.7 us -> none
  transfers between devices with their start and end apart: 2 -> 22, of which waited for: 2 -> 14; matrix products, arithmetic and copies ran while one was open for 3% -> 3% of each run, Pallas kernels for 0% -> 21%
where the time goes in v1:
time: 577 us; the launch traced here: 575 us
  waiting for transfers between devices  385 us (67%)
  Pallas kernels  127 us (22%)
  starting transfers between devices  29.8 us (5%)
  other arithmetic  22.6 us (4%)
  local copies, waits for them, and re-layouts  6.54 us (1%)
    ppermute x10, waiting for transfers between devices, from_sibling(): return lax.ppermute(block, 'front', route)  273 us
    pallas_call x6, Pallas kernels, add_rows(): pl.pallas_call(functools.partial(add_kernel, blocks, len(pieces)), grid_s...  61.2 us
    pallas_call x8, Pallas kernels, updated_blocks(): pl.pallas_call(functools.partial(update_kernel, unit, stride, offset), gr...  56.1 us
    ppermute x2, waiting for transfers between devices, line_gather(): lax.ppermute(jnp.where(place == 2, below2, above2), 'col', [(2, 3), (1, 0)])  38 us
    ppermute x2, waiting for transfers between devices, line_gather(): above2 = lax.ppermute(above, 'col', down[:2])  35.7 us
    ppermute x2, waiting for transfers between devices, line_gather(): below = lax.ppermute(mine, 'col', up)  31.2 us
  transfers between devices with their start and end apart: 22, of which 14 were waited for; matrix products, arithmetic and copies ran while one was open for 3% of the time, Pallas kernels for 21%

profile of v1, /device:TPU:0, one launch (start us, length us, event | category | flops | bytes accessed | tf_op | source)
XLA Modules:
  0.0 575.4 jit_solution(8135015031748243836)
XLA Ops:
  1.5 2.6 convolution_convert_fusion
  4.1 6.1 %collective-permute-start.1 = (bf16[1536,512]{1,0:T(8,128)(2,1)S(1)}, bf16[1536,512]{1,0:T(8,128)(2,1)}, u32[]{:S(2)}, u32[]{:S(2)}) collective-permute-start(bf16[1536,512]{1,0:T(8,128)(2,1)S(1)} %convolution_convert_fusion), channel_id=1, source_target_pairs={{0,1},{1,2},{2,3},{4,5},{5,6},{6,7},{8,9},{9,10},{10,11},{12,13},{... | collective-permute-start | bytes 4718600 | tf_op jit(solution)/shard_map/ppermute | solution.py:141
  11.4 31.2 %collective-permute-done.1 = bf16[1536,512]{1,0:T(8,128)(2,1)} collective-permute-done((bf16[1536,512]{1,0:T(8,128)(2,1)S(1)}, bf16[1536,512]{1,0:T(8,128)(2,1)}, u32[]{:S(2)}, u32[]{:S(2)}) %collective-permute-start.1) | collective-permute-done | bytes 1572896 | tf_op jit(solution)/shard_map/ppermute | solution.py:141
  43.4 4.6 collective-permute-done.3
  49.3 35.7 %collective-permute-done.4 = bf16[1536,512]{1,0:T(8,128)(2,1)S(1)} collective-permute-done((bf16[1536,512]{1,0:T(8,128)(2,1)}, bf16[1536,512]{1,0:T(8,128)(2,1)S(1)}, u32[]{:S(2)}, u32[]{:S(2)}) %collective-permute-start.4) | collective-permute-done | bytes 1572896 | tf_op jit(solution)/shard_map/ppermute | solution.py:144
  85.0 1.4 broadcast_select_fusion.4
  88.0 34.9 %collective-permute-done.5 = bf16[1536,512]{1,0:T(8,128)(2,1)} collective-permute-done((bf16[1536,512]{1,0:T(8,128)(2,1)}, bf16[1536,512]{1,0:T(8,128)(2,1)}, u32[]{:S(2)}, u32[]{:S(2)}) %collective-permute-start.5) | collective-permute-done | bytes 1572896 | tf_op jit(solution)/shard_map/ppermute | solution.py:145
  122.9 6.2 %broadcast_select_fusion.2 = (bf16[1536,512]{1,0:T(8,128)(2,1)S(1)}, bf16[1536,512]{1,0:T(8,128)(2,1)}, bf16[1536,512]{1,0:T(8,128)(2,1)}, bf16[1536,512]{1,0:T(...) fusion(pred[]{:T(512)S(6)} %eq.76, ...), kind=kLoop, calls=%fused_computation.14 | loop fusion | flops 15728640 | bytes 22020100 | tf_op jit(solution)/shard_map/jit(_where)/select_n | solution.py:243
  129.1 1.9 pad_maximum_fusion.1
  131.9 1.5 collective-permute-start.11
  133.4 18.1 %collective-permute-done.11 = bf16[768,512]{1,0:T(8,128)(2,1)} collective-permute-done((bf16[768,512]{1,0:T(8,128)(2,1)S(1)}, bf16[768,512]{1,0:T(8,128)(2,1)}, u32[]{:S(2)}, u32[]{:S(2)}) %collective-permute-start.11) | collective-permute-done | bytes 786464 | tf_op jit(solution)/shard_map/ppermute | solution.py:185
  151.5 2.3 collective-permute-start.12
  155.2 5.5 shard_map.84
  160.7 1.5 collective-permute-start.20
  162.7 4.0 shard_map.80
  166.7 1.4 copy-done.3
  170.7 1.6 collective-permute-start.13
  172.2 2.2 collective-permute-done.14
  176.6 36.6 %collective-permute-done = s32[48]{0:T(128)S(1)} collective-permute-done((s32[48]{0:T(128)S(1)}, s32[48]{0:T(128)S(1)}, u32[]{:S(2)}, u32[]{:S(2)}) %collective-permute-start) | collective-permute-done | bytes 224 | tf_op jit(solution)/shard_map/ppermute | solution.py:185
  213.1 1.5 collective-permute-start.10
  216.1 1.5 collective-permute-start.16
  217.6 2.3 broadcast_select_fusion.col_ref
  219.9 11.6 %shard_map.83 = bf16[768,3072]{1,0:T(8,128)(2,1)} custom-call(s32[3]{0:T(128)S(1)} %iota_add_fusion.4.rows_ref, s32[3]{0:T(128)S(1)} %iota_add_fusion.3.fac_ref, bf16[6144,3072]{1,0:T(8,128)(2,1)} %bitcast.24, bf16[1536,512]{1,0:T(8,128)(2,1)S(1)} %get-tuple-element.8.factor_ref, bf16[3072,512]{1,0:T(8,128)(2,1)S(1)} %broadcast_select_fusion.col_ref), custom_call_target="tpu_custom_call" | custom-call | flops 2415919104 | bytes 12582912 | tf_op jit(solution)/shard_map/pallas_call | solution.py:46
  232.0 3.1 collective-permute-done.16
  235.2 2.4 select_select_fusion.6
  237.8 7.6 %shard_map.86 = bf16[768,1536]{1,0:T(8,128)(2,1)} custom-call(s32[3]{0:T(128)S(1)} %iota_add_fusion.2.rows_ref, s32[3]{0:T(128)S(1)} %iota.80.fac_ref, bf16[6144,3072]{1,0:T(8,128)(2,1)} %bitcast.25, bf16[1536,512]{1,0:T(8,128)(2,1)S(1)} %get-tuple-element.8.factor_ref, bf16[3072,512]{1,0:T(8,128)(2,1)} %copy-done), custom_call_target="tpu_custom_call" | custom-call | flops 1207959552 | bytes 7864320 | tf_op jit(solution)/shard_map/pallas_call | solution.py:46
  246.8 7.6 %shard_map.82 = bf16[768,1536]{1,0:T(8,128)(2,1)} custom-call(s32[3]{0:T(128)S(1)} %iota_add_fusion.5.rows_ref, s32[3]{0:T(128)S(1)} %iota.75.fac_ref, bf16[6144,3072]{1,0:T(8,128)(2,1)} %bitcast.26, bf16[1536,512]{1,0:T(8,128)(2,1)S(1)} %get-tuple-element.24.factor_ref, bf16[3072,512]{1,0:T(8,128)(2,1)} %copy-done), custom_call_target="tpu_custom_call" | custom-call | flops 1207959552 | bytes 7864320 | tf_op jit(solution)/shard_map/pallas_call | solution.py:46
  254.4 1.5 collective-permute-start.18
  256.4 5.4 shard_map.85.refs_0_
  261.8 5.7 collective-permute-done.10.front_ref
  268.9 5.4 shard_map.81.refs_0_
  274.3 6.0 %shard_map.79 = bf16[256,3072]{1,0:T(8,128)(2,1)} custom-call(s32[1]{0:T(128)} %get-tuple-element.35.rows_ref, s32[1]{0:T(128)S(6)} %add.166.fac_ref, bf16[6144,3072]{1,0:T(8,128)(2,1)} %bitcast.27, bf16[1536,512]{1,0:T(8,128)(2,1)S(1)} %get-tuple-element.24.factor_ref, bf16[3072,512]{1,0:T(8,128)(2,1)} %copy-done), custom_call_target="tpu_custom_call" | custom-call | flops 805306368 | bytes 6291456 | tf_op jit(solution)/shard_map/pallas_call | solution.py:46
  280.4 1.5 collective-permute-start.9
  281.9 6.2 %shard_map.78 = bf16[256,3072]{1,0:T(8,128)(2,1)} custom-call(s32[1]{0:T(128)} %get-tuple-element.36.rows_ref, s32[1]{0:T(128)S(6)} %add.165.fac_ref, bf16[6144,3072]{1,0:T(8,128)(2,1)} %bitcast.28, bf16[1536,512]{1,0:T(8,128)(2,1)S(1)} %get-tuple-element.24.factor_ref, bf16[3072,512]{1,0:T(8,128)(2,1)} %copy-done), custom_call_target="tpu_custom_call" | custom-call | flops 805306368 | bytes 6291456 | tf_op jit(solution)/shard_map/pallas_call | solution.py:46
  288.6 6.3 %shard_map.77 = bf16[256,3072]{1,0:T(8,128)(2,1)} custom-call(s32[1]{0:T(128)} %get-tuple-element.37.rows_ref, s32[1]{0:T(128)S(6)} %add.164.fac_ref, bf16[6144,3072]{1,0:T(8,128)(2,1)} %bitcast.29, bf16[1536,512]{1,0:T(8,128)(2,1)S(1)} %get-tuple-element.24.factor_ref, bf16[3072,512]{1,0:T(8,128)(2,1)} %copy-done), custom_call_target="tpu_custom_call" | custom-call | flops 805306368 | bytes 6291456 | tf_op jit(solution)/shard_map/pallas_call | solution.py:46
  294.9 124.4 %collective-permute-done.21.refs_1_ = bf16[768,1536]{1,0:T(8,128)(2,1)} collective-permute-done((bf16[768,1536]{1,0:T(8,128)(2,1)}, bf16[768,1536]{1,0:T(8,128)(2,1)}, u32[]{:S(2)}, u32[]{:S(2)}) %collective-permute-start.21) | collective-permute-done | bytes 2359328 | tf_op jit(solution)/shard_map/ppermute | solution.py:185
  419.3 1.5 collective-permute-start.7
  420.8 5.2 pad_maximum_fusion.factor_ref
  426.0 14.0 %shard_map.87.refs_1_ = f32[3072,3072]{1,0:T(8,128)} custom-call(s32[3]{0:T(128)S(1)} %get-tuple-element.46.target_ref, s32[3]{0:T(128)S(1)} %broadcast_subtract_fusion.own_ref, s32[4,12]{1,0:T(4,128)S(1)} %pad_add_fusion.place_ref, bf16[6144,3072]{1,0:T(8,128)(2,1)} %bitcast.30, bf16[6144,512]{1,0:T(8,128)(2,1)} %pad_maximum_fusion.factor_ref, ...), custom_call_target="tpu_custom_call" | custom-call | flops 2415919104 | bytes 26738688 | tf_op jit(solution)/shard_map/pallas_call | solution.py:119
  440.0 12.3 %shard_map.88.refs_2_ = f32[3072,3072]{1,0:T(8,128)} custom-call(s32[3]{0:T(128)S(1)} %get-tuple-element.11.target_ref, s32[3]{0:T(128)S(1)} %broadcast_subtract_fusion.1.own_ref, s32[2,12]{1,0:T(2,128)S(1)} %pad_add_fusion.1.place_ref, bf16[6144,3072]{1,0:T(8,128)(2,1)} %bitcast.31, ...), custom_call_target="tpu_custom_call", output_to_operand_aliasing={{}: (8, {})} | custom-call | flops 2415919104 | bytes 26738688 | tf_op jit(solution)/shard_map/pallas_call | solution.py:119
  452.4 17.4 %collective-permute-done.18.refs_1_ = bf16[768,1536]{1,0:T(8,128)(2,1)S(1)} collective-permute-done((bf16[768,1536]{1,0:T(8,128)(2,1)}, bf16[768,1536]{1,0:T(8,128)(2,1)S(1)}, u32[]{:S(2)}, u32[]{:S(2)}) %collective-permute-start.18) | collective-permute-done | bytes 2359328 | tf_op jit(solution)/shard_map/ppermute | solution.py:185
  469.8 13.3 %shard_map.89.refs_1_ = f32[3072,3072]{1,0:T(8,128)} custom-call(s32[3]{0:T(128)S(1)} %get-tuple-element.44.target_ref, s32[3]{0:T(128)S(1)} %broadcast_subtract_fusion.2.own_ref, s32[4,12]{1,0:T(4,128)S(1)} %pad_add_fusion.place_ref, bf16[6144,3072]{1,0:T(8,128)(2,1)} %bitcast.32, ...), custom_call_target="tpu_custom_call", output_to_operand_aliasing={{}: (9, {})} | custom-call | flops 2415919104 | bytes 26738688 | tf_op jit(solution)/shard_map/pallas_call | solution.py:119
  483.0 20.4 %collective-permute-done.9.refs_0_ = bf16[256,3072]{1,0:T(8,128)(2,1)S(1)} collective-permute-done((bf16[256,3072]{1,0:T(8,128)(2,1)}, bf16[256,3072]{1,0:T(8,128)(2,1)S(1)}, u32[]{:S(2)}, u32[]{:S(2)}) %collective-permute-start.9) | collective-permute-done | bytes 1572896 | tf_op jit(solution)/shard_map/ppermute | solution.py:185
  503.5 6.9 %shard_map.90.refs_1_ = f32[3072,3072]{1,0:T(8,128)} custom-call(s32[1]{0:T(128)} %get-tuple-element.52.target_ref, s32[1]{0:T(128)} %get-tuple-element.38.own_ref, s32[2,12]{1,0:T(2,128)S(1)} %pad_add_fusion.1.place_ref, bf16[6144,3072]{1,0:T(8,128)(2,1)} %bitcast.33, bf16[6144,512]{1,0:T(8,128)(2,1)} %pad_maximum_fusion.factor_ref, ...), custom_call_target="tpu_custom_call", output_to_operand_aliasing={{}: (8, {})} | custom-call | flops 805306368 | bytes 11010048 | tf_op jit(solution)/shard_map/pallas_call | solution.py:119
  510.3 27.0 %collective-permute-done.8.refs_0_ = bf16[256,3072]{1,0:T(8,128)(2,1)} collective-permute-done((bf16[256,3072]{1,0:T(8,128)(2,1)}, bf16[256,3072]{1,0:T(8,128)(2,1)}, u32[]{:S(2)}, u32[]{:S(2)}) %collective-permute-start.8) | collective-permute-done | bytes 1572896 | tf_op jit(solution)/shard_map/ppermute | solution.py:185
  537.3 7.3 %shard_map.91.refs_1_ = f32[3072,3072]{1,0:T(8,128)} custom-call(s32[1]{0:T(128)} %get-tuple-element.51.target_ref, s32[1]{0:T(128)} %get-tuple-element.39.own_ref, s32[2,12]{1,0:T(2,128)S(1)} %pad_add_fusion.1.place_ref, bf16[6144,3072]{1,0:T(8,128)(2,1)} %bitcast.34, bf16[6144,512]{1,0:T(8,128)(2,1)} %pad_maximum_fusion.factor_ref, ...), custom_call_target="tpu_custom_call", output_to_operand_aliasing={{}: (8, {})} | custom-call | flops 805306368 | bytes 11010048 | tf_op jit(solution)/shard_map/pallas_call | solution.py:119
  544.6 23.4 %collective-permute-done.7.refs_0_ = bf16[256,3072]{1,0:T(8,128)(2,1)} collective-permute-done((bf16[256,3072]{1,0:T(8,128)(2,1)}, bf16[256,3072]{1,0:T(8,128)(2,1)}, u32[]{:S(2)}, u32[]{:S(2)}) %collective-permute-start.7) | collective-permute-done | bytes 1572896 | tf_op jit(solution)/shard_map/ppermute | solution.py:185
  568.0 7.4 %shard_map.92 = f32[3072,3072]{1,0:T(8,128)} custom-call(s32[1]{0:T(128)} %get-tuple-element.50.target_ref, s32[1]{0:T(128)} %get-tuple-element.40.own_ref, s32[2,12]{1,0:T(2,128)S(1)} %pad_add_fusion.1.place_ref, bf16[6144,3072]{1,0:T(8,128)(2,1)} %bitcast.35, bf16[6144,512]{1,0:T(8,128)(2,1)} %pad_maximum_fusion.factor_ref, ...), custom_call_target="tpu_custom_call", output_to_operand_aliasing={{}: (8, {})} | custom-call | flops 805306368 | bytes 11010048 | tf_op jit(solution)/shard_map/pallas_call | solution.py:119
  (86 shorter events, 17.8 us)
Async XLA Ops:
  4.0 39.3 %copy-start.11 = (bf16[1536,512]{1,0:T(8,128)(2,1)}, bf16[1536,512]{1,0:T(8,128)(2,1)S(1)}, u32[]{:S(2)}) copy-start(bf16[1536,512]{1,0:T(8,128)(2,1)S(1)} %convolution_convert_fusion) | copy-start | bytes 4718596
  4.1 38.6 %collective-permute-start.1 = (bf16[1536,512]{1,0:T(8,128)(2,1)S(1)}, bf16[1536,512]{1,0:T(8,128)(2,1)}, u32[]{:S(2)}, u32[]{:S(2)}) collective-permute-start(bf16[1536,512]{1,0:T(8,128)(2,1)S(1)} %convolution_convert_fusion), channel_id=1, source_target_pairs={{0,1},{1,2},{2,3},{4,5},{5,6},{6,7},{8,9},{9,10},{10,11},{12,13},{... | collective-permute-start | bytes 4718600 | tf_op jit(solution)/shard_map/ppermute | solution.py:141
  10.1 37.8 %collective-permute-start.3 = (bf16[1536,512]{1,0:T(8,128)(2,1)S(1)}, bf16[1536,512]{1,0:T(8,128)(2,1)}, u32[]{:S(2)}, u32[]{:S(2)}) collective-permute-start(bf16[1536,512]{1,0:T(8,128)(2,1)S(1)} %convolution_convert_fusion), channel_id=1, source_target_pairs={{1,0},{2,1},{3,2},{5,4},{6,5},{7,6},{9,8},{10,9},{11,10},{13,12},{... | collective-permute-start | bytes 4718600 | tf_op jit(solution)/shard_map/ppermute | solution.py:142
  42.6 6.7 %collective-permute-start.2 = (bf16[1536,512]{1,0:T(8,128)(2,1)}, bf16[1536,512]{1,0:T(8,128)(2,1)S(1)}, u32[]{:S(2)}, u32[]{:S(2)}) collective-permute-start(bf16[1536,512]{1,0:T(8,128)(2,1)} %collective-permute-done.1), channel_id=1, source_target_pairs={{1,2},{2,3},{5,6},{6,7},{9,10},{10,11},{13,14},{14,15},{17,18},{18... | collective-permute-start | bytes 4718600 | tf_op jit(solution)/shard_map/ppermute | solution.py:143
  48.0 37.0 %collective-permute-start.4 = (bf16[1536,512]{1,0:T(8,128)(2,1)}, bf16[1536,512]{1,0:T(8,128)(2,1)S(1)}, u32[]{:S(2)}, u32[]{:S(2)}) collective-permute-start(bf16[1536,512]{1,0:T(8,128)(2,1)} %collective-permute-done.3), channel_id=1, source_target_pairs={{1,0},{2,1},{5,4},{6,5},{9,8},{10,9},{13,12},{14,13},{17,16},{18,1... | collective-permute-start | bytes 4718600 | tf_op jit(solution)/shard_map/ppermute | solution.py:144
  49.3 37.2 %copy-start.9 = (bf16[1536,512]{1,0:T(8,128)(2,1)}, bf16[1536,512]{1,0:T(8,128)(2,1)S(1)}, u32[]{:S(2)}) copy-start(bf16[1536,512]{1,0:T(8,128)(2,1)S(1)} %collective-permute-done.2) | copy-start | bytes 4718596
  85.0 1.7 copy-start.10
  86.7 36.2 %collective-permute-start.5 = (bf16[1536,512]{1,0:T(8,128)(2,1)}, bf16[1536,512]{1,0:T(8,128)(2,1)}, u32[]{:S(2)}, u32[]{:S(2)}) collective-permute-start(bf16[1536,512]{1,0:T(8,128)(2,1)} %broadcast_select_fusion.4), channel_id=1, source_target_pairs={{2,3},{1,0},{6,7},{5,4},{10,11},{9,8},{14,15},{13,12},{18,19},{17,... | collective-permute-start | bytes 4718600 | tf_op jit(solution)/shard_map/ppermute | solution.py:145
  129.1 2.2 copy-start.4
  129.1 2.8 copy-start.6
  129.1 2.8 copy-start.12
  131.3 86.2 %collective-permute-start.6 = (bf16[3072,512]{1,0:T(8,128)(2,1)}, bf16[3072,512]{1,0:T(8,128)(2,1)}, u32[]{:S(2)}, u32[]{:S(2)}) collective-permute-start(bf16[3072,512]{1,0:T(8,128)(2,1)} %pad_maximum_fusion.1), channel_id=1, source_target_pairs={{0,4},{4,0},{1,5},{5,1},{2,6},{6,2},{3,7},{7,3},{8,12},{12,8},{9,1... | collective-permute-start | bytes 9437192 | tf_op jit(solution)/shard_map/ppermute | solution.py:166
  131.9 19.6 %collective-permute-start.11 = (bf16[768,512]{1,0:T(8,128)(2,1)S(1)}, bf16[768,512]{1,0:T(8,128)(2,1)}, u32[]{:S(2)}, u32[]{:S(2)}) collective-permute-start(bf16[768,512]{1,0:T(8,128)(2,1)S(1)} %slice.52), channel_id=1, source_target_pairs={{0,8},{8,0},{16,24},{24,16},{1,9},{9,1},{17,25},{25,17},{2,10},{10... | collective-permute-start | bytes 2359304 | tf_op jit(solution)/shard_map/ppermute | solution.py:185
  151.5 19.2 %collective-permute-start.12 = (bf16[768,512]{1,0:T(8,128)(2,1)}, bf16[768,512]{1,0:T(8,128)(2,1)}, u32[]{:S(2)}, u32[]{:S(2)}) collective-permute-start(bf16[768,512]{1,0:T(8,128)(2,1)} %collective-permute-done.11), channel_id=1, source_target_pairs={{0,1},{1,2},{2,3},{4,5},{5,6},{6,7},{8,9},{9,10},{10,11},{12,13},{... | collective-permute-start | bytes 2359304 | tf_op jit(solution)/shard_map/ppermute | solution.py:141
  153.8 20.6 %collective-permute-start.14 = (bf16[768,512]{1,0:T(8,128)(2,1)}, bf16[768,512]{1,0:T(8,128)(2,1)}, u32[]{:S(2)}, u32[]{:S(2)}) collective-permute-start(bf16[768,512]{1,0:T(8,128)(2,1)} %collective-permute-done.11), channel_id=1, source_target_pairs={{1,0},{2,1},{3,2},{5,4},{6,5},{7,6},{9,8},{10,9},{11,10},{13,12},{... | collective-permute-start | bytes 2359304 | tf_op jit(solution)/shard_map/ppermute | solution.py:142
  155.1 7.0 %copy-start.14 = (s32[1,48]{1,0:T(1,128)S(1)}, s32[1,48]{1,0:T(1,128)}, u32[]{:S(2)}) copy-start(s32[1,48]{1,0:T(1,128)} %param.10) | copy-start | bytes 580
  160.7 95.7 %collective-permute-start.20 = (bf16[768,1536]{1,0:T(8,128)(2,1)}, bf16[768,1536]{1,0:T(8,128)(2,1)}, u32[]{:S(2)}, u32[]{:S(2)}) collective-permute-start(bf16[768,1536]{1,0:T(8,128)(2,1)} %shard_map.84), channel_id=1, source_target_pairs={{0,8},{8,0},{16,24},{24,16},{1,9},{9,1},{17,25},{25,17},{2,10},{10... | collective-permute-start | bytes 7077896 | tf_op jit(solution)/shard_map/ppermute | solution.py:185
  162.2 51.0 %collective-permute-start = (s32[48]{0:T(128)S(1)}, s32[48]{0:T(128)S(1)}, u32[]{:S(2)}, u32[]{:S(2)}) collective-permute-start(s32[48]{0:T(128)S(1)} %bitcast.46), channel_id=1, source_target_pairs={{0,8},{8,0},{16,24},{24,16},{1,9},{9,1},{17,25},{25,17},{2,10},{10... | collective-permute-start | bytes 584 | tf_op jit(solution)/shard_map/ppermute | solution.py:185
  166.7 1.4 copy-start.3
  170.7 44.1 %collective-permute-start.13 = (bf16[768,512]{1,0:T(8,128)(2,1)}, bf16[768,512]{1,0:T(8,128)(2,1)}, u32[]{:S(2)}, u32[]{:S(2)}) collective-permute-start(bf16[768,512]{1,0:T(8,128)(2,1)} %collective-permute-done.12), channel_id=1, source_target_pairs={{1,2},{2,3},{5,6},{6,7},{9,10},{10,11},{13,14},{14,15},{17,18},{18... | collective-permute-start | bytes 2359304 | tf_op jit(solution)/shard_map/ppermute | solution.py:143
  174.5 40.4 %collective-permute-start.15 = (bf16[768,512]{1,0:T(8,128)(2,1)}, bf16[768,512]{1,0:T(8,128)(2,1)}, u32[]{:S(2)}, u32[]{:S(2)}) collective-permute-start(bf16[768,512]{1,0:T(8,128)(2,1)} %collective-permute-done.14), channel_id=1, source_target_pairs={{1,0},{2,1},{5,4},{6,5},{9,8},{10,9},{13,12},{14,13},{17,16},{18,1... | collective-permute-start | bytes 2359304 | tf_op jit(solution)/shard_map/ppermute | solution.py:144
  176.6 41.0 %copy-start.5 = (bf16[1536,512]{1,0:T(8,128)(2,1)S(1)}, bf16[1536,512]{1,0:T(8,128)(2,1)}, u32[]{:S(2)}) copy-start(bf16[1536,512]{1,0:T(8,128)(2,1)} %copy-done.4) | copy-start | bytes 4718596
  213.1 54.4 %collective-permute-start.10 = (bf16[768,1536]{1,0:T(8,128)(2,1)}, bf16[768,1536]{1,0:T(8,128)(2,1)S(1)}, u32[]{:S(2)}, u32[]{:S(2)}) collective-permute-start(bf16[768,1536]{1,0:T(8,128)(2,1)} %copy-done.3), channel_id=1, source_target_pairs={{0,8},{8,0},{16,24},{24,16},{1,9},{9,1},{17,25},{25,17},{2,10},{10... | collective-permute-start | bytes 7077896 | tf_op jit(solution)/shard_map/ppermute | solution.py:185
  216.1 19.1 %collective-permute-start.16 = (bf16[768,512]{1,0:T(8,128)(2,1)S(1)}, bf16[768,512]{1,0:T(8,128)(2,1)S(1)}, u32[]{:S(2)}, u32[]{:S(2)}) collective-permute-start(bf16[768,512]{1,0:T(8,128)(2,1)S(1)} %broadcast_select_fusion.5), channel_id=1, source_target_pairs={{2,3},{1,0},{6,7},{5,4},{10,11},{9,8},{14,15},{13,12},{18,19},{17,... | collective-permute-start | bytes 2359304 | tf_op jit(solution)/shard_map/ppermute | solution.py:145
  219.9 11.6 %copy-start = (bf16[3072,512]{1,0:T(8,128)(2,1)}, bf16[3072,512]{1,0:T(8,128)(2,1)S(1)}, u32[]{:S(2)}) copy-start(bf16[3072,512]{1,0:T(8,128)(2,1)S(1)} %broadcast_select_fusion.col_ref) | copy-start | bytes 9437188
  231.5 208.5 %collective-permute-start.19 = (bf16[768,3072]{1,0:T(8,128)(2,1)}, bf16[768,3072]{1,0:T(8,128)(2,1)}, u32[]{:S(2)}, u32[]{:S(2)}) collective-permute-start(bf16[768,3072]{1,0:T(8,128)(2,1)} %shard_map.83), channel_id=1, source_target_pairs={{0,8},{8,0},{16,24},{24,16},{1,9},{9,1},{17,25},{25,17},{2,10},{10... | collective-permute-start | bytes 14155784 | tf_op jit(solution)/shard_map/ppermute | solution.py:185
  237.6 16.8 %collective-permute-start.17 = (bf16[1536,512]{1,0:T(8,128)(2,1)S(1)}, bf16[1536,512]{1,0:T(8,128)(2,1)S(1)}, u32[]{:S(2)}, u32[]{:S(2)}) collective-permute-start(bf16[1536,512]{1,0:T(8,128)(2,1)S(1)} %pad_maximum_fusion.2), channel_id=1, source_target_pairs={{0,4},{4,0},{1,5},{5,1},{2,6},{6,2},{3,7},{7,3},{8,12},{12,8},{9,1... | collective-permute-start | bytes 4718600 | tf_op jit(solution)/shard_map/ppermute | solution.py:166
  245.4 173.9 %collective-permute-start.21 = (bf16[768,1536]{1,0:T(8,128)(2,1)}, bf16[768,1536]{1,0:T(8,128)(2,1)}, u32[]{:S(2)}, u32[]{:S(2)}) collective-permute-start(bf16[768,1536]{1,0:T(8,128)(2,1)} %shard_map.86), channel_id=1, source_target_pairs={{0,8},{8,0},{16,24},{24,16},{1,9},{9,1},{17,25},{25,17},{2,10},{10... | collective-permute-start | bytes 7077896 | tf_op jit(solution)/shard_map/ppermute | solution.py:185
  254.4 215.3 %collective-permute-start.18 = (bf16[768,1536]{1,0:T(8,128)(2,1)}, bf16[768,1536]{1,0:T(8,128)(2,1)S(1)}, u32[]{:S(2)}, u32[]{:S(2)}) collective-permute-start(bf16[768,1536]{1,0:T(8,128)(2,1)} %shard_map.82), channel_id=1, source_target_pairs={{0,8},{8,0},{16,24},{24,16},{1,9},{9,1},{17,25},{25,17},{2,10},{10... | collective-permute-start | bytes 7077896 | tf_op jit(solution)/shard_map/ppermute | solution.py:185
  267.5 1.4 copy-start.13
  280.4 223.1 %collective-permute-start.9 = (bf16[256,3072]{1,0:T(8,128)(2,1)}, bf16[256,3072]{1,0:T(8,128)(2,1)S(1)}, u32[]{:S(2)}, u32[]{:S(2)}) collective-permute-start(bf16[256,3072]{1,0:T(8,128)(2,1)} %shard_map.79), channel_id=1, source_target_pairs={{0,8},{8,0},{16,24},{24,16},{1,9},{9,1},{17,25},{25,17},{2,10},{10... | collective-permute-start | bytes 4718600 | tf_op jit(solution)/shard_map/ppermute | solution.py:185
  288.0 249.3 %collective-permute-start.8 = (bf16[256,3072]{1,0:T(8,128)(2,1)}, bf16[256,3072]{1,0:T(8,128)(2,1)}, u32[]{:S(2)}, u32[]{:S(2)}) collective-permute-start(bf16[256,3072]{1,0:T(8,128)(2,1)} %shard_map.78), channel_id=1, source_target_pairs={{0,8},{8,0},{16,24},{24,16},{1,9},{9,1},{17,25},{25,17},{2,10},{10... | collective-permute-start | bytes 4718600 | tf_op jit(solution)/shard_map/ppermute | solution.py:185
  288.6 132.2 %copy-start.7 = (bf16[1536,512]{1,0:T(8,128)(2,1)S(1)}, bf16[1536,512]{1,0:T(8,128)(2,1)}, u32[]{:S(2)}) copy-start(bf16[1536,512]{1,0:T(8,128)(2,1)} %get-tuple-element.9) | copy-start | bytes 4718596
  288.6 132.2 %copy-start.8 = (bf16[1536,512]{1,0:T(8,128)(2,1)S(1)}, bf16[1536,512]{1,0:T(8,128)(2,1)}, u32[]{:S(2)}) copy-start(bf16[1536,512]{1,0:T(8,128)(2,1)} %get-tuple-element.10) | copy-start | bytes 4718596
  419.3 148.7 %collective-permute-start.7 = (bf16[256,3072]{1,0:T(8,128)(2,1)}, bf16[256,3072]{1,0:T(8,128)(2,1)}, u32[]{:S(2)}, u32[]{:S(2)}) collective-permute-start(bf16[256,3072]{1,0:T(8,128)(2,1)} %shard_map.77), channel_id=1, source_target_pairs={{0,8},{8,0},{16,24},{24,16},{1,9},{9,1},{17,25},{25,17},{2,10},{10... | collective-permute-start | bytes 4718600 | tf_op jit(solution)/shard_map/ppermute | solution.py:185
  426.0 14.0 %copy-start.1 = (bf16[3072,512]{1,0:T(8,128)(2,1)S(1)}, bf16[3072,512]{1,0:T(8,128)(2,1)}, u32[]{:S(2)}) copy-start(bf16[3072,512]{1,0:T(8,128)(2,1)} %copy-done) | copy-start | bytes 9437188
  469.8 33.7 %copy-start.2 = (bf16[3072,512]{1,0:T(8,128)(2,1)S(1)}, bf16[3072,512]{1,0:T(8,128)(2,1)}, u32[]{:S(2)}) copy-start(bf16[3072,512]{1,0:T(8,128)(2,1)} %copy-done) | copy-start | bytes 9437188

commit v2 on v0

v2 whole, which is shorter than its diff:
```python
import functools

import jax
import jax.numpy as jnp
from jax import lax
from jax.experimental import pallas as pl
from jax.experimental.pallas import tpu as pltpu
from jax.sharding import PartitionSpec as P

BLK = 256
NT = (((1,), (1,)), ((), ()))
VMEM_LIMIT = 48 * 1024 * 1024
STEP = 128
RAW_PIECES = ((0, 1), (1, 4), (5, 5), (10, 2))


def block_inverse(mapping):
    block_total = mapping.shape[0]
    target = jnp.arange(block_total, dtype=jnp.int32)
    matches = (mapping[:, None] == target[None, :]).astype(jnp.int32)
    return jnp.sum(matches * target[:, None], axis=0)


SMALL = pl.CostEstimate(flops=1, bytes_accessed=1, transcendentals=0)


def update_kernel(unit, stride, offset, at_ref, front_ref, factor_ref, col_ref, out_ref):
    first = (pl.program_id(1) * stride + offset) * unit
    col = col_ref[pl.ds(pl.multiple_of(first, unit), unit), :]
    product = lax.dot_general(factor_ref[...], col, NT, preferred_element_type=jnp.float32)
    out_ref[...] = (front_ref[...].astype(jnp.float32) - product).astype(jnp.bfloat16)


def updated_rows(front, at, front_row, factor, factor_row, col_side, grid, height, unit, stride, offset):
    pivots = factor.shape[1]
    return pl.pallas_call(
        functools.partial(update_kernel, unit, stride, offset),
        grid_spec=pltpu.PrefetchScalarGridSpec(
            num_scalar_prefetch=1,
            grid=grid,
            in_specs=[
                pl.BlockSpec((height, unit), lambda i, j, at: (front_row(i, at), j * stride + offset)),
                pl.BlockSpec((height, pivots), lambda i, j, at: (factor_row(i, at), 0)),
                pl.BlockSpec(col_side.shape, lambda i, j, at: (0, 0)),
            ],
            out_specs=pl.BlockSpec((height, unit), lambda i, j, at: (i, j)),
        ),
        out_shape=jax.ShapeDtypeStruct((grid[0] * height, grid[1] * unit), jnp.bfloat16),
        compiler_params=pltpu.CompilerParams(vmem_limit_bytes=VMEM_LIMIT),
        cost_estimate=SMALL,
    )(at, front, factor, col_side)


def pick_kernel(at_ref, front_ref, out_ref):
    out_ref[...] = front_ref[...]


def picked_rows(front, at, front_row, grid, height, unit, stride):
    return pl.pallas_call(
        pick_kernel,
        grid_spec=pltpu.PrefetchScalarGridSpec(
            num_scalar_prefetch=1,
            grid=grid,
            in_specs=[pl.BlockSpec((height, unit), lambda i, j, at: (front_row(i, at), j * stride))],
            out_specs=pl.BlockSpec((height, unit), lambda i, j, at: (i, j)),
        ),
        out_shape=jax.ShapeDtypeStruct((grid[0] * height, grid[1] * unit), jnp.bfloat16),
        compiler_params=pltpu.CompilerParams(vmem_limit_bytes=VMEM_LIMIT),
        cost_estimate=SMALL,
    )(at, front)


def assemble_kernel(plan, sources, at_ref, *refs):
    outs, sem = refs[sources:-1], refs[-1]
    for step, (out, first, rows, choice, options) in enumerate(plan):
        chosen = choice(at_ref)
        for value, (source, start) in options.items():
            @pl.when(chosen == value)
            def _():
                pltpu.make_async_copy(
                    refs[source].at[pl.ds(start, rows)], outs[out].at[pl.ds(first, rows)], sem.at[step]
                ).start()
    for step, (out, first, rows, _, options) in enumerate(plan):
        source, start = next(iter(options.values()))
        pltpu.make_async_copy(
            refs[source].at[pl.ds(start, rows)], outs[out].at[pl.ds(first, rows)], sem.at[step]
        ).wait()


def assembled(at, sources, plan, out_rows):
    width = sources[0].shape[1]
    return pl.pallas_call(
        functools.partial(assemble_kernel, plan, len(sources)),
        grid_spec=pltpu.PrefetchScalarGridSpec(
            num_scalar_prefetch=1,
            grid=(1,),
            in_specs=[pl.BlockSpec(memory_space=pl.ANY)] * len(sources),
            out_specs=[pl.BlockSpec((rows, width), lambda i, at: (0, 0)) for rows in out_rows],
            scratch_shapes=[pltpu.SemaphoreType.DMA((len(plan),))],
        ),
        out_shape=[jax.ShapeDtypeStruct((rows, width), jnp.bfloat16) for rows in out_rows],
        compiler_params=pltpu.CompilerParams(vmem_limit_bytes=VMEM_LIMIT),
        cost_estimate=SMALL,
    )(at, *sources)


def base_kernel(blocks, target_ref, own_ref, place_ref, front_ref, factor_ref, col_ref, given_ref, out_ref):
    factor = factor_ref[...]
    for block in range(blocks):
        here = pl.ds(block * BLK, BLK)
        own = pl.ds(pl.multiple_of(place_ref[block] * BLK, BLK), BLK)
        product = lax.dot_general(factor, col_ref[own, :], NT, preferred_element_type=jnp.float32)
        kept = (front_ref[:, own].astype(jnp.float32) - product).astype(jnp.bfloat16)
        out_ref[:, here] = given_ref[:, here].astype(jnp.float32) + kept.astype(jnp.float32)


def kept_rows(targets, owns, places, front, factor, col_side, given):
    count = targets.shape[0]
    cols = front.shape[1]
    pivots = factor.shape[1]
    return pl.pallas_call(
        functools.partial(base_kernel, cols // BLK),
        grid_spec=pltpu.PrefetchScalarGridSpec(
            num_scalar_prefetch=3,
            grid=(count,),
            in_specs=[
                pl.BlockSpec((BLK, cols), lambda i, targets, owns, places: (owns[i], 0)),
                pl.BlockSpec((BLK, pivots), lambda i, targets, owns, places: (owns[i], 0)),
                pl.BlockSpec(col_side.shape, lambda i, targets, owns, places: (0, 0)),
                pl.BlockSpec((BLK, cols), lambda i, targets, owns, places: (targets[i], 0)),
            ],
            out_specs=pl.BlockSpec((BLK, cols), lambda i, targets, owns, places: (targets[i], 0)),
        ),
        out_shape=jax.ShapeDtypeStruct(given.shape, jnp.float32),
        compiler_params=pltpu.CompilerParams(vmem_limit_bytes=VMEM_LIMIT),
        cost_estimate=SMALL,
    )(targets, owns, places, front, factor, col_side, given)


def add_kernel(blocks, pieces, target_ref, place_ref, *refs):
    piece_refs, base_ref, out_ref = refs[:pieces], refs[-2], refs[-1]
    for block in range(blocks):
        here = pl.ds(block * BLK, BLK)
        arrived = piece_refs[0][:, pl.ds(pl.multiple_of(place_ref[0, block] * BLK, BLK), BLK)]
        if pieces == 2:
            other = piece_refs[1][:, pl.ds(pl.multiple_of(place_ref[1, block] * BLK, BLK), BLK)]
            arrived = jnp.where(place_ref[2, block] == 0, arrived, other)
        out_ref[:, here] = base_ref[:, here] + arrived.astype(jnp.float32)


def add_rows(base, targets, places, pieces, first=0):
    parts = BLK // STEP
    skip = first // STEP
    count = pieces[0].shape[0] // STEP
    cols = base.shape[1]
    row = pl.BlockSpec(
        (STEP, cols),
        lambda i, targets, places: (targets[(i + skip) // parts] * parts + (i + skip) % parts, 0),
    )
    in_specs = [pl.BlockSpec((STEP, piece.shape[1]), lambda i, *_: (i, 0)) for piece in pieces]
    return pl.pallas_call(
        functools.partial(add_kernel, cols // BLK, len(pieces)),
        grid_spec=pltpu.PrefetchScalarGridSpec(
            num_scalar_prefetch=2, grid=(count,), in_specs=in_specs + [row], out_specs=row
        ),
        out_shape=jax.ShapeDtypeStruct(base.shape, jnp.float32),
        input_output_aliases={2 + len(pieces): 0},
        compiler_params=pltpu.CompilerParams(vmem_limit_bytes=VMEM_LIMIT),
        cost_estimate=SMALL,
    )(targets, places, *pieces, base)


def take_block(table, first, count):
    return lax.dynamic_slice_in_dim(table, first, count, 0)


def hop(up_block, down_block, up, down):
    return lax.ppermute(up_block, "col", up), lax.ppermute(down_block, "col", down)


UP = [(0, 1), (1, 2), (2, 3)]
DOWN = [(1, 0), (2, 1), (3, 2)]
FAR = [(2, 3), (1, 0)]


def other_core(block):
    return lax.ppermute(block, "row", [(0, 1), (1, 0)])


def segment_at(segment, at_ref):
    away = segment - at_ref[0]
    far = jnp.where(away == 2, 4, 5)
    near = jnp.where(away == -1, 1, jnp.where(away == 1, 2, jnp.where(away == -2, 3, far)))
    return jnp.where(away == 0, 0, near)


def col_pieces(at, sources):
    size = sources[0].shape[0]
    half = size // 2
    plan = []
    for index in range(4):
        segment = index // 2
        choice = functools.partial(lambda segment, at_ref: segment_at(at_ref[0] % 2 * 2 + segment, at_ref), segment)
        plan.append((index, 0, half, choice, {k: (k, index % 2 * half) for k in range(5)}))
    return plan, [half] * 4


def owned_cols(at, pieces, swapped):
    size = pieces[0].shape[0]
    plan = [
        (0, i * size, size, lambda at_ref: jnp.where(at_ref[1] == at_ref[0] // 2, 0, 1), {0: (i, 0), 1: (4 + i, 0)})
        for i in range(4)
    ]
    return assembled(at, [*pieces, *swapped], plan, [4 * size])[0]


def factor_of(panel, inverse, fill, first_row):
    local_rows = panel.shape[0]
    positions = (first_row + jnp.arange(local_rows, dtype=jnp.int32)) // BLK
    blocks = jnp.arange(fill.shape[0], dtype=jnp.int32)
    row_fill = jnp.sum(
        (positions[:, None] == blocks[None, :]).astype(jnp.int32) * fill[None, :], axis=1
    )
    masked = panel * row_fill[:, None].astype(jnp.bfloat16)
    return jnp.dot(masked, jnp.triu(inverse), preferred_element_type=jnp.float32).astype(jnp.bfloat16)


def from_sibling(block):
    route = []
    for low in range(0, lax.axis_size("front"), 2):
        route += [(low, low + 1), (low + 1, low)]
    return lax.ppermute(block, "front", route)


def shards(front, panel, inverse, fill, block_map, parent_front):
    front, panel, given = front[0], panel[0], parent_front[0]
    col_count = lax.axis_size("col")
    row_count = lax.axis_size("row")
    core = lax.axis_index("row")
    place = lax.axis_index("col")
    parity = lax.axis_index("front") % 2
    local_rows = panel.shape[0]
    tile_rows, tile_cols = front.shape
    half_blocks = tile_rows // 2 // BLK
    col_blocks = tile_cols // BLK
    seg = local_rows // BLK
    row_base = core * (tile_rows // BLK)
    sibling_map = from_sibling(block_map[0])
    source = block_inverse(block_map[0])
    col_source = take_block(source, place * col_blocks, col_blocks) - place * col_blocks
    first_row = (core * col_count + place) * local_rows

    closed = half_blocks % col_blocks == 0
    line = (
        row_count == 2 and col_count == 4 and closed and tile_rows == 2 * tile_cols
        and local_rows % (2 * BLK) == 0 and 2 * local_rows == tile_cols
    )
    if not line:
        factor = factor_of(panel, inverse[0], fill[0], first_row)
        all_rows = lax.all_gather(factor, ("row", "col"), axis=0, tiled=True)
        row_side = take_block(all_rows, core * tile_rows, tile_rows)
        col_side = take_block(all_rows, place * tile_cols, tile_cols)
        sent = take_block(source, row_base + (1 - parity) * half_blocks, half_blocks) - row_base
        owns = take_block(source, row_base + parity * half_blocks, half_blocks) - row_base
        targets = jnp.arange(half_blocks, dtype=jnp.int32)
        grid = (half_blocks, 1)
        arrived = from_sibling(updated_rows(
            front, sent, lambda i, at: at[i], row_side, lambda i, at: at[i], col_side, grid, BLK,
            tile_cols, 1, 0,
        ))
        sibling_cols = take_block(block_inverse(sibling_map), place * col_blocks, col_blocks)
        sibling_cols = sibling_cols - place * col_blocks
        base = kept_rows(targets, owns, col_source, front, row_side, col_side, given)
        out = add_rows(base, targets, sibling_cols[None], [arrived])
        return factor[None], out[None]

    cut = seg // 2
    unit = cut * BLK
    parts = BLK // STEP
    at = jnp.stack([place, core, parity]).astype(jnp.int32)
    after = lax.optimization_barrier

    def sent_row(inner, per_block):
        def row(at):
            sent = 1 - at[2]
            return (sent * half_blocks + (at[2] if inner else sent) * seg) * per_block
        return row

    def raw_row(first):
        def row(i, at):
            index = i + first
            in_cut = cut * parts
            inner = index < in_cut
            start = jnp.where(inner, sent_row(True, parts)(at), sent_row(False, parts)(at))
            return start + index - jnp.where(inner, 0, in_cut)
        return row

    raw = [
        picked_rows(front, at, raw_row(first), (count, 2), STEP, unit, 2) for first, count in RAW_PIECES
    ]
    raw[0] = from_sibling(raw[0])
    raw[1] = from_sibling(raw[1])
    factor = factor_of(panel, inverse[0], fill[0], first_row)
    factor, raw[0], sibling_map = after((factor, raw[0], sibling_map))
    below, above = hop(factor, factor, UP, DOWN)
    raw[2] = from_sibling(raw[2])
    below, above, raw[1] = after((below, above, raw[1]))
    below2, above2 = hop(below, above, UP[1:], DOWN[:2])
    raw[3] = jnp.concatenate([raw[3], factor[:unit].reshape(-1, raw[3].shape[1])], axis=0)
    raw[3] = from_sibling(raw[3])
    at2, raw[2] = after((at, raw[2]))
    near = [factor, below, above, below2, above2]
    plan, sizes = col_pieces(at2, near)
    plan.append((
        4, 0, local_rows, lambda at_ref: segment_at(jnp.where(at_ref[2] == 1, 1, 2), at_ref),
        {k: (k, 0) for k in range(5)},
    ))
    *pieces, inner_rows = assembled(at2, near, plan, sizes + [local_rows])
    col_side = owned_cols(at, pieces, [other_core(piece) for piece in pieces])
    far = lax.ppermute(jnp.where(place == 2, below2, above2), "col", FAR)

    def contribution(at, inner, first, rows, kind_x, factor):
        height = min(rows, BLK)
        start = sent_row(inner, BLK // height)
        skip = first // height
        grid, layout = ((rows // height, 2), (2, 1)) if kind_x else ((rows // height, 4), (1, 0))
        return from_sibling(updated_rows(
            front, at, lambda i, at: start(at) + skip + i, factor,
            lambda i, at: i + skip if inner else start(at) + skip + i, col_side, grid, height, unit, *layout,
        ))

    arrived = [contribution(at, True, 0, unit, True, inner_rows)]
    for i in range(cut):
        at_i = at
        if i == 0:
            raw[3], sibling_map = after((raw[3], sibling_map))
            at_i, sibling_map = after((at, other_core(sibling_map)))
        elif i == 2:
            at_i, arrived[0] = after((at, arrived[0]))
        arrived.append(contribution(at_i, True, unit + i * BLK, BLK, False, inner_rows))
    plan = [
        (0, k * local_rows, local_rows, functools.partial(segment_at, k), {j: (j, 0) for j in range(6)})
        for k in range(4)
    ]
    far, arrived[1] = after((far, arrived[1]))
    row_side = assembled(at, [*near, far], plan, [tile_rows])[0]
    arrived.append(contribution(at, False, 0, unit, True, row_side))

    sibling_part = raw[3][RAW_PIECES[3][1] * STEP:].reshape(unit, -1)
    raw[3] = raw[3][:RAW_PIECES[3][1] * STEP]
    part_below, part_above = hop(sibling_part, sibling_part, UP, DOWN)
    part_below, part_above, arrived[0] = after((part_below, part_above, arrived[0]))
    part_below2, part_above2 = hop(part_below, part_above, UP[1:], DOWN[:2])
    part_far = lax.ppermute(jnp.where(place == 2, part_below2, part_above2), "col", FAR)
    parts_near = [sibling_part, part_below, part_above, part_below2, part_above2]
    plan, sizes = col_pieces(at, parts_near)
    part_pieces = assembled(at, parts_near, plan, sizes)
    sibling_col = owned_cols(at, part_pieces, [other_core(piece) for piece in part_pieces])
    plan = [
        (0, k * unit, unit, functools.partial(
            lambda k, at_ref: segment_at(jnp.where(at_ref[2] == 0, 1 - k, 2 + k), at_ref), k
        ), {j: (j, 0) for j in range(6)})
        for k in range(2)
    ]
    part_rows = assembled(at, [*parts_near, part_far], plan, [2 * unit])[0]
    finished = updated_rows(
        jnp.concatenate(raw, axis=0), at, lambda i, at: i, part_rows, lambda i, at: i, sibling_col,
        (2 * cut, 2), BLK, unit, 1, 0,
    )

    kept_base = row_base + parity * half_blocks
    owns = take_block(source, kept_base, half_blocks) - row_base
    base = kept_rows(
        jnp.arange(half_blocks, dtype=jnp.int32), owns, col_source, front, row_side, col_side, given
    )
    sibling_cols = take_block(block_inverse(sibling_map), place * col_blocks, col_blocks)
    sibling_cols = sibling_cols - place * col_blocks
    landed = take_block(sibling_map, kept_base, half_blocks) - kept_base
    seg_at = sibling_cols // seg * cut
    seg_in = sibling_cols % seg
    places_x = jnp.stack([
        seg_at + jnp.minimum(seg_in, cut - 1),
        seg_at + jnp.maximum(seg_in - cut, 0),
        jnp.where(seg_in < cut, 0, 1),
    ])
    places_y = sibling_cols[None]
    kept_inner = (1 - parity) * seg
    kept_outer = seg - kept_inner

    def add(out, index):
        start = kept_inner if index <= cut else kept_outer
        which = index % (1 + cut)
        if which == 0:
            now = finished[:unit] if index == 0 else finished[unit:]
            return add_rows(out, take_block(landed, start, cut), places_x, [now, arrived[index]])
        targets = take_block(landed, start + cut + which - 1, 1)
        if isinstance(arrived[index], list):
            for piece, first in arrived[index]:
                out = add_rows(out, targets, places_y, [piece], first)
            return out
        return add_rows(out, targets, places_y, [arrived[index]])

    out, added = base, 0
    for i in range(cut):
        at_i, arrived[2 + i], out = after((at, arrived[2 + i], out))
        first = unit + i * BLK
        if i < cut - 1:
            arrived.append(contribution(at_i, False, first, BLK, False, row_side))
        else:
            arrived.append([
                (contribution(at_i, False, first + k, STEP, False, row_side), k) for k in range(0, BLK, STEP)
            ])
        for _ in range(2):
            out = add(out, added)
            added += 1
    while added < len(arrived):
        out = add(out, added)
        added += 1
    return factor[None], out[None]


def solution(mesh):
    placed = (
        P("front", "row", "col"),
        P("front", ("row", "col"), None),
        P("front", None, None),
        P("front", None),
        P("front", None),
        P("front", "row", "col"),
    )
    return jax.shard_map(
        shards,
        mesh=mesh,
        in_specs=placed,
        out_specs=(P("front", ("row", "col"), None), P("front", "row", "col")),
        check_vma=False,
    )
```

time: 934 us -> 433 us (0.46)
  waiting for transfers between devices: 497 us -> 176 us
  local copies, waits for them, and re-layouts: 262 us -> 16.2 us
  Pallas kernels: 0 us -> 180 us
  other arithmetic: 112 us -> 11.5 us
  starting transfers between devices: 1.5 us -> 45.6 us
  matrix products: 43.9 us -> 1.07 us
  between operations: 14.1 us -> 1.05 us
    ppermute x1 -> x33, waiting for transfers between devices: 379 us -> 176 us  [the longest x14 154 us: from_sibling(): return lax.ppermute(block, 'front', route)]
    gather x6 -> x0, local copies, waits for them, and re-layouts: 183 us -> none  [the longest x3 129 us: shards(): jnp.take(schur.reshape(row_blocks, BLK, tile_cols), row_source, axis=0)]
    pallas_call x0 -> x30, Pallas kernels: none -> 180 us  [the longest x10 59.1 us: updated_rows(): pl.pallas_call(functools.partial(update_kernel, unit, stride, offset), gr...]
    all_gather x1 -> x0, waiting for transfers between devices: 118 us -> none  [shards(): all_rows = lax.all_gather(factor, ('row', 'col'), axis=0, tiled=True)]
    unnamed x4 -> x36, local copies, waits for them, and re-layouts: 61.4 us -> 6.04 us
    ppermute x1 -> x33, starting transfers between devices: 1.46 us -> 45.6 us  [the longest x14 21.7 us: from_sibling(): return lax.ppermute(block, 'front', route)]
    dot_general x2 -> x1, matrix products: 43.9 us -> 1.07 us  [factor_of(): jnp.dot(masked, jnp.triu(inverse), preferred_element_type=jnp.float32)]
    broadcast_in_dim x1 -> x0, other arithmetic: 32.9 us -> none  [shards(): return (factor[None], parent[None])]
  transfers between devices with their start and end apart: 2 -> 33, of which waited for: 2 -> 20; matrix products, arithmetic and copies ran while one was open for 3% -> 5% of each run, Pallas kernels for 0% -> 40%
where the time goes in v2:
time: 433 us; the launch traced here: 431 us
  Pallas kernels  180 us (42%)
  waiting for transfers between devices  176 us (41%)
  starting transfers between devices  45.6 us (11%)
  local copies, waits for them, and re-layouts  16.2 us (4%)
  other arithmetic  11.5 us (3%)
    ppermute x14, waiting for transfers between devices, from_sibling(): return lax.ppermute(block, 'front', route)  154 us
    pallas_call x10, Pallas kernels, updated_rows(): pl.pallas_call(functools.partial(update_kernel, unit, stride, offset), gr...  59.1 us
    pallas_call x9, Pallas kernels, add_rows(): pl.pallas_call(functools.partial(add_kernel, cols // BLK, len(pieces)), g...  51.4 us
    pallas_call x1, Pallas kernels, kept_rows(): pl.pallas_call(functools.partial(base_kernel, cols // BLK), grid_spec=plt...  34.3 us
    ppermute x14, starting transfers between devices, from_sibling(): return lax.ppermute(block, 'front', route)  21.7 us
    pallas_call x4, Pallas kernels, picked_rows(): pl.pallas_call(pick_kernel, grid_spec=pltpu.PrefetchScalarGridSpec(num_sc...  17.4 us
    pallas_call x6, Pallas kernels, assembled(): pl.pallas_call(functools.partial(assemble_kernel, plan, len(sources)), gr...  17.4 us
    ppermute x4, waiting for transfers between devices, hop(): lax.ppermute(down_block, 'col', down)  14.7 us
  transfers between devices with their start and end apart: 33, of which 20 were waited for; matrix products, arithmetic and copies ran while one was open for 5% of the time, Pallas kernels for 40%

profile of v2, /device:TPU:0, one launch (start us, length us, event | category | flops | bytes accessed | tf_op | source)
XLA Modules:
  0.0 431.3 jit_solution(13027845744515814240)
XLA Ops:
  2.4 3.0 collective-permute-start
  5.5 6.0 %shard_map.79 = bf16[512,1536]{1,0:T(8,128)(2,1)} custom-call(s32[3]{0:T(128)S(1)} %pad_add_fusion.1.at_ref, bf16[6144,3072]{1,0:T(8,128)(2,1)} %bitcast.31), custom_call_target="tpu_custom_call" | custom-call | flops 1 | bytes 1 | tf_op jit(solution)/shard_map/pallas_call | solution.py:59
  15.1 3.9 collective-permute-start.4
  20.3 7.1 %shard_map.80 = bf16[640,1536]{1,0:T(8,128)(2,1)} custom-call(s32[3]{0:T(128)S(1)} %pad_add_fusion.1.at_ref, bf16[6144,3072]{1,0:T(8,128)(2,1)} %bitcast.32), custom_call_target="tpu_custom_call" | custom-call | flops 1 | bytes 1 | tf_op jit(solution)/shard_map/pallas_call | solution.py:59
  28.9 20.3 %collective-permute-done.6 = bf16[512,1536]{1,0:T(8,128)(2,1)} collective-permute-done((bf16[512,1536]{1,0:T(8,128)(2,1)}, bf16[512,1536]{1,0:T(8,128)(2,1)}, u32[]{:S(2)}, u32[]{:S(2)}) %collective-permute-start.6) | collective-permute-done | bytes 1572896 | tf_op jit(solution)/shard_map/ppermute | solution.py:232
  51.1 4.2 collective-permute-done.5.refs_2_
  58.4 2.7 shard_map.78
  63.0 2.2 reshape.67
  68.1 23.2 %collective-permute-done.10 = bf16[640,1536]{1,0:T(8,128)(2,1)} collective-permute-done((bf16[640,1536]{1,0:T(8,128)(2,1)}, bf16[640,1536]{1,0:T(8,128)(2,1)}, u32[]{:S(2)}, u32[]{:S(2)}) %collective-permute-start.10) | collective-permute-done | bytes 1966112 | tf_op jit(solution)/shard_map/ppermute | solution.py:232
  91.3 3.8 collective-permute-done.8.refs_4_
  95.0 3.0 shard_map.81
  104.6 2.5 shard_map.82.col_ref
  107.2 7.6 %shard_map.86 = bf16[768,1536]{1,0:T(8,128)(2,1)} custom-call(s32[3]{0:T(128)S(1)} %pad_add_fusion.1.at_ref, bf16[6144,3072]{1,0:T(8,128)(2,1)} %bitcast.34, bf16[1536,512]{1,0:T(8,128)(2,1)S(1)} %get-tuple-element.47.factor_ref, bf16[3072,512]{1,0:T(8,128)(2,1)} %shard_map.82.col_ref), custom_call_target="tpu_custom_call" | custom-call | flops 1 | bytes 1 | tf_op jit(solution)/shard_map/pallas_call | solution.py:36
  116.1 8.9 %collective-permute-done.2 = bf16[512,1536]{1,0:T(8,128)(2,1)} collective-permute-done((bf16[512,1536]{1,0:T(8,128)(2,1)S(1)}, bf16[512,1536]{1,0:T(8,128)(2,1)}, u32[]{:S(2)}, u32[]{:S(2)}) %collective-permute-start.2) | collective-permute-done | bytes 1572896 | tf_op jit(solution)/shard_map/ppermute | solution.py:232
  126.1 2.7 broadcast_select_fusion
  130.1 6.0 %shard_map.83 = bf16[256,3072]{1,0:T(8,128)(2,1)} custom-call(s32[3]{0:T(128)S(1)} %pad_add_fusion.1.at_ref, bf16[6144,3072]{1,0:T(8,128)(2,1)} %bitcast.35, bf16[1536,512]{1,0:T(8,128)(2,1)S(1)} %get-tuple-element.47.factor_ref, bf16[3072,512]{1,0:T(8,128)(2,1)} %shard_map.82.col_ref), custom_call_target="tpu_custom_call" | custom-call | flops 1 | bytes 1 | tf_op jit(solution)/shard_map/pallas_call | solution.py:36
  138.1 2.4 fusion.16
  141.8 6.7 %collective-permute-start.19 = (bf16[768,512]{1,0:T(8,128)(2,1)}, bf16[768,512]{1,0:T(8,128)(2,1)}, u32[]{:S(2)}, u32[]{:S(2)}) collective-permute-start(bf16[768,512]{1,0:T(8,128)(2,1)} %reshape.68.refs_0_), channel_id=1, source_target_pairs={{0,1},{1,2},{2,3},{4,5},{5,6},{6,7},{8,9},{9,10},{10,11},{12,13},{... | collective-permute-start | bytes 2359304 | tf_op jit(solution)/shard_map/ppermute | solution.py:178
  149.8 6.0 %shard_map.92 = bf16[256,3072]{1,0:T(8,128)(2,1)} custom-call(s32[3]{0:T(128)S(1)} %pad_add_fusion.1.at_ref, bf16[6144,3072]{1,0:T(8,128)(2,1)} %bitcast.36, bf16[1536,512]{1,0:T(8,128)(2,1)S(1)} %get-tuple-element.47.factor_ref, bf16[3072,512]{1,0:T(8,128)(2,1)} %shard_map.82.col_ref), custom_call_target="tpu_custom_call" | custom-call | flops 1 | bytes 1 | tf_op jit(solution)/shard_map/pallas_call | solution.py:36
  155.8 19.7 %collective-permute-done.17.refs_1_ = bf16[768,1536]{1,0:T(8,128)(2,1)} collective-permute-done((bf16[768,1536]{1,0:T(8,128)(2,1)}, bf16[768,1536]{1,0:T(8,128)(2,1)}, u32[]{:S(2)}, u32[]{:S(2)}) %collective-permute-start.17) | collective-permute-done | bytes 2359328 | tf_op jit(solution)/shard_map/ppermute | solution.py:232
  177.6 6.8 %collective-permute-done.20.refs_2_ = bf16[768,512]{1,0:T(8,128)(2,1)} collective-permute-done((bf16[768,512]{1,0:T(8,128)(2,1)}, bf16[768,512]{1,0:T(8,128)(2,1)}, u32[]{:S(2)}, u32[]{:S(2)}) %collective-permute-start.20) | collective-permute-done | bytes 786464 | tf_op jit(solution)/shard_map/ppermute | solution.py:178
  187.3 21.9 %collective-permute-done.15.refs_0_ = bf16[256,3072]{1,0:T(8,128)(2,1)} collective-permute-done((bf16[256,3072]{1,0:T(8,128)(2,1)}, bf16[256,3072]{1,0:T(8,128)(2,1)}, u32[]{:S(2)}, u32[]{:S(2)}) %collective-permute-start.15) | collective-permute-done | bytes 1572896 | tf_op jit(solution)/shard_map/ppermute | solution.py:232
  212.1 5.4 %shard_map.84.factor_ref = bf16[6144,512]{1,0:T(8,128)(2,1)} custom-call(s32[3]{0:T(128)S(1)} %pad_add_fusion.1.at_ref, bf16[1536,512]{1,0:T(8,128)(2,1)S(1)} %copy-done.3, bf16[1536,512]{1,0:T(8,128)(2,1)S(1)} %copy-done.7, bf16[1536,512]{1,0:T(8,128)(2,1)S(1)} %copy-done.9, bf16[1536,512]{1,0:T(8,128)(2,1)} %collective-permute-done.7.refs_3_, ...), custom_call_target="tpu_custom_call" | custom-call | flops 1 | bytes 1 | tf_op jit(solution)/shard_map/pallas_call | solution.py:92
  217.5 5.4 %pad_maximum_fusion.front_ref = bf16[1536,1536]{1,0:T(8,128)(2,1)} fusion(bf16[256,1536]{1,0:T(8,128)(2,1)S(1)} %copy-done.11, bf16[640,1536]{1,0:T(8,128)(2,1)} %collective-permute-done.10, bf16[512,1536]{1,0:T(8,128)(2,1)} %collective-permute-done.6, bf16[128,1536]{1,0:T(8,128)(2,1)S(1)} %collective-permute-done), kind=kLoop, calls=%fused_computation | loop fusion | flops 18874368 | bytes 9437184 | tf_op jit(solution)/shard_map/concatenate | solution.py:367
  223.0 6.7 %shard_map.85 = bf16[768,1536]{1,0:T(8,128)(2,1)} custom-call(s32[3]{0:T(128)S(1)} %pad_add_fusion.1.at_ref, bf16[6144,3072]{1,0:T(8,128)(2,1)} %bitcast.37, bf16[6144,512]{1,0:T(8,128)(2,1)} %shard_map.84.factor_ref, bf16[3072,512]{1,0:T(8,128)(2,1)S(1)} %copy-done), custom_call_target="tpu_custom_call" | custom-call | flops 1 | bytes 1 | tf_op jit(solution)/shard_map/pallas_call | solution.py:36
  231.6 4.9 %shard_map.87 = bf16[256,3072]{1,0:T(8,128)(2,1)S(1)} custom-call(s32[3]{0:T(128)S(1)} %pad_add_fusion.1.at_ref, bf16[6144,3072]{1,0:T(8,128)(2,1)} %bitcast.38, bf16[1536,512]{1,0:T(8,128)(2,1)S(1)} %get-tuple-element.47.factor_ref, bf16[3072,512]{1,0:T(8,128)(2,1)} %shard_map.82.col_ref), custom_call_target="tpu_custom_call" | custom-call | flops 1 | bytes 1 | tf_op jit(solution)/shard_map/pallas_call | solution.py:36
  240.7 2.3 collective-permute-done.28.refs_0_
  245.9 34.3 %shard_map.93.refs_2_ = f32[3072,3072]{1,0:T(8,128)} custom-call(s32[12]{0:T(128)S(1)} %iota.38.target_ref, s32[12]{0:T(128)S(1)} %get-tuple-element.93.own_ref, s32[12]{0:T(128)S(1)} %get-tuple-element.92.place_ref, bf16[6144,3072]{1,0:T(8,128)(2,1)} %bitcast.39, bf16[6144,512]{1,0:T(8,128)(2,1)} %shard_map.84.factor_ref, bf16[3072,512]{1,0:T(8,128)(2,1)S(1)} %copy-done.1, ...), custom_call_target="tpu_custom_call" | custom-call | flops 1 | bytes 1 | tf_op jit(solution)/shard_map/pallas_call | solution.py:121
  280.2 5.1 %shard_map.101 = bf16[256,3072]{1,0:T(8,128)(2,1)} custom-call(s32[3]{0:T(128)S(1)} %pad_add_fusion.1.at_ref, bf16[6144,3072]{1,0:T(8,128)(2,1)} %bitcast.40, bf16[6144,512]{1,0:T(8,128)(2,1)} %shard_map.84.factor_ref, bf16[3072,512]{1,0:T(8,128)(2,1)S(1)} %copy-done.1), custom_call_target="tpu_custom_call" | custom-call | flops 1 | bytes 1 | tf_op jit(solution)/shard_map/pallas_call | solution.py:36
  286.7 3.0 shard_map.88.factor_ref
  293.2 11.2 %shard_map.91 = bf16[1536,1536]{1,0:T(8,128)(2,1)} custom-call(s32[3]{0:T(128)S(1)} %pad_add_fusion.1.at_ref, bf16[1536,1536]{1,0:T(8,128)(2,1)} %pad_maximum_fusion.front_ref, bf16[1536,512]{1,0:T(8,128)(2,1)S(1)} %copy-done.5, bf16[1536,512]{1,0:T(8,128)(2,1)S(1)} %shard_map.90.col_ref), custom_call_target="tpu_custom_call" | custom-call | flops 1 | bytes 1 | tf_op jit(solution)/shard_map/pallas_call | solution.py:36
  304.4 2.7 fusion.15
  307.1 10.0 %shard_map.94.refs_1_ = f32[3072,3072]{1,0:T(8,128)} custom-call(s32[3]{0:T(128)S(1)} %get-tuple-element.85.target_ref, s32[3,12]{1,0:T(4,128)S(1)} %pad_add_fusion.place_ref, bf16[768,1536]{1,0:T(8,128)(2,1)S(1)} %get-tuple-element.81.refs_0_, bf16[768,1536]{1,0:T(8,128)(2,1)} %collective-permute-done.17.refs_1_, ...), custom_call_target="tpu_custom_call", output_to_operand_aliasing={{}: (4, {})} | custom-call | flops 1 | bytes 1 | tf_op jit(solution)/shard_map/pallas_call | solution.py:161
  317.1 4.9 %shard_map.95.refs_1_ = f32[3072,3072]{1,0:T(8,128)} custom-call(s32[1]{0:T(128)} %get-tuple-element.89.target_ref, s32[1,12]{1,0:T(1,128)S(1)} %bitcast.23, bf16[256,3072]{1,0:T(8,128)(2,1)} %collective-permute-done.15.refs_0_, f32[3072,3072]{1,0:T(8,128)} %shard_map.94.refs_1_), custom_call_target="tpu_custom_call", output_to_operand_aliasing={{}: (3, {})} | custom-call | flops 1 | bytes 1 | tf_op jit(solution)/shard_map/pallas_call | solution.py:161
  322.0 5.2 %collective-permute-done.18.refs_0_ = bf16[256,3072]{1,0:T(8,128)(2,1)S(1)} collective-permute-done((bf16[256,3072]{1,0:T(8,128)(2,1)S(1)}, bf16[256,3072]{1,0:T(8,128)(2,1)S(1)}, u32[]{:S(2)}, u32[]{:S(2)}) %collective-permute-start.18) | collective-permute-done | bytes 1572896 | tf_op jit(solution)/shard_map/ppermute | solution.py:232
  327.1 4.0 shard_map.100
  333.2 4.8 %shard_map.96.refs_1_ = f32[3072,3072]{1,0:T(8,128)} custom-call(s32[1]{0:T(128)} %get-tuple-element.88.target_ref, s32[1,12]{1,0:T(1,128)S(1)} %bitcast.24, bf16[256,3072]{1,0:T(8,128)(2,1)} %collective-permute-done.28.refs_0_, f32[3072,3072]{1,0:T(8,128)} %shard_map.95.refs_1_), custom_call_target="tpu_custom_call", output_to_operand_aliasing={{}: (3, {})} | custom-call | flops 1 | bytes 1 | tf_op jit(solution)/shard_map/pallas_call | solution.py:161
  338.0 4.5 %shard_map.97.refs_2_ = f32[3072,3072]{1,0:T(8,128)} custom-call(s32[1]{0:T(128)} %get-tuple-element.90.target_ref, s32[1,12]{1,0:T(1,128)S(1)} %bitcast.25, bf16[256,3072]{1,0:T(8,128)(2,1)S(1)} %collective-permute-done.18.refs_0_, f32[3072,3072]{1,0:T(8,128)} %shard_map.96.refs_1_), custom_call_target="tpu_custom_call", output_to_operand_aliasing={{}: (3, {})} | custom-call | flops 1 | bytes 1 | tf_op jit(solution)/shard_map/pallas_call | solution.py:161
  342.5 3.8 shard_map.99
  346.4 3.8 shard_map.98
  352.2 10.0 %shard_map.102.refs_1_ = f32[3072,3072]{1,0:T(8,128)} custom-call(s32[3]{0:T(128)S(1)} %get-tuple-element.84.target_ref, s32[3,12]{1,0:T(4,128)S(1)} %pad_add_fusion.place_ref, bf16[768,1536]{1,0:T(8,128)(2,1)S(1)} %get-tuple-element.80.refs_0_, bf16[768,1536]{1,0:T(8,128)(2,1)} %collective-permute-done.16.refs_1_, ...), custom_call_target="tpu_custom_call", output_to_operand_aliasing={{}: (4, {})} | custom-call | flops 1 | bytes 1 | tf_op jit(solution)/shard_map/pallas_call | solution.py:161
  362.2 4.9 %shard_map.103.refs_1_ = f32[3072,3072]{1,0:T(8,128)} custom-call(s32[1]{0:T(128)} %get-tuple-element.86.target_ref, s32[1,12]{1,0:T(1,128)S(1)} %bitcast.26, bf16[256,3072]{1,0:T(8,128)(2,1)} %collective-permute-done.32.refs_0_, f32[3072,3072]{1,0:T(8,128)} %shard_map.102.refs_1_), custom_call_target="tpu_custom_call", output_to_operand_aliasing={{}: (3, {})} | custom-call | flops 1 | bytes 1 | tf_op jit(solution)/shard_map/pallas_call | solution.py:161
  367.2 27.4 %collective-permute-done.31.refs_0_ = bf16[256,3072]{1,0:T(8,128)(2,1)S(1)} collective-permute-done((bf16[256,3072]{1,0:T(8,128)(2,1)S(1)}, bf16[256,3072]{1,0:T(8,128)(2,1)S(1)}, u32[]{:S(2)}, u32[]{:S(2)}) %collective-permute-start.31) | collective-permute-done | bytes 1572896 | tf_op jit(solution)/shard_map/ppermute | solution.py:232
  394.5 4.4 %shard_map.104.refs_1_ = f32[3072,3072]{1,0:T(8,128)} custom-call(s32[1]{0:T(128)} %get-tuple-element.87.target_ref, s32[1,12]{1,0:T(1,128)S(1)} %bitcast.27, bf16[256,3072]{1,0:T(8,128)(2,1)S(1)} %collective-permute-done.31.refs_0_, f32[3072,3072]{1,0:T(8,128)} %shard_map.103.refs_1_), custom_call_target="tpu_custom_call", output_to_operand_aliasing={{}: (3, {})} | custom-call | flops 1 | bytes 1 | tf_op jit(solution)/shard_map/pallas_call | solution.py:161
  399.0 12.4 %collective-permute-done.30.refs_0_ = bf16[128,3072]{1,0:T(8,128)(2,1)S(1)} collective-permute-done((bf16[128,3072]{1,0:T(8,128)(2,1)S(1)}, bf16[128,3072]{1,0:T(8,128)(2,1)S(1)}, u32[]{:S(2)}, u32[]{:S(2)}) %collective-permute-start.30) | collective-permute-done | bytes 786464 | tf_op jit(solution)/shard_map/ppermute | solution.py:232
  411.4 3.9 shard_map.105.refs_1_
  415.3 12.1 %collective-permute-done.29.refs_0_ = bf16[128,3072]{1,0:T(8,128)(2,1)S(1)} collective-permute-done((bf16[128,3072]{1,0:T(8,128)(2,1)S(1)}, bf16[128,3072]{1,0:T(8,128)(2,1)S(1)}, u32[]{:S(2)}, u32[]{:S(2)}) %collective-permute-start.29) | collective-permute-done | bytes 786464 | tf_op jit(solution)/shard_map/ppermute | solution.py:232
  427.4 3.9 shard_map.106
  (109 shorter events, 58.6 us)
Async XLA Ops:
  0.7 4.7 %copy-start.16 = (s32[1,48]{1,0:T(1,128)S(1)}, s32[1,48]{1,0:T(1,128)}, u32[]{:S(2)}) copy-start(s32[1,48]{1,0:T(1,128)} %param.10) | copy-start | bytes 580
  2.4 12.7 %collective-permute-start = (bf16[128,1536]{1,0:T(8,128)(2,1)S(1)}, bf16[128,1536]{1,0:T(8,128)(2,1)S(1)}, u32[]{:S(2)}, u32[]{:S(2)}) collective-permute-start(bf16[128,1536]{1,0:T(8,128)(2,1)S(1)} %shard_map.77), channel_id=1, source_target_pairs={{0,8},{8,0},{16,24},{24,16},{1,9},{9,1},{17,25},{25,17},{2,10},{10... | collective-permute-start | bytes 1179656 | tf_op jit(solution)/shard_map/ppermute | solution.py:232
  5.4 8.1 %copy-start.13 = (s32[1,48]{1,0:T(1,128)S(1)}, s32[1,48]{1,0:T(1,128)}, u32[]{:S(2)}) copy-start(s32[1,48]{1,0:T(1,128)} %param.9) | copy-start | bytes 580
  5.4 8.3 %copy-start.14 = (bf16[1,1536,512]{2,1,0:T(8,128)(2,1)S(1)}, bf16[1,1536,512]{2,1,0:T(8,128)(2,1)}, u32[]{:S(2)}) copy-start(bf16[1,1536,512]{2,1,0:T(8,128)(2,1)} %param.7) | copy-start | bytes 4718596
  5.4 8.3 %copy-start.15 = (bf16[1,512,512]{2,1,0:T(8,128)(2,1)S(1)}, bf16[1,512,512]{2,1,0:T(8,128)(2,1)}, u32[]{:S(2)}) copy-start(bf16[1,512,512]{2,1,0:T(8,128)(2,1)} %param.8) | copy-start | bytes 1572868
  5.4 9.7 %collective-permute-start.1 = (s32[48]{0:T(128)S(1)}, s32[48]{0:T(128)S(1)}, u32[]{:S(2)}, u32[]{:S(2)}) collective-permute-start(s32[48]{0:T(128)S(1)} %bitcast.47), channel_id=1, source_target_pairs={{0,8},{8,0},{16,24},{24,16},{1,9},{9,1},{17,25},{25,17},{2,10},{10... | collective-permute-start | bytes 584 | tf_op jit(solution)/shard_map/ppermute | solution.py:232
  11.5 37.6 %collective-permute-start.6 = (bf16[512,1536]{1,0:T(8,128)(2,1)}, bf16[512,1536]{1,0:T(8,128)(2,1)}, u32[]{:S(2)}, u32[]{:S(2)}) collective-permute-start(bf16[512,1536]{1,0:T(8,128)(2,1)} %shard_map.79), channel_id=1, source_target_pairs={{0,8},{8,0},{16,24},{24,16},{1,9},{9,1},{17,25},{25,17},{2,10},{10... | collective-permute-start | bytes 4718600 | tf_op jit(solution)/shard_map/ppermute | solution.py:232
  14.8 46.3 %copy-start.2 = (bf16[1536,512]{1,0:T(8,128)(2,1)}, bf16[1536,512]{1,0:T(8,128)(2,1)S(1)}, u32[]{:S(2)}) copy-start(bf16[1536,512]{1,0:T(8,128)(2,1)S(1)} %convolution_convert_fusion.refs_0_) | copy-start | bytes 4718596
  15.1 36.0 %collective-permute-start.4 = (bf16[1536,512]{1,0:T(8,128)(2,1)S(1)}, bf16[1536,512]{1,0:T(8,128)(2,1)S(1)}, u32[]{:S(2)}, u32[]{:S(2)}) collective-permute-start(bf16[1536,512]{1,0:T(8,128)(2,1)S(1)} %convolution_convert_fusion.refs_0_), channel_id=1, source_target_pairs={{0,1},{1,2},{2,3},{4,5},{5,6},{6,7},{8,9},{9,10},{10,11},{12,13},{... | collective-permute-start | bytes 4718600 | tf_op jit(solution)/shard_map/ppermute | solution.py:178
  19.0 36.3 %collective-permute-start.5 = (bf16[1536,512]{1,0:T(8,128)(2,1)S(1)}, bf16[1536,512]{1,0:T(8,128)(2,1)S(1)}, u32[]{:S(2)}, u32[]{:S(2)}) collective-permute-start(bf16[1536,512]{1,0:T(8,128)(2,1)S(1)} %convolution_convert_fusion.refs_0_), channel_id=1, source_target_pairs={{1,0},{2,1},{3,2},{5,4},{6,5},{7,6},{9,8},{10,9},{11,10},{13,12},{... | collective-permute-start | bytes 4718600 | tf_op jit(solution)/shard_map/ppermute | solution.py:178
  27.4 63.9 %collective-permute-start.10 = (bf16[640,1536]{1,0:T(8,128)(2,1)}, bf16[640,1536]{1,0:T(8,128)(2,1)}, u32[]{:S(2)}, u32[]{:S(2)}) collective-permute-start(bf16[640,1536]{1,0:T(8,128)(2,1)} %shard_map.80), channel_id=1, source_target_pairs={{0,8},{8,0},{16,24},{24,16},{1,9},{9,1},{17,25},{25,17},{2,10},{10... | collective-permute-start | bytes 5898248 | tf_op jit(solution)/shard_map/ppermute | solution.py:232
  51.1 10.0 %copy-start.6 = (bf16[1536,512]{1,0:T(8,128)(2,1)}, bf16[1536,512]{1,0:T(8,128)(2,1)S(1)}, u32[]{:S(2)}) copy-start(bf16[1536,512]{1,0:T(8,128)(2,1)S(1)} %collective-permute-done.4.refs_1_) | copy-start | bytes 4718596
  55.3 5.8 %copy-start.8 = (bf16[1536,512]{1,0:T(8,128)(2,1)}, bf16[1536,512]{1,0:T(8,128)(2,1)S(1)}, u32[]{:S(2)}) copy-start(bf16[1536,512]{1,0:T(8,128)(2,1)S(1)} %collective-permute-done.5.refs_2_) | copy-start | bytes 4718596
  55.3 36.0 %collective-permute-start.7 = (bf16[1536,512]{1,0:T(8,128)(2,1)S(1)}, bf16[1536,512]{1,0:T(8,128)(2,1)}, u32[]{:S(2)}, u32[]{:S(2)}) collective-permute-start(bf16[1536,512]{1,0:T(8,128)(2,1)S(1)} %collective-permute-done.4.refs_1_), channel_id=1, source_target_pairs={{1,2},{2,3},{5,6},{6,7},{9,10},{10,11},{13,14},{14,15},{17,18},{18... | collective-permute-start | bytes 4718600 | tf_op jit(solution)/shard_map/ppermute | solution.py:178
  57.2 37.9 %collective-permute-start.8 = (bf16[1536,512]{1,0:T(8,128)(2,1)S(1)}, bf16[1536,512]{1,0:T(8,128)(2,1)}, u32[]{:S(2)}, u32[]{:S(2)}) collective-permute-start(bf16[1536,512]{1,0:T(8,128)(2,1)S(1)} %collective-permute-done.5.refs_2_), channel_id=1, source_target_pairs={{1,0},{2,1},{5,4},{6,5},{9,8},{10,9},{13,12},{14,13},{17,16},{18,1... | collective-permute-start | bytes 4718600 | tf_op jit(solution)/shard_map/ppermute | solution.py:178
  66.7 58.3 %collective-permute-start.2 = (bf16[512,1536]{1,0:T(8,128)(2,1)S(1)}, bf16[512,1536]{1,0:T(8,128)(2,1)}, u32[]{:S(2)}, u32[]{:S(2)}) collective-permute-start(bf16[512,1536]{1,0:T(8,128)(2,1)S(1)} %pad_maximum_fusion.1), channel_id=1, source_target_pairs={{0,8},{8,0},{16,24},{24,16},{1,9},{9,1},{17,25},{25,17},{2,10},{10... | collective-permute-start | bytes 4718600 | tf_op jit(solution)/shard_map/ppermute | solution.py:232
  98.0 2.4 collective-permute-start.11
  98.1 3.4 collective-permute-start.12
  98.6 4.0 collective-permute-start.13
  98.7 5.1 %collective-permute-start.14 = (bf16[768,512]{1,0:T(8,128)(2,1)S(1)}, bf16[768,512]{1,0:T(8,128)(2,1)S(1)}, u32[]{:S(2)}, u32[]{:S(2)}) collective-permute-start(bf16[768,512]{1,0:T(8,128)(2,1)S(1)} %get-tuple-element.51.refs_3_), channel_id=1, source_target_pairs={{0,4},{4,0},{1,5},{5,1},{2,6},{6,2},{3,7},{7,3},{8,12},{12,8},{9,1... | collective-permute-start | bytes 2359304 | tf_op jit(solution)/shard_map/ppermute | solution.py:187
  114.8 60.8 %collective-permute-start.17 = (bf16[768,1536]{1,0:T(8,128)(2,1)}, bf16[768,1536]{1,0:T(8,128)(2,1)}, u32[]{:S(2)}, u32[]{:S(2)}) collective-permute-start(bf16[768,1536]{1,0:T(8,128)(2,1)} %shard_map.86), channel_id=1, source_target_pairs={{0,8},{8,0},{16,24},{24,16},{1,9},{9,1},{17,25},{25,17},{2,10},{10... | collective-permute-start | bytes 7077896 | tf_op jit(solution)/shard_map/ppermute | solution.py:232
  125.0 1.1 collective-permute-start.3
  128.8 58.5 %collective-permute-start.9 = (bf16[1536,512]{1,0:T(8,128)(2,1)}, bf16[1536,512]{1,0:T(8,128)(2,1)}, u32[]{:S(2)}, u32[]{:S(2)}) collective-permute-start(bf16[1536,512]{1,0:T(8,128)(2,1)} %broadcast_select_fusion), channel_id=1, source_target_pairs={{2,3},{1,0},{6,7},{5,4},{10,11},{9,8},{14,15},{13,12},{18,19},{17,... | collective-permute-start | bytes 4718600 | tf_op jit(solution)/shard_map/ppermute | solution.py:320
  136.2 73.1 %collective-permute-start.15 = (bf16[256,3072]{1,0:T(8,128)(2,1)}, bf16[256,3072]{1,0:T(8,128)(2,1)}, u32[]{:S(2)}, u32[]{:S(2)}) collective-permute-start(bf16[256,3072]{1,0:T(8,128)(2,1)} %shard_map.83), channel_id=1, source_target_pairs={{0,8},{8,0},{16,24},{24,16},{1,9},{9,1},{17,25},{25,17},{2,10},{10... | collective-permute-start | bytes 4718600 | tf_op jit(solution)/shard_map/ppermute | solution.py:232
  141.7 35.8 %copy-start.17 = (s32[1,48]{1,0:T(1,128)S(1)}, s32[1,48]{1,0:T(1,128)}, u32[]{:S(2)}) copy-start(s32[1,48]{1,0:T(1,128)} %param.10) | copy-start | bytes 580
  141.7 67.5 %copy-start.3 = (bf16[1536,512]{1,0:T(8,128)(2,1)S(1)}, bf16[1536,512]{1,0:T(8,128)(2,1)}, u32[]{:S(2)}) copy-start(bf16[1536,512]{1,0:T(8,128)(2,1)} %copy-done.2) | copy-start | bytes 4718596
  141.8 35.9 %collective-permute-start.19 = (bf16[768,512]{1,0:T(8,128)(2,1)}, bf16[768,512]{1,0:T(8,128)(2,1)}, u32[]{:S(2)}, u32[]{:S(2)}) collective-permute-start(bf16[768,512]{1,0:T(8,128)(2,1)} %reshape.68.refs_0_), channel_id=1, source_target_pairs={{0,1},{1,2},{2,3},{4,5},{5,6},{6,7},{8,9},{9,10},{10,11},{12,13},{... | collective-permute-start | bytes 2359304 | tf_op jit(solution)/shard_map/ppermute | solution.py:178
  148.5 35.9 %collective-permute-start.20 = (bf16[768,512]{1,0:T(8,128)(2,1)}, bf16[768,512]{1,0:T(8,128)(2,1)}, u32[]{:S(2)}, u32[]{:S(2)}) collective-permute-start(bf16[768,512]{1,0:T(8,128)(2,1)} %reshape.68.refs_0_), channel_id=1, source_target_pairs={{1,0},{2,1},{3,2},{5,4},{6,5},{7,6},{9,8},{10,9},{11,10},{13,12},{... | collective-permute-start | bytes 2359304 | tf_op jit(solution)/shard_map/ppermute | solution.py:178
  175.6 67.4 %collective-permute-start.28 = (bf16[256,3072]{1,0:T(8,128)(2,1)}, bf16[256,3072]{1,0:T(8,128)(2,1)}, u32[]{:S(2)}, u32[]{:S(2)}) collective-permute-start(bf16[256,3072]{1,0:T(8,128)(2,1)} %shard_map.92), channel_id=1, source_target_pairs={{0,8},{8,0},{16,24},{24,16},{1,9},{9,1},{17,25},{25,17},{2,10},{10... | collective-permute-start | bytes 4718600 | tf_op jit(solution)/shard_map/ppermute | solution.py:232
  184.4 52.3 %collective-permute-start.21 = (bf16[768,512]{1,0:T(8,128)(2,1)}, bf16[768,512]{1,0:T(8,128)(2,1)}, u32[]{:S(2)}, u32[]{:S(2)}) collective-permute-start(bf16[768,512]{1,0:T(8,128)(2,1)} %collective-permute-done.19.refs_1_), channel_id=1, source_target_pairs={{1,2},{2,3},{5,6},{6,7},{9,10},{10,11},{13,14},{14,15},{17,18},{18... | collective-permute-start | bytes 2359304 | tf_op jit(solution)/shard_map/ppermute | solution.py:178
  186.0 50.7 %collective-permute-start.22 = (bf16[768,512]{1,0:T(8,128)(2,1)}, bf16[768,512]{1,0:T(8,128)(2,1)}, u32[]{:S(2)}, u32[]{:S(2)}) collective-permute-start(bf16[768,512]{1,0:T(8,128)(2,1)} %collective-permute-done.20.refs_2_), channel_id=1, source_target_pairs={{1,0},{2,1},{5,4},{6,5},{9,8},{10,9},{13,12},{14,13},{17,16},{18,1... | collective-permute-start | bytes 2359304 | tf_op jit(solution)/shard_map/ppermute | solution.py:178
  209.3 1.4 copy-start.7
  210.7 1.4 copy-start.9
  212.1 5.4 %copy-start.11 = (bf16[256,1536]{1,0:T(8,128)(2,1)S(1)}, bf16[256,1536]{1,0:T(8,128)(2,1)}, u32[]{:S(2)}) copy-start(bf16[256,1536]{1,0:T(8,128)(2,1)} %get-tuple-element.83) | copy-start | bytes 2359300
  217.5 5.4 %copy-start = (bf16[3072,512]{1,0:T(8,128)(2,1)S(1)}, bf16[3072,512]{1,0:T(8,128)(2,1)}, u32[]{:S(2)}) copy-start(bf16[3072,512]{1,0:T(8,128)(2,1)} %shard_map.82.col_ref) | copy-start | bytes 9437188
  229.6 7.1 %copy-start.4 = (bf16[768,512]{1,0:T(8,128)(2,1)S(1)}, bf16[768,512]{1,0:T(8,128)(2,1)}, u32[]{:S(2)}) copy-start(bf16[768,512]{1,0:T(8,128)(2,1)} %reshape.68.refs_0_) | copy-start | bytes 2359300
  229.6 112.9 %collective-permute-start.16 = (bf16[768,1536]{1,0:T(8,128)(2,1)}, bf16[768,1536]{1,0:T(8,128)(2,1)}, u32[]{:S(2)}, u32[]{:S(2)}) collective-permute-start(bf16[768,1536]{1,0:T(8,128)(2,1)} %shard_map.85), channel_id=1, source_target_pairs={{0,8},{8,0},{16,24},{24,16},{1,9},{9,1},{17,25},{25,17},{2,10},{10... | collective-permute-start | bytes 7077896 | tf_op jit(solution)/shard_map/ppermute | solution.py:232
  236.6 90.5 %collective-permute-start.18 = (bf16[256,3072]{1,0:T(8,128)(2,1)S(1)}, bf16[256,3072]{1,0:T(8,128)(2,1)S(1)}, u32[]{:S(2)}, u32[]{:S(2)}) collective-permute-start(bf16[256,3072]{1,0:T(8,128)(2,1)S(1)} %shard_map.87), channel_id=1, source_target_pairs={{0,8},{8,0},{16,24},{24,16},{1,9},{9,1},{17,25},{25,17},{2,10},{10... | collective-permute-start | bytes 4718600 | tf_op jit(solution)/shard_map/ppermute | solution.py:232
  236.7 9.2 %copy-start.1 = (bf16[3072,512]{1,0:T(8,128)(2,1)S(1)}, bf16[3072,512]{1,0:T(8,128)(2,1)}, u32[]{:S(2)}) copy-start(bf16[3072,512]{1,0:T(8,128)(2,1)} %shard_map.82.col_ref) | copy-start | bytes 9437188
  238.9 6.3 %collective-permute-start.24 = (bf16[384,512]{1,0:T(8,128)(2,1)S(1)}, bf16[384,512]{1,0:T(8,128)(2,1)S(1)}, u32[]{:S(2)}, u32[]{:S(2)}) collective-permute-start(bf16[384,512]{1,0:T(8,128)(2,1)S(1)} %get-tuple-element.62.refs_0_), channel_id=1, source_target_pairs={{0,4},{4,0},{1,5},{5,1},{2,6},{6,2},{3,7},{7,3},{8,12},{12,8},{9,1... | collective-permute-start | bytes 1179656 | tf_op jit(solution)/shard_map/ppermute | solution.py:187
  238.9 6.3 %collective-permute-start.25 = (bf16[384,512]{1,0:T(8,128)(2,1)S(1)}, bf16[384,512]{1,0:T(8,128)(2,1)S(1)}, u32[]{:S(2)}, u32[]{:S(2)}) collective-permute-start(bf16[384,512]{1,0:T(8,128)(2,1)S(1)} %get-tuple-element.63.refs_1_), channel_id=1, source_target_pairs={{0,4},{4,0},{1,5},{5,1},{2,6},{6,2},{3,7},{7,3},{8,12},{12,8},{9,1... | collective-permute-start | bytes 1179656 | tf_op jit(solution)/shard_map/ppermute | solution.py:187
  243.0 43.7 %collective-permute-start.23 = (bf16[768,512]{1,0:T(8,128)(2,1)S(1)}, bf16[768,512]{1,0:T(8,128)(2,1)S(1)}, u32[]{:S(2)}, u32[]{:S(2)}) collective-permute-start(bf16[768,512]{1,0:T(8,128)(2,1)S(1)} %broadcast_select_fusion.1), channel_id=1, source_target_pairs={{2,3},{1,0},{6,7},{5,4},{10,11},{9,8},{14,15},{13,12},{18,19},{17,... | collective-permute-start | bytes 2359304 | tf_op jit(solution)/shard_map/ppermute | solution.py:354
  245.2 40.1 %collective-permute-start.26 = (bf16[384,512]{1,0:T(8,128)(2,1)S(1)}, bf16[384,512]{1,0:T(8,128)(2,1)S(1)}, u32[]{:S(2)}, u32[]{:S(2)}) collective-permute-start(bf16[384,512]{1,0:T(8,128)(2,1)S(1)} %get-tuple-element.64.refs_2_), channel_id=1, source_target_pairs={{0,4},{4,0},{1,5},{5,1},{2,6},{6,2},{3,7},{7,3},{8,12},{12,8},{9,1... | collective-permute-start | bytes 1179656 | tf_op jit(solution)/shard_map/ppermute | solution.py:187
  245.3 40.0 %collective-permute-start.27 = (bf16[384,512]{1,0:T(8,128)(2,1)S(1)}, bf16[384,512]{1,0:T(8,128)(2,1)S(1)}, u32[]{:S(2)}, u32[]{:S(2)}) collective-permute-start(bf16[384,512]{1,0:T(8,128)(2,1)S(1)} %get-tuple-element.65.refs_3_), channel_id=1, source_target_pairs={{0,4},{4,0},{1,5},{5,1},{2,6},{6,2},{3,7},{7,3},{8,12},{12,8},{9,1... | collective-permute-start | bytes 1179656 | tf_op jit(solution)/shard_map/ppermute | solution.py:187
  289.7 72.6 %collective-permute-start.32 = (bf16[256,3072]{1,0:T(8,128)(2,1)}, bf16[256,3072]{1,0:T(8,128)(2,1)}, u32[]{:S(2)}, u32[]{:S(2)}) collective-permute-start(bf16[256,3072]{1,0:T(8,128)(2,1)} %shard_map.101), channel_id=1, source_target_pairs={{0,8},{8,0},{16,24},{24,16},{1,9},{9,1},{17,25},{25,17},{2,10},{10... | collective-permute-start | bytes 4718600 | tf_op jit(solution)/shard_map/ppermute | solution.py:232
  331.1 63.4 %collective-permute-start.31 = (bf16[256,3072]{1,0:T(8,128)(2,1)S(1)}, bf16[256,3072]{1,0:T(8,128)(2,1)S(1)}, u32[]{:S(2)}, u32[]{:S(2)}) collective-permute-start(bf16[256,3072]{1,0:T(8,128)(2,1)S(1)} %shard_map.100), channel_id=1, source_target_pairs={{0,8},{8,0},{16,24},{24,16},{1,9},{9,1},{17,25},{25,17},{2,10},{10... | collective-permute-start | bytes 4718600 | tf_op jit(solution)/shard_map/ppermute | solution.py:232
  346.3 65.1 %collective-permute-start.30 = (bf16[128,3072]{1,0:T(8,128)(2,1)S(1)}, bf16[128,3072]{1,0:T(8,128)(2,1)S(1)}, u32[]{:S(2)}, u32[]{:S(2)}) collective-permute-start(bf16[128,3072]{1,0:T(8,128)(2,1)S(1)} %shard_map.99), channel_id=1, source_target_pairs={{0,8},{8,0},{16,24},{24,16},{1,9},{9,1},{17,25},{25,17},{2,10},{10... | collective-permute-start | bytes 2359304 | tf_op jit(solution)/shard_map/ppermute | solution.py:232
  350.2 77.2 %collective-permute-start.29 = (bf16[128,3072]{1,0:T(8,128)(2,1)S(1)}, bf16[128,3072]{1,0:T(8,128)(2,1)S(1)}, u32[]{:S(2)}, u32[]{:S(2)}) collective-permute-start(bf16[128,3072]{1,0:T(8,128)(2,1)S(1)} %shard_map.98), channel_id=1, source_target_pairs={{0,8},{8,0},{16,24},{24,16},{1,9},{9,1},{17,25},{25,17},{2,10},{10... | collective-permute-start | bytes 2359304 | tf_op jit(solution)/shard_map/ppermute | solution.py:232
  (3 other events, 3.2 us)

commit v3 on v2

v3 whole, which is shorter than its diff:
```python
import functools

import jax
import jax.numpy as jnp
from jax import lax
from jax.experimental import pallas as pl
from jax.experimental.pallas import tpu as pltpu
from jax.sharding import PartitionSpec as P

BLK = 256
NT = (((1,), (1,)), ((), ()))
VMEM_LIMIT = 48 * 1024 * 1024
STEP = 128
MAP_ROWS = 16


def block_inverse(mapping):
    block_total = mapping.shape[0]
    target = jnp.arange(block_total, dtype=jnp.int32)
    matches = (mapping[:, None] == target[None, :]).astype(jnp.int32)
    return jnp.sum(matches * target[:, None], axis=0)


SMALL = pl.CostEstimate(flops=1, bytes_accessed=1, transcendentals=0)


def update_kernel(unit, col_unit, at_ref, front_ref, factor_ref, col_ref, out_ref):
    first = col_unit(pl.program_id(1)) * unit
    col = col_ref[pl.ds(pl.multiple_of(first, unit), unit), :]
    product = lax.dot_general(factor_ref[...], col, NT, preferred_element_type=jnp.float32)
    out_ref[...] = (front_ref[...].astype(jnp.float32) - product).astype(jnp.bfloat16)


def updated_rows(front, at, front_row, front_col, factor, factor_row, col_side, col_unit, grid, height, unit):
    pivots = factor.shape[1]
    return pl.pallas_call(
        functools.partial(update_kernel, unit, col_unit),
        grid_spec=pltpu.PrefetchScalarGridSpec(
            num_scalar_prefetch=1,
            grid=grid,
            in_specs=[
                pl.BlockSpec((height, unit), lambda i, j, at: (front_row(i, at), front_col(j, at))),
                pl.BlockSpec((height, pivots), lambda i, j, at: (factor_row(i, at), 0)),
                pl.BlockSpec(col_side.shape, lambda i, j, at: (0, 0)),
            ],
            out_specs=pl.BlockSpec((height, unit), lambda i, j, at: (i, j)),
        ),
        out_shape=jax.ShapeDtypeStruct((grid[0] * height, grid[1] * unit), jnp.bfloat16),
        compiler_params=pltpu.CompilerParams(vmem_limit_bytes=VMEM_LIMIT),
        cost_estimate=SMALL,
    )(at, front, factor, col_side)


def pick_kernel(at_ref, front_ref, out_ref):
    out_ref[...] = front_ref[...]


def picked_rows(front, at, first_row, rows, unit, stride, offset):
    units = front.shape[1] // unit // stride
    return pl.pallas_call(
        pick_kernel,
        grid_spec=pltpu.PrefetchScalarGridSpec(
            num_scalar_prefetch=1,
            grid=(units,),
            in_specs=[pl.BlockSpec(
                (pl.Element(rows), pl.Element(unit)),
                lambda j, at: (first_row(0, at), (j * stride + offset) * unit),
            )],
            out_specs=pl.BlockSpec((rows, unit), lambda j, at: (0, j)),
        ),
        out_shape=jax.ShapeDtypeStruct((rows, units * unit), jnp.bfloat16),
        compiler_params=pltpu.CompilerParams(vmem_limit_bytes=VMEM_LIMIT),
        cost_estimate=SMALL,
    )(at, front)


def assemble_kernel(plan, sources, at_ref, *refs):
    outs, sem = refs[sources:-1], refs[-1]
    for step, (out, first, rows, choice, options) in enumerate(plan):
        chosen = choice(at_ref)
        for value, (source, start) in options.items():
            @pl.when(chosen == value)
            def _():
                pltpu.make_async_copy(
                    refs[source].at[pl.ds(start, rows)], outs[out].at[pl.ds(first, rows)], sem.at[step]
                ).start()
    for step, (out, first, rows, _, options) in enumerate(plan):
        source, start = next(iter(options.values()))
        pltpu.make_async_copy(
            refs[source].at[pl.ds(start, rows)], outs[out].at[pl.ds(first, rows)], sem.at[step]
        ).wait()


def assembled(at, sources, plan, out_rows):
    width = sources[0].shape[1]
    return pl.pallas_call(
        functools.partial(assemble_kernel, plan, len(sources)),
        grid_spec=pltpu.PrefetchScalarGridSpec(
            num_scalar_prefetch=1,
            grid=(1,),
            in_specs=[pl.BlockSpec(memory_space=pl.ANY)] * len(sources),
            out_specs=[pl.BlockSpec((rows, width), lambda i, at: (0, 0)) for rows in out_rows],
            scratch_shapes=[pltpu.SemaphoreType.DMA((len(plan),))],
        ),
        out_shape=[jax.ShapeDtypeStruct((rows, width), jnp.bfloat16) for rows in out_rows],
        compiler_params=pltpu.CompilerParams(vmem_limit_bytes=VMEM_LIMIT),
        cost_estimate=SMALL,
    )(at, *sources)


def base_kernel(blocks, target_ref, own_ref, place_ref, front_ref, factor_ref, col_ref, given_ref, out_ref):
    factor = factor_ref[...]
    for block in range(blocks):
        here = pl.ds(block * BLK, BLK)
        own = pl.ds(pl.multiple_of(place_ref[block] * BLK, BLK), BLK)
        product = lax.dot_general(factor, col_ref[own, :], NT, preferred_element_type=jnp.float32)
        kept = (front_ref[:, own].astype(jnp.float32) - product).astype(jnp.bfloat16)
        out_ref[:, here] = given_ref[:, here].astype(jnp.float32) + kept.astype(jnp.float32)


def kept_rows(targets, owns, places, front, factor, col_side, given):
    count = targets.shape[0]
    cols = front.shape[1]
    pivots = factor.shape[1]
    return pl.pallas_call(
        functools.partial(base_kernel, cols // BLK),
        grid_spec=pltpu.PrefetchScalarGridSpec(
            num_scalar_prefetch=3,
            grid=(count,),
            in_specs=[
                pl.BlockSpec((BLK, cols), lambda i, targets, owns, places: (owns[i], 0)),
                pl.BlockSpec((BLK, pivots), lambda i, targets, owns, places: (owns[i], 0)),
                pl.BlockSpec(col_side.shape, lambda i, targets, owns, places: (0, 0)),
                pl.BlockSpec((BLK, cols), lambda i, targets, owns, places: (targets[i], 0)),
            ],
            out_specs=pl.BlockSpec((BLK, cols), lambda i, targets, owns, places: (targets[i], 0)),
        ),
        out_shape=jax.ShapeDtypeStruct(given.shape, jnp.float32),
        compiler_params=pltpu.CompilerParams(vmem_limit_bytes=VMEM_LIMIT),
        cost_estimate=SMALL,
    )(targets, owns, places, front, factor, col_side, given)


def add_kernel(blocks, pieces, target_ref, place_ref, *refs):
    base_ref, out_ref = refs[-2], refs[-1]
    for block in range(blocks):
        here = pl.ds(block * BLK, BLK)
        arrived = None
        for k in range(pieces):
            part = refs[k][:, pl.ds(pl.multiple_of(place_ref[1 + k, block] * BLK, BLK), BLK)]
            arrived = part if arrived is None else jnp.where(place_ref[0, block] == k, part, arrived)
        out_ref[:, here] = base_ref[:, here] + arrived.astype(jnp.float32)


def add_rows(base, targets, places, pieces, count, step=STEP, first=0):
    parts = BLK // step
    skip = first // step
    cols = base.shape[1]
    row = pl.BlockSpec(
        (step, cols),
        lambda i, targets, places: (targets[(i + skip) // parts] * parts + (i + skip) % parts, 0),
    )
    in_specs = [
        pl.BlockSpec((step, piece.shape[1]), functools.partial(lambda begin, i, *_: (i + begin, 0), begin // step))
        for piece, begin in pieces
    ]
    return pl.pallas_call(
        functools.partial(add_kernel, cols // BLK, len(pieces)),
        grid_spec=pltpu.PrefetchScalarGridSpec(
            num_scalar_prefetch=2, grid=(count // step,), in_specs=in_specs + [row], out_specs=row
        ),
        out_shape=jax.ShapeDtypeStruct(base.shape, jnp.float32),
        input_output_aliases={2 + len(pieces): 0},
        compiler_params=pltpu.CompilerParams(vmem_limit_bytes=VMEM_LIMIT),
        cost_estimate=SMALL,
    )(targets, places, *(piece for piece, _ in pieces), base)


def take_block(table, first, count):
    return lax.dynamic_slice_in_dim(table, first, count, 0)


def hop(up_block, down_block, up, down):
    return lax.ppermute(up_block, "col", up), lax.ppermute(down_block, "col", down)


UP = [(0, 1), (1, 2), (2, 3)]
DOWN = [(1, 0), (2, 1), (3, 2)]
FAR = [(2, 3), (1, 0)]


def other_core(block):
    return lax.ppermute(block, "row", [(0, 1), (1, 0)])


def segment_at(segment, at_ref):
    away = segment - at_ref[0]
    far = jnp.where(away == 2, 4, 5)
    near = jnp.where(away == -1, 1, jnp.where(away == 1, 2, jnp.where(away == -2, 3, far)))
    return jnp.where(away == 0, 0, near)


def settled(array, table, turns):
    array, table = lax.optimization_barrier((array, table))
    for _ in range(turns):
        table = other_core(table)
    return array, table


def near_source(at_ref):
    own = segment_at(col_segment(False)(at_ref), at_ref)
    other = jnp.where((at_ref[0] == 1) | (at_ref[0] == 2), 3, 4)
    return jnp.where(not_owner(at_ref) == 0, own, other)


def options(sources, rows=0):
    return {k: (k, rows) for k in range(sources)}


def col_segment(far):
    def segment(at_ref):
        low = at_ref[0] % 2 * 2
        near = at_ref[0] // 2
        return low + (1 - near if far else near)
    return segment


def inner_segment(at_ref):
    return jnp.where(at_ref[2] == 1, 1, 2)


def at_segment(segment):
    return lambda at_ref: segment_at(segment(at_ref), at_ref)


def not_owner(at_ref):
    return jnp.where(at_ref[1] == at_ref[0] // 2, 0, 1)


def factor_of(panel, inverse, fill, first_row):
    local_rows = panel.shape[0]
    positions = (first_row + jnp.arange(local_rows, dtype=jnp.int32)) // BLK
    blocks = jnp.arange(fill.shape[0], dtype=jnp.int32)
    row_fill = jnp.sum(
        (positions[:, None] == blocks[None, :]).astype(jnp.int32) * fill[None, :], axis=1
    )
    masked = panel * row_fill[:, None].astype(jnp.bfloat16)
    return jnp.dot(masked, jnp.triu(inverse), preferred_element_type=jnp.float32).astype(jnp.bfloat16)


def from_sibling(block):
    route = []
    for low in range(0, lax.axis_size("front"), 2):
        route += [(low, low + 1), (low + 1, low)]
    return lax.ppermute(block, "front", route)


def shards(front, panel, inverse, fill, block_map, parent_front):
    front, panel, given = front[0], panel[0], parent_front[0]
    col_count = lax.axis_size("col")
    row_count = lax.axis_size("row")
    core = lax.axis_index("row")
    place = lax.axis_index("col")
    parity = lax.axis_index("front") % 2
    local_rows = panel.shape[0]
    tile_rows, tile_cols = front.shape
    half_blocks = tile_rows // 2 // BLK
    col_blocks = tile_cols // BLK
    seg = local_rows // BLK
    row_base = core * (tile_rows // BLK)
    source = block_inverse(block_map[0])
    col_source = take_block(source, place * col_blocks, col_blocks) - place * col_blocks
    first_row = (core * col_count + place) * local_rows

    closed = half_blocks % col_blocks == 0
    line = (
        row_count == 2 and col_count == 4 and closed and tile_rows == 2 * tile_cols
        and local_rows == 6 * BLK and 2 * local_rows == tile_cols
    )
    if not line:
        sibling_map = from_sibling(block_map[0])
        factor = factor_of(panel, inverse[0], fill[0], first_row)
        all_rows = lax.all_gather(factor, ("row", "col"), axis=0, tiled=True)
        row_side = take_block(all_rows, core * tile_rows, tile_rows)
        col_side = take_block(all_rows, place * tile_cols, tile_cols)
        sent = take_block(source, row_base + (1 - parity) * half_blocks, half_blocks) - row_base
        owns = take_block(source, row_base + parity * half_blocks, half_blocks) - row_base
        targets = jnp.arange(half_blocks, dtype=jnp.int32)
        grid = (half_blocks, 1)
        arrived = from_sibling(updated_rows(
            front, sent, lambda i, at: at[i], lambda j, at: j, row_side, lambda i, at: at[i], col_side,
            lambda j: j, grid, BLK, tile_cols,
        ))
        sibling_cols = take_block(block_inverse(sibling_map), place * col_blocks, col_blocks)
        sibling_cols = sibling_cols - place * col_blocks
        base = kept_rows(targets, owns, col_source, front, row_side, col_side, given)
        places = jnp.stack([jnp.zeros_like(sibling_cols), sibling_cols])
        out = add_rows(base, targets, places, [(arrived, 0)], half_blocks * BLK)
        return factor[None], out[None]

    half = local_rows // 2
    cut = local_rows * 3 // 8
    thin = local_rows // 8
    wide = local_rows // 3
    at = jnp.stack([place, core, parity]).astype(jnp.int32)
    after = lax.optimization_barrier

    def sent_row(inner, height):
        def row(at):
            sent = 1 - at[2]
            return sent * (half_blocks * BLK // height) + (at[2] if inner else sent) * (local_rows // height)
        return row

    def raw_rows(inner, first, rows):
        start = sent_row(inner, thin)
        skip = (local_rows - cut + first) // thin
        return picked_rows(front, at, lambda i, at: (start(at) + skip) * thin, rows, wide, 3, 2)

    raw = [raw_rows(*piece) for piece in ((True, 0, cut - thin), (False, 0, cut), (True, cut - thin, thin))]
    panel, raw[0] = after((panel, raw[0]))
    factor_a = factor_of(panel[:half], inverse[0], fill[0], first_row)
    raw[0] = from_sibling(raw[0])
    below_a, above_a = hop(factor_a, factor_a, UP, DOWN)
    factor_b = factor_of(panel[half:], inverse[0], fill[0], first_row + half)
    raw[1] = from_sibling(raw[1])
    near_part = assembled(
        at, [factor_a, below_a, above_a], [(0, 0, half, at_segment(col_segment(False)), options(3))], [half]
    )[0]
    near_other = other_core(near_part)
    raw[0], own_map = settled(raw[0], block_map[0], 1)
    below_a, above_a, own_map = after((below_a, above_a, own_map))
    below2_a, above2_a = hop(below_a, above_a, UP[1:], DOWN[:2])
    width = raw[2].shape[1]
    map_rows = jnp.pad(block_map[0].astype(jnp.bfloat16), (0, width - block_map.shape[1]))
    map_rows = jnp.broadcast_to(map_rows[None], (MAP_ROWS, width))
    part = factor_b[half - cut:].reshape(-1, width)
    raw[2] = jnp.concatenate([raw[2], part, map_rows], axis=0)
    raw[2] = from_sibling(raw[2])
    raw[1], own_map = settled(raw[1], own_map, 1)
    at_a, own_map = after((at, own_map))
    sources_a = [factor_a, below_a, above_a, below2_a, above2_a]
    near_a = assembled(
        at, [near_part, near_other], [(0, 0, half, not_owner, {0: (0, 0), 1: (1, 0)})], [half]
    )[0]
    inner_a = assembled(at_a, sources_a, [(0, 0, half, at_segment(inner_segment), options(5))], [half])[0]

    arrived = []

    def contribution(at, inner, first, rows, factor, factor_first, col_side, unit, units, front_col, col_unit):
        height = thin if rows % thin == 0 else min(rows, BLK)
        start = sent_row(inner, height)
        piece = updated_rows(
            front, at, lambda i, at: start(at) + first // height + i, front_col, factor,
            lambda i, at: factor_first(at, height) + i, col_side, col_unit, (rows // height, units), height, unit,
        )
        return piece

    def quarter(at, col_side, far, second):
        def front_col(j, at):
            near = at[0] // 2
            return (1 - near if far else near) * 2 + second
        return contribution(
            at, True, 0, half, inner_a, lambda at, height: 0, col_side, half, 1, front_col, lambda j: 0
        )

    piece = quarter(at_a, near_a, False, 0)
    at_f, piece = after((at_a, piece))
    arrived.append(from_sibling(piece))
    far_part = assembled(
        at_f, sources_a, [(0, 0, half, at_segment(col_segment(True)), options(5))], [half]
    )[0]
    far_a = assembled(
        at, [far_part, other_core(far_part)], [(0, 0, half, not_owner, {0: (0, 0), 1: (1, 0)})], [half]
    )[0]

    raw[2], own_map = settled(raw[2], own_map, 1)
    later, far_a, own_map, own_other = after((factor_b, far_a, own_map, other_core(factor_b)))
    arrived.append(from_sibling(quarter(at, far_a, True, 0)))
    below_b, above_b = hop(later, later, UP, DOWN)
    cross = lax.ppermute(later, ("row", "col"), [(2, col_count + 1), (col_count + 1, 2)])
    arrived[0], own_map = settled(arrived[0], own_map, 2)
    below_b, above_b, cross, own_map = after((below_b, above_b, cross, own_map))
    near_b = assembled(at, [factor_b, below_b, above_b, cross, own_other], [
        (0, 0, half, near_source, options(5))
    ], [half])[0]
    below2_b, above2_b = hop(below_b, above_b, UP[1:], DOWN[:2])
    arrived.append(from_sibling(quarter(at, near_b, False, 1)))
    sources_b = [factor_b, below_b, above_b, below2_b, above2_b]
    second = options(5)
    inner_b, far_part = assembled(at, sources_b, [
        (0, 0, half, at_segment(inner_segment), second),
        (1, 0, half, at_segment(col_segment(True)), second),
    ], [half] * 2)
    arrived[1], own_map = settled(arrived[1], own_map, 3)
    far_part, own_map = after((far_part, own_map))
    far_b = assembled(
        at, [far_part, other_core(far_part)], [(0, 0, half, not_owner, {0: (0, 0), 1: (1, 0)})], [half]
    )[0]
    arrived.append(from_sibling(quarter(at, far_b, True, 1)))
    col_side = assembled(at, [near_a, far_a, near_b, far_b], [
        (0, (2 * segment + k) * half, half, functools.partial(
            lambda segment, at_ref: jnp.where(at_ref[0] // 2 == segment, 0, 1), segment
        ), {0: (2 * k, 0), 1: (2 * k + 1, 0)})
        for segment in range(2) for k in range(2)
    ], [tile_cols])[0]

    def whole_row(at, inner, first, rows, factor, factor_first):
        arrived.append(from_sibling(contribution(
            at, inner, first, rows, factor, factor_first, col_side, half, 4, lambda j, at: j, lambda j: j
        )))

    def cut_rows(at, inner, factor, factor_first):
        arrived.append(from_sibling(contribution(
            at, inner, local_rows - cut, cut, factor, factor_first, col_side, wide, 4,
            lambda j, at: j + j // 2, lambda j: j + j // 2,
        )))

    arrived[2], own_map = settled(arrived[2], own_map, 1)
    at_i, own_map = after((at, own_map))
    cut_rows(at_i, True, inner_b, lambda at, height: 1)
    arrived[3], turned = settled(arrived[3], inner_b[:576], 2)
    whole_row(at, True, half, thin, turned, lambda at, height: 0)

    last_hop = assembled(at, [below2_a, above2_a, below2_b, above2_b], [
        (0, k * half, half, lambda at_ref: jnp.where(at_ref[0] == 2, 0, 1), {0: (2 * k, 0), 1: (2 * k + 1, 0)})
        for k in range(2)
    ], [local_rows])[0]
    last_hop, arrived[1] = after((last_hop, arrived[1]))
    far = lax.ppermute(last_hop, "col", FAR)
    row_side = assembled(at, [*sources_a, *sources_b, far], [
        (0, (2 * segment + k) * half, half, functools.partial(segment_at, segment), {
            **{j: (j + 5 * k, 0) for j in range(5)}, 5: (10, k * half)
        })
        for segment in range(4) for k in range(2)
    ], [tile_rows])[0]

    def outer_row(first):
        return lambda at, height: sent_row(False, height)(at) + first // height

    at_i, arrived[4] = after((at, arrived[4]))
    whole_row(at_i, False, 0, BLK, row_side, outer_row(0))

    sibling_map = raw[2][-1, :block_map.shape[1]].astype(jnp.int32)
    part = raw[2][thin:-MAP_ROWS].reshape(cut, -1)
    raw[2] = raw[2][:thin]
    part_below, part_above = hop(part, part, UP, DOWN)
    part_below, part_above, arrived[3] = after((part_below, part_above, arrived[3]))
    part_below2, part_above2 = hop(part_below, part_above, UP[1:], DOWN[:2])
    part_far = lax.ppermute(jnp.where(place == 2, part_below2, part_above2), "col", FAR)
    parts_near = [part, part_below, part_above, part_below2, part_above2]
    part_cols = assembled(at, parts_near, [
        (k, 0, wide, functools.partial(lambda k, at_ref: segment_at(at_ref[0] % 2 * 2 + k, at_ref), k),
         options(5, cut - wide))
        for k in range(2)
    ], [wide] * 2)
    others = [other_core(piece) for piece in part_cols]
    sibling_col = assembled(at, [*part_cols, *others], [
        (0, k * wide, wide, not_owner, {0: (k, 0), 1: (2 + k, 0)}) for k in range(2)
    ], [2 * wide])[0]
    part_rows = assembled(at, [*parts_near, part_far], [
        (0, k * cut, cut, functools.partial(
            lambda k, at_ref: segment_at(jnp.where(at_ref[2] == 0, 1 - k, 2 + k), at_ref), k
        ), options(6))
        for k in range(2)
    ], [2 * cut])[0]
    finished = updated_rows(
        jnp.concatenate([raw[0], raw[2], raw[1]], axis=0), at, lambda i, at: i, lambda j, at: j, part_rows, lambda i, at: i, sibling_col,
        lambda j: j, (2 * cut // thin, 2), thin, wide,
    )

    kept_base = row_base + parity * half_blocks
    source = block_inverse(own_map)
    owns = take_block(source, kept_base, half_blocks) - row_base
    col_source = take_block(source, place * col_blocks, col_blocks) - place * col_blocks
    base = kept_rows(
        jnp.arange(half_blocks, dtype=jnp.int32), owns, col_source, front, row_side, col_side, given
    )
    sibling_cols = take_block(block_inverse(sibling_map), place * col_blocks, col_blocks)
    sibling_cols = sibling_cols - place * col_blocks
    landed = take_block(sibling_map, kept_base, half_blocks) - kept_base
    segment, within = sibling_cols // seg, sibling_cols % seg
    cut_blocks = wide // BLK
    cut_first = seg - cut_blocks
    is_far = jnp.where(segment == place // 2, 0, 1)
    quarter_at = within % (seg // 2)
    places_q = jnp.stack([within // (seg // 2) * 2 + is_far] + [quarter_at] * 4)
    places_w = jnp.stack([jnp.zeros_like(sibling_cols), sibling_cols])
    places_c = jnp.stack([
        jnp.where(within < cut_first, 1, 0),
        segment * cut_blocks + jnp.maximum(within - cut_first, 0),
        segment * cut_first + jnp.minimum(within, cut_first - 1),
    ])
    kept_inner = (1 - parity) * seg
    kept_outer = seg - kept_inner

    small = STEP // 2

    def add_whole(out, start, index, rows=BLK, step=STEP, first=0):
        targets = take_block(landed, start, 1)
        return add_rows(out, targets, places_w, [(arrived[index], 0)], rows, step, first)

    def add_cut(out, start, index, first):
        targets = take_block(landed, start + seg // 2, seg // 2)
        pieces = [(finished, first), (arrived[index], 0)]
        return add_rows(out, targets, places_c, pieces, cut, small, thin)

    at_i, arrived[5], out = after((at, arrived[5], base))
    whole_row(at_i, False, BLK, BLK, row_side, outer_row(BLK))
    out = add_rows(
        out, take_block(landed, kept_inner, seg // 2), places_q, [(arrived[k], 0) for k in range(4)], half
    )
    at_i, arrived[6], out = after((at, arrived[6], out))
    cut_rows(at_i, False, row_side, outer_row(local_rows - cut))
    at_i, arrived[7], out = after((at, arrived[7], out))
    whole_row(at_i, False, 2 * BLK, BLK, row_side, outer_row(2 * BLK))
    out = add_cut(out, kept_inner, 4, 0)
    out = add_whole(out, kept_inner + seg // 2, 5, thin, small)
    out = add_whole(out, kept_outer, 6)
    at_i, arrived[8], out = after((at, arrived[8], out))
    whole_row(at_i, False, 3 * BLK, STEP, row_side, outer_row(3 * BLK))
    out = add_whole(out, kept_outer + 1, 7)
    out = add_cut(out, kept_outer, 8, cut)
    at_i, arrived[9], out = after((at, arrived[9], out))
    whole_row(at_i, False, 3 * BLK + STEP, small, row_side, outer_row(3 * BLK + STEP))
    out = add_whole(out, kept_outer + 2, 9)
    out = add_whole(out, kept_outer + 3, 10, STEP)
    out = add_whole(out, kept_outer + 3, 11, small, small // 2, STEP)
    factor = jnp.concatenate([factor_a, factor_b], axis=0)
    return factor[None], out[None]


def solution(mesh):
    placed = (
        P("front", "row", "col"),
        P("front", ("row", "col"), None),
        P("front", None, None),
        P("front", None),
        P("front", None),
        P("front", "row", "col"),
    )
    return jax.shard_map(
        shards,
        mesh=mesh,
        in_specs=placed,
        out_specs=(P("front", ("row", "col"), None), P("front", "row", "col")),
        check_vma=False,
    )
```

time: 433 us -> 430 us (level)
  waiting for transfers between devices: 176 us -> 153 us
  Pallas kernels: 180 us -> 195 us
  starting transfers between devices: 45.6 us -> 51.3 us
    ppermute x14 -> x15, waiting for transfers between devices: 154 us -> 96.1 us  [from_sibling(): return lax.ppermute(block, 'front', route)]
    ppermute x1 -> x2, waiting for transfers between devices: 0.01 us -> 19.4 us  [the longest x1 19.4 us: shards(): far = lax.ppermute(last_hop, 'col', FAR)]
    pallas_call x10 -> x13, Pallas kernels: 59.1 us -> 73.6 us  [updated_rows(): pl.pallas_call(functools.partial(update_kernel, unit, col_unit), grid_spe...]
    pallas_call x4 -> x3, Pallas kernels: 17.4 us -> 6.08 us  [picked_rows(): pl.pallas_call(pick_kernel, grid_spec=pltpu.PrefetchScalarGridSpec(num_sc...]
    ppermute x9 -> x17, waiting for transfers between devices: 5.77 us -> 12.9 us  [other_core(): return lax.ppermute(block, 'row', [(0, 1), (1, 0)])]
    pallas_call x9, Pallas kernels: 51.4 us -> 58.3 us  [add_rows(): pl.pallas_call(functools.partial(add_kernel, cols // BLK, len(pieces)), g...]
    pallas_call x6 -> x14, Pallas kernels: 17.4 us -> 22.9 us  [assembled(): pl.pallas_call(functools.partial(assemble_kernel, plan, len(sources)), gr...]
    ppermute x4 -> x6, waiting for transfers between devices: 14.7 us -> 18.9 us  [hop(): lax.ppermute(down_block, 'col', down)]
  transfers between devices with their start and end apart: 33 -> 47, of which waited for: 20 -> 29; matrix products, arithmetic and copies ran while one was open for 5% -> 5% of each run, Pallas kernels for 40% -> 45%
where the time goes in v3:
time: 430 us; the launch traced here: 427 us
  Pallas kernels  195 us (45%)
  waiting for transfers between devices  153 us (36%)
  starting transfers between devices  51.3 us (12%)
  local copies, waits for them, and re-layouts  12.8 us (3%)
  other arithmetic  11.1 us (3%)
    ppermute x15, waiting for transfers between devices, from_sibling(): return lax.ppermute(block, 'front', route)  96.1 us
    pallas_call x13, Pallas kernels, updated_rows(): pl.pallas_call(functools.partial(update_kernel, unit, col_unit), grid_spe...  73.6 us
    pallas_call x9, Pallas kernels, add_rows(): pl.pallas_call(functools.partial(add_kernel, cols // BLK, len(pieces)), g...  58.3 us
    pallas_call x1, Pallas kernels, kept_rows(): pl.pallas_call(functools.partial(base_kernel, cols // BLK), grid_spec=plt...  34.3 us
    pallas_call x14, Pallas kernels, assembled(): pl.pallas_call(functools.partial(assemble_kernel, plan, len(sources)), gr...  22.9 us
    ppermute x15, starting transfers between devices, from_sibling(): return lax.ppermute(block, 'front', route)  22.4 us
    ppermute x1, waiting for transfers between devices, shards(): far = lax.ppermute(last_hop, 'col', FAR)  19.4 us
    ppermute x6, waiting for transfers between devices, hop(): lax.ppermute(down_block, 'col', down)  18.9 us
  transfers between devices with their start and end apart: 47, of which 29 were waited for; matrix products, arithmetic and copies ran while one was open for 5% of the time, Pallas kernels for 45%

profile of v3, /device:TPU:0, one launch (start us, length us, event | category | flops | bytes accessed | tf_op | source)
XLA Modules:
  0.0 427.3 jit_solution(11589607953186401217)
XLA Ops:
  2.5 3.0 collective-permute-start.4
  7.5 4.4 %collective-permute-start.2 = (bf16[768,512]{1,0:T(8,128)(2,1)S(1)}, bf16[768,512]{1,0:T(8,128)(2,1)}, u32[]{:S(2)}, u32[]{:S(2)}) collective-permute-start(bf16[768,512]{1,0:T(8,128)(2,1)S(1)} %convolution_convert_fusion.1.refs_0_), channel_id=1, source_target_pairs={{0,1},{1,2},{2,3},{4,5},{5,6},{6,7},{8,9},{9,10},{10,11},{12,13},{... | collective-permute-start | bytes 2359304 | tf_op jit(solution)/shard_map/ppermute | solution.py:184
  13.2 2.7 shard_map.79
  18.0 5.8 %collective-permute-done.4 = bf16[384,1024]{1,0:T(8,128)(2,1)S(1)} collective-permute-done((bf16[384,1024]{1,0:T(8,128)(2,1)S(1)}, bf16[384,1024]{1,0:T(8,128)(2,1)S(1)}, u32[]{:S(2)}, u32[]{:S(2)}) %collective-permute-start.4) | collective-permute-done | bytes 786464 | tf_op jit(solution)/shard_map/ppermute | solution.py:255
  23.9 3.6 collective-permute-done.2.refs_1_
  27.5 5.1 %collective-permute-done.3.refs_2_ = bf16[768,512]{1,0:T(8,128)(2,1)} collective-permute-done((bf16[768,512]{1,0:T(8,128)(2,1)S(1)}, bf16[768,512]{1,0:T(8,128)(2,1)}, u32[]{:S(2)}, u32[]{:S(2)}) %collective-permute-start.3) | collective-permute-done | bytes 786464 | tf_op jit(solution)/shard_map/ppermute | solution.py:184
  41.7 7.6 %collective-permute-done.1 = bf16[576,1024]{1,0:T(8,128)(2,1)} collective-permute-done((bf16[576,1024]{1,0:T(8,128)(2,1)}, bf16[576,1024]{1,0:T(8,128)(2,1)}, u32[]{:S(2)}, u32[]{:S(2)}) %collective-permute-start.1) | collective-permute-done | bytes 1179680 | tf_op jit(solution)/shard_map/ppermute | solution.py:255
  52.1 7.4 %collective-permute-done.8.refs_4_.refs_1_ = bf16[768,512]{1,0:T(8,128)(2,1)S(1)} collective-permute-done((bf16[768,512]{1,0:T(8,128)(2,1)}, bf16[768,512]{1,0:T(8,128)(2,1)S(1)}, u32[]{:S(2)}, u32[]{:S(2)}) %collective-permute-start.8) | collective-permute-done | bytes 786464 | tf_op jit(solution)/shard_map/ppermute | solution.py:184
  60.1 3.8 shard_map.83
  67.9 3.0 collective-permute-done
  72.0 3.9 collective-permute-start.13
  77.9 3.8 shard_map.87
  83.5 12.7 %collective-permute-done.16.refs_0_ = bf16[768,768]{1,0:T(8,128)(2,1)S(1)} collective-permute-done((bf16[768,768]{1,0:T(8,128)(2,1)S(1)}, bf16[768,768]{1,0:T(8,128)(2,1)S(1)}, u32[]{:S(2)}, u32[]{:S(2)}) %collective-permute-start.16) | collective-permute-done | bytes 1179680 | tf_op jit(solution)/shard_map/ppermute | solution.py:255
  101.2 3.8 shard_map.93
  107.1 14.4 %collective-permute-done.21.refs_1_ = bf16[768,768]{1,0:T(8,128)(2,1)S(1)} collective-permute-done((bf16[768,768]{1,0:T(8,128)(2,1)S(1)}, bf16[768,768]{1,0:T(8,128)(2,1)S(1)}, u32[]{:S(2)}, u32[]{:S(2)}) %collective-permute-start.21) | collective-permute-done | bytes 1179680 | tf_op jit(solution)/shard_map/ppermute | solution.py:255
  123.9 4.3 %collective-permute-done.20.refs_4_.refs_3_.refs_9_ = bf16[768,512]{1,0:T(8,128)(2,1)S(1)} collective-permute-done((bf16[768,512]{1,0:T(8,128)(2,1)S(1)}, bf16[768,512]{1,0:T(8,128)(2,1)S(1)}, u32[]{:S(2)}, u32[]{:S(2)}) %collective-permute-start.20) | collective-permute-done | bytes 786464 | tf_op jit(solution)/shard_map/ppermute | solution.py:184
  132.0 4.8 %shard_map.89 = bf16[768,768]{1,0:T(8,128)(2,1)} custom-call(s32[3]{0:T(128)S(1)} %pad_add_fusion.1.at_ref, bf16[6144,3072]{1,0:T(8,128)(2,1)} %bitcast.46, bf16[768,512]{1,0:T(8,128)(2,1)S(1)} %shard_map.80.factor_ref, bf16[768,512]{1,0:T(8,128)(2,1)S(1)} %shard_map.88.col_ref.refs_3_), custom_call_target="tpu_custom_call" | custom-call | flops 1 | bytes 1 | tf_op jit(solution)/shard_map/pallas_call | solution.py:36
  138.4 8.3 %collective-permute-done.30.refs_2_ = bf16[768,768]{1,0:T(8,128)(2,1)S(1)} collective-permute-done((bf16[768,768]{1,0:T(8,128)(2,1)S(1)}, bf16[768,768]{1,0:T(8,128)(2,1)S(1)}, u32[]{:S(2)}, u32[]{:S(2)}) %collective-permute-start.30) | collective-permute-done | bytes 1179680 | tf_op jit(solution)/shard_map/ppermute | solution.py:255
  147.9 2.5 shard_map.91.col_ref
  150.4 11.0 %shard_map.98 = bf16[576,2048]{1,0:T(8,128)(2,1)} custom-call(s32[3]{0:T(128)S(1)} %pad_add_fusion.1.at_ref, bf16[6144,3072]{1,0:T(8,128)(2,1)} %bitcast.47, bf16[768,512]{1,0:T(8,128)(2,1)S(1)} %get-tuple-element.86.factor_ref, bf16[3072,512]{1,0:T(8,128)(2,1)} %shard_map.91.col_ref), custom_call_target="tpu_custom_call" | custom-call | flops 1 | bytes 1 | tf_op jit(solution)/shard_map/pallas_call | solution.py:36
  165.6 6.5 %collective-permute-done.26.refs_3_ = bf16[768,768]{1,0:T(8,128)(2,1)} collective-permute-done((bf16[768,768]{1,0:T(8,128)(2,1)}, bf16[768,768]{1,0:T(8,128)(2,1)}, u32[]{:S(2)}, u32[]{:S(2)}) %collective-permute-start.26) | collective-permute-done | bytes 1179680 | tf_op jit(solution)/shard_map/ppermute | solution.py:255
  176.2 4.8 %shard_map.92 = bf16[192,3072]{1,0:T(8,128)(2,1)} custom-call(s32[3]{0:T(128)S(1)} %pad_add_fusion.1.at_ref, bf16[6144,3072]{1,0:T(8,128)(2,1)} %bitcast.48, bf16[576,512]{1,0:T(8,128)(2,1)S(1)} %collective-permute-done.28.factor_ref, bf16[3072,512]{1,0:T(8,128)(2,1)S(1)} %copy-done), custom_call_target="tpu_custom_call" | custom-call | flops 1 | bytes 1 | tf_op jit(solution)/shard_map/pallas_call | solution.py:36
  183.0 19.4 %collective-permute-done.32.refs_10_ = bf16[1536,512]{1,0:T(8,128)(2,1)S(1)} collective-permute-done((bf16[1536,512]{1,0:T(8,128)(2,1)S(1)}, bf16[1536,512]{1,0:T(8,128)(2,1)S(1)}, u32[]{:S(2)}, u32[]{:S(2)}) %collective-permute-start.32) | collective-permute-done | bytes 1572896 | tf_op jit(solution)/shard_map/ppermute | solution.py:429
  203.5 5.5 %shard_map.95.factor_ref = bf16[6144,512]{1,0:T(8,128)(2,1)} custom-call(s32[3]{0:T(128)S(1)} %pad_add_fusion.1.at_ref, bf16[768,512]{1,0:T(8,128)(2,1)S(1)} %copy-done.2, bf16[768,512]{1,0:T(8,128)(2,1)} %collective-permute-done.2.refs_1_, bf16[768,512]{1,0:T(8,128)(2,1)} %collective-permute-done.3.refs_2_, bf16[768,512]{1,0:T(8,128)(2,1)S(1)} %copy-done.8, ...), custom_call_target="tpu_custom_call" | custom-call | flops 1 | bytes 1 | tf_op jit(solution)/shard_map/pallas_call | solution.py:96
  209.1 13.5 %collective-permute-done.34.refs_1_ = bf16[576,2048]{1,0:T(8,128)(2,1)S(1)} collective-permute-done((bf16[576,2048]{1,0:T(8,128)(2,1)}, bf16[576,2048]{1,0:T(8,128)(2,1)S(1)}, u32[]{:S(2)}, u32[]{:S(2)}) %collective-permute-start.34) | collective-permute-done | bytes 2359328 | tf_op jit(solution)/shard_map/ppermute | solution.py:255
  222.6 5.3 %shard_map.99 = bf16[256,3072]{1,0:T(8,128)(2,1)} custom-call(s32[3]{0:T(128)S(1)} %pad_add_fusion.1.at_ref, bf16[6144,3072]{1,0:T(8,128)(2,1)} %bitcast.49, bf16[6144,512]{1,0:T(8,128)(2,1)} %shard_map.95.factor_ref, bf16[3072,512]{1,0:T(8,128)(2,1)S(1)} %copy-done), custom_call_target="tpu_custom_call" | custom-call | flops 1 | bytes 1 | tf_op jit(solution)/shard_map/pallas_call | solution.py:36
  233.9 4.3 %collective-permute-start.36 = (bf16[576,512]{1,0:T(8,128)(2,1)}, bf16[576,512]{1,0:T(8,128)(2,1)}, u32[]{:S(2)}, u32[]{:S(2)}) collective-permute-start(bf16[576,512]{1,0:T(8,128)(2,1)} %reshape.76.refs_0_), channel_id=1, source_target_pairs={{0,1},{1,2},{2,3},{4,5},{5,6},{6,7},{8,9},{9,10},{10,11},{12,13},{... | collective-permute-start | bytes 1769480 | tf_op jit(solution)/shard_map/ppermute | solution.py:184
  241.6 34.3 %shard_map.96.refs_4_ = f32[3072,3072]{1,0:T(8,128)} custom-call(s32[12]{0:T(128)S(1)} %iota.48.target_ref, s32[12]{0:T(128)S(1)} %get-tuple-element.145.own_ref, s32[12]{0:T(128)S(1)} %get-tuple-element.144.place_ref, bf16[6144,3072]{1,0:T(8,128)(2,1)} %bitcast.50, bf16[6144,512]{1,0:T(8,128)(2,1)} %shard_map.95.factor_ref, bf16[3072,512]{1,0:T(8,128)(2,1)S(1)} %copy-done, ...), custom_call_target="tpu_custom_call" | custom-call | flops 1 | bytes 1 | tf_op jit(solution)/shard_map/pallas_call | solution.py:125
  275.9 5.0 %shard_map.97 = bf16[256,3072]{1,0:T(8,128)(2,1)} custom-call(s32[3]{0:T(128)S(1)} %pad_add_fusion.1.at_ref, bf16[6144,3072]{1,0:T(8,128)(2,1)} %bitcast.51, bf16[6144,512]{1,0:T(8,128)(2,1)} %shard_map.95.factor_ref, bf16[3072,512]{1,0:T(8,128)(2,1)S(1)} %copy-done), custom_call_target="tpu_custom_call" | custom-call | flops 1 | bytes 1 | tf_op jit(solution)/shard_map/pallas_call | solution.py:36
  285.7 10.1 %shard_map.100.refs_2_ = f32[3072,3072]{1,0:T(8,128)} custom-call(s32[3]{0:T(128)S(1)} %get-tuple-element.142.target_ref, s32[5,12]{1,0:T(8,128)S(1)} %stack.50.place_ref, bf16[768,768]{1,0:T(8,128)(2,1)S(1)} %copy-done.19, bf16[768,768]{1,0:T(8,128)(2,1)S(1)} %copy-done.21, bf16[768,768]{1,0:T(8,128)(2,1)S(1)} %copy-done.23, ...), custom_call_target="tpu_custom_call", output_to_operand_aliasing={{}: (6, {})} | custom-call | flops 1 | bytes 1 | tf_op jit(solution)/shard_map/pallas_call | solution.py:167
  295.8 10.3 %shard_map.106 = bf16[576,2048]{1,0:T(8,128)(2,1)} custom-call(s32[3]{0:T(128)S(1)} %pad_add_fusion.1.at_ref, bf16[6144,3072]{1,0:T(8,128)(2,1)} %bitcast.52, bf16[6144,512]{1,0:T(8,128)(2,1)} %shard_map.95.factor_ref, bf16[3072,512]{1,0:T(8,128)(2,1)S(1)} %copy-done), custom_call_target="tpu_custom_call" | custom-call | flops 1 | bytes 1 | tf_op jit(solution)/shard_map/pallas_call | solution.py:36
  310.7 7.8 %collective-permute-done.33.refs_0_ = bf16[256,3072]{1,0:T(8,128)(2,1)} collective-permute-done((bf16[256,3072]{1,0:T(8,128)(2,1)}, bf16[256,3072]{1,0:T(8,128)(2,1)}, u32[]{:S(2)}, u32[]{:S(2)}) %collective-permute-start.33) | collective-permute-done | bytes 1572896 | tf_op jit(solution)/shard_map/ppermute | solution.py:255
  318.5 5.0 %shard_map.101 = bf16[256,3072]{1,0:T(8,128)(2,1)} custom-call(s32[3]{0:T(128)S(1)} %pad_add_fusion.1.at_ref, bf16[6144,3072]{1,0:T(8,128)(2,1)} %bitcast.53, bf16[6144,512]{1,0:T(8,128)(2,1)} %shard_map.95.factor_ref, bf16[3072,512]{1,0:T(8,128)(2,1)S(1)} %copy-done), custom_call_target="tpu_custom_call" | custom-call | flops 1 | bytes 1 | tf_op jit(solution)/shard_map/pallas_call | solution.py:36
  329.3 2.7 shard_map.103
  333.9 3.1 pad_maximum_fusion.front_ref
  342.6 8.8 %shard_map.105.refs_0_ = bf16[1152,1024]{1,0:T(8,128)(2,1)S(1)} custom-call(s32[3]{0:T(128)S(1)} %pad_add_fusion.1.at_ref, bf16[1152,1024]{1,0:T(8,128)(2,1)} %pad_maximum_fusion.front_ref, bf16[1152,512]{1,0:T(8,128)(2,1)S(1)} %shard_map.102.factor_ref, bf16[1024,512]{1,0:T(8,128)(2,1)S(1)} %shard_map.104.col_ref), custom_call_target="tpu_custom_call" | custom-call | flops 1 | bytes 1 | tf_op jit(solution)/shard_map/pallas_call | solution.py:36
  351.5 10.3 %shard_map.107.refs_1_ = f32[3072,3072]{1,0:T(8,128)} custom-call(s32[3]{0:T(128)S(1)} %get-tuple-element.140.target_ref, s32[3,12]{1,0:T(4,128)S(1)} %pad_add_fusion.place_ref, bf16[1152,1024]{1,0:T(8,128)(2,1)S(1)} %shard_map.105.refs_0_, bf16[576,2048]{1,0:T(8,128)(2,1)S(1)} %copy-done.17, ...), custom_call_target="tpu_custom_call", output_to_operand_aliasing={{}: (4, {})} | custom-call | flops 1 | bytes 1 | tf_op jit(solution)/shard_map/pallas_call | solution.py:167
  361.8 5.4 %shard_map.108.refs_1_ = f32[3072,3072]{1,0:T(8,128)} custom-call(s32[1]{0:T(128)} %bitcast.21.target_ref, s32[2,12]{1,0:T(2,128)S(1)} %stack.47.place_ref, bf16[192,3072]{1,0:T(8,128)(2,1)} %collective-permute-done.29.refs_0_, f32[3072,3072]{1,0:T(8,128)} %shard_map.107.refs_1_), custom_call_target="tpu_custom_call", output_to_operand_aliasing={{}: (3, {})} | custom-call | flops 1 | bytes 1 | tf_op jit(solution)/shard_map/pallas_call | solution.py:167
  367.2 5.0 %shard_map.109.refs_1_ = f32[3072,3072]{1,0:T(8,128)} custom-call(s32[1]{0:T(128)} %bitcast.20.target_ref, s32[2,12]{1,0:T(2,128)S(1)} %stack.47.place_ref, bf16[256,3072]{1,0:T(8,128)(2,1)} %collective-permute-done.35.refs_0_, f32[3072,3072]{1,0:T(8,128)} %shard_map.108.refs_1_), custom_call_target="tpu_custom_call", output_to_operand_aliasing={{}: (3, {})} | custom-call | flops 1 | bytes 1 | tf_op jit(solution)/shard_map/pallas_call | solution.py:167
  372.2 3.8 shard_map.113
  378.0 4.9 %shard_map.110.refs_2_ = f32[3072,3072]{1,0:T(8,128)} custom-call(s32[1]{0:T(128)} %bitcast.23.target_ref, s32[2,12]{1,0:T(2,128)S(1)} %stack.47.place_ref, bf16[256,3072]{1,0:T(8,128)(2,1)} %collective-permute-done.33.refs_0_, f32[3072,3072]{1,0:T(8,128)} %shard_map.109.refs_1_), custom_call_target="tpu_custom_call", output_to_operand_aliasing={{}: (3, {})} | custom-call | flops 1 | bytes 1 | tf_op jit(solution)/shard_map/pallas_call | solution.py:167
  383.0 10.7 %shard_map.111.refs_1_ = f32[3072,3072]{1,0:T(8,128)} custom-call(s32[3]{0:T(128)S(1)} %get-tuple-element.141.target_ref, s32[3,12]{1,0:T(4,128)S(1)} %pad_add_fusion.place_ref, bf16[1152,1024]{1,0:T(8,128)(2,1)S(1)} %shard_map.105.refs_0_, bf16[576,2048]{1,0:T(8,128)(2,1)} %collective-permute-done.44.refs_1_, ...), custom_call_target="tpu_custom_call", output_to_operand_aliasing={{}: (4, {})} | custom-call | flops 1 | bytes 1 | tf_op jit(solution)/shard_map/pallas_call | solution.py:167
  393.7 9.0 %collective-permute-done.38.refs_0_ = bf16[256,3072]{1,0:T(8,128)(2,1)} collective-permute-done((bf16[256,3072]{1,0:T(8,128)(2,1)}, bf16[256,3072]{1,0:T(8,128)(2,1)}, u32[]{:S(2)}, u32[]{:S(2)}) %collective-permute-start.38) | collective-permute-done | bytes 1572896 | tf_op jit(solution)/shard_map/ppermute | solution.py:255
  402.7 3.5 shard_map.112
  408.0 4.8 %shard_map.114.refs_1_ = f32[3072,3072]{1,0:T(8,128)} custom-call(s32[1]{0:T(128)} %bitcast.24.target_ref, s32[2,12]{1,0:T(2,128)S(1)} %stack.47.place_ref, bf16[256,3072]{1,0:T(8,128)(2,1)} %collective-permute-done.38.refs_0_, f32[3072,3072]{1,0:T(8,128)} %shard_map.111.refs_1_), custom_call_target="tpu_custom_call", output_to_operand_aliasing={{}: (3, {})} | custom-call | flops 1 | bytes 1 | tf_op jit(solution)/shard_map/pallas_call | solution.py:167
  412.8 6.7 %collective-permute-done.46.refs_0_ = bf16[128,3072]{1,0:T(8,128)(2,1)S(1)} collective-permute-done((bf16[128,3072]{1,0:T(8,128)(2,1)S(1)}, bf16[128,3072]{1,0:T(8,128)(2,1)S(1)}, u32[]{:S(2)}, u32[]{:S(2)}) %collective-permute-start.46) | collective-permute-done | bytes 786464 | tf_op jit(solution)/shard_map/ppermute | solution.py:255
  419.5 3.9 shard_map.115.refs_1_
  424.1 3.1 shard_map.116
  (190 shorter events, 92.5 us)
Async XLA Ops:
  2.5 21.4 %collective-permute-start.4 = (bf16[384,1024]{1,0:T(8,128)(2,1)S(1)}, bf16[384,1024]{1,0:T(8,128)(2,1)S(1)}, u32[]{:S(2)}, u32[]{:S(2)}) collective-permute-start(bf16[384,1024]{1,0:T(8,128)(2,1)S(1)} %shard_map.77), channel_id=1, source_target_pairs={{0,8},{8,0},{16,24},{24,16},{1,9},{9,1},{17,25},{25,17},{2,10},{10... | collective-permute-start | bytes 2359304 | tf_op jit(solution)/shard_map/ppermute | solution.py:255
  7.5 20.0 %collective-permute-start.2 = (bf16[768,512]{1,0:T(8,128)(2,1)S(1)}, bf16[768,512]{1,0:T(8,128)(2,1)}, u32[]{:S(2)}, u32[]{:S(2)}) collective-permute-start(bf16[768,512]{1,0:T(8,128)(2,1)S(1)} %convolution_convert_fusion.1.refs_0_), channel_id=1, source_target_pairs={{0,1},{1,2},{2,3},{4,5},{5,6},{6,7},{8,9},{9,10},{10,11},{12,13},{... | collective-permute-start | bytes 2359304 | tf_op jit(solution)/shard_map/ppermute | solution.py:184
  11.9 20.7 %collective-permute-start.3 = (bf16[768,512]{1,0:T(8,128)(2,1)S(1)}, bf16[768,512]{1,0:T(8,128)(2,1)}, u32[]{:S(2)}, u32[]{:S(2)}) collective-permute-start(bf16[768,512]{1,0:T(8,128)(2,1)S(1)} %convolution_convert_fusion.1.refs_0_), channel_id=1, source_target_pairs={{1,0},{2,1},{3,2},{5,4},{6,5},{7,6},{9,8},{10,9},{11,10},{13,12},{... | collective-permute-start | bytes 2359304 | tf_op jit(solution)/shard_map/ppermute | solution.py:184
  15.8 33.4 %collective-permute-start.1 = (bf16[576,1024]{1,0:T(8,128)(2,1)}, bf16[576,1024]{1,0:T(8,128)(2,1)}, u32[]{:S(2)}, u32[]{:S(2)}) collective-permute-start(bf16[576,1024]{1,0:T(8,128)(2,1)} %shard_map.79), channel_id=1, source_target_pairs={{0,8},{8,0},{16,24},{24,16},{1,9},{9,1},{17,25},{25,17},{2,10},{10... | collective-permute-start | bytes 3538952 | tf_op jit(solution)/shard_map/ppermute | solution.py:255
  23.9 10.3 %collective-permute-start.5 = (s32[48]{0:T(128)S(1)}, s32[48]{0:T(128)S(1)}, u32[]{:S(2)}, u32[]{:S(2)}) collective-permute-start(s32[48]{0:T(128)S(1)} %bitcast.62), channel_id=1, source_target_pairs={{0,4},{4,0},{1,5},{5,1},{2,6},{6,2},{3,7},{7,3},{8,12},{12,8},{9,1... | collective-permute-start | bytes 584 | tf_op jit(solution)/shard_map/ppermute | solution.py:193
  34.1 16.3 %collective-permute-start.9 = (bf16[768,512]{1,0:T(8,128)(2,1)}, bf16[768,512]{1,0:T(8,128)(2,1)}, u32[]{:S(2)}, u32[]{:S(2)}) collective-permute-start(bf16[768,512]{1,0:T(8,128)(2,1)} %shard_map.81.refs_0_), channel_id=1, source_target_pairs={{0,4},{4,0},{1,5},{5,1},{2,6},{6,2},{3,7},{7,3},{8,12},{12,8},{9,1... | collective-permute-start | bytes 2359304 | tf_op jit(solution)/shard_map/ppermute | solution.py:193
  34.2 17.9 %collective-permute-start.7 = (bf16[768,512]{1,0:T(8,128)(2,1)}, bf16[768,512]{1,0:T(8,128)(2,1)S(1)}, u32[]{:S(2)}, u32[]{:S(2)}) collective-permute-start(bf16[768,512]{1,0:T(8,128)(2,1)} %collective-permute-done.2.refs_1_), channel_id=1, source_target_pairs={{1,2},{2,3},{5,6},{6,7},{9,10},{10,11},{13,14},{14,15},{17,18},{18... | collective-permute-start | bytes 2359304 | tf_op jit(solution)/shard_map/ppermute | solution.py:184
  34.9 24.6 %collective-permute-start.8 = (bf16[768,512]{1,0:T(8,128)(2,1)}, bf16[768,512]{1,0:T(8,128)(2,1)S(1)}, u32[]{:S(2)}, u32[]{:S(2)}) collective-permute-start(bf16[768,512]{1,0:T(8,128)(2,1)} %collective-permute-done.3.refs_2_), channel_id=1, source_target_pairs={{1,0},{2,1},{5,4},{6,5},{9,8},{10,9},{13,12},{14,13},{17,16},{18,1... | collective-permute-start | bytes 2359304 | tf_op jit(solution)/shard_map/ppermute | solution.py:184
  36.9 91.4 %copy-start.4 = (bf16[768,512]{1,0:T(8,128)(2,1)}, bf16[768,512]{1,0:T(8,128)(2,1)S(1)}, u32[]{:S(2)}) copy-start(bf16[768,512]{1,0:T(8,128)(2,1)S(1)} %convolution_convert_fusion.refs_0_.refs_5_) | copy-start | bytes 2359300
  41.1 29.8 %collective-permute-start = (bf16[496,1024]{1,0:T(8,128)(2,1)S(1)}, bf16[496,1024]{1,0:T(8,128)(2,1)S(1)}, u32[]{:S(2)}, u32[]{:S(2)}) collective-permute-start(bf16[496,1024]{1,0:T(8,128)(2,1)S(1)} %pad_maximum_fusion.1), channel_id=1, source_target_pairs={{0,8},{8,0},{16,24},{24,16},{1,9},{9,1},{17,25},{25,17},{2,10},{10... | collective-permute-start | bytes 3047432 | tf_op jit(solution)/shard_map/ppermute | solution.py:255
  49.3 1.1 collective-permute-start.6
  65.7 5.2 %collective-permute-start.10 = (bf16[768,512]{1,0:T(8,128)(2,1)S(1)}, bf16[768,512]{1,0:T(8,128)(2,1)S(1)}, u32[]{:S(2)}, u32[]{:S(2)}) collective-permute-start(bf16[768,512]{1,0:T(8,128)(2,1)S(1)} %shard_map.84.refs_0_), channel_id=1, source_target_pairs={{0,4},{4,0},{1,5},{5,1},{2,6},{6,2},{3,7},{7,3},{8,12},{12,8},{9,1... | collective-permute-start | bytes 2359304 | tf_op jit(solution)/shard_map/ppermute | solution.py:193
  65.8 5.8 %collective-permute-start.12 = (bf16[768,512]{1,0:T(8,128)(2,1)S(1)}, bf16[768,512]{1,0:T(8,128)(2,1)S(1)}, u32[]{:S(2)}, u32[]{:S(2)}) collective-permute-start(bf16[768,512]{1,0:T(8,128)(2,1)S(1)} %convolution_convert_fusion.refs_0_.refs_5_), channel_id=1, source_target_pairs={{0,4},{4,0},{1,5},{5,1},{2,6},{6,2},{3,7},{7,3},{8,12},{12,8},{9,1... | collective-permute-start | bytes 2359304 | tf_op jit(solution)/shard_map/ppermute | solution.py:193
  66.3 29.9 %collective-permute-start.16 = (bf16[768,768]{1,0:T(8,128)(2,1)S(1)}, bf16[768,768]{1,0:T(8,128)(2,1)S(1)}, u32[]{:S(2)}, u32[]{:S(2)}) collective-permute-start(bf16[768,768]{1,0:T(8,128)(2,1)S(1)} %shard_map.83), channel_id=1, source_target_pairs={{0,8},{8,0},{16,24},{24,16},{1,9},{9,1},{17,25},{25,17},{2,10},{10... | collective-permute-start | bytes 3538952 | tf_op jit(solution)/shard_map/ppermute | solution.py:255
  70.9 1.1 collective-permute-start.11
  72.0 26.4 %collective-permute-start.13 = (bf16[768,512]{1,0:T(8,128)(2,1)S(1)}, bf16[768,512]{1,0:T(8,128)(2,1)S(1)}, u32[]{:S(2)}, u32[]{:S(2)}) collective-permute-start(bf16[768,512]{1,0:T(8,128)(2,1)S(1)} %convolution_convert_fusion.refs_0_.refs_5_), channel_id=1, source_target_pairs={{0,1},{1,2},{2,3},{4,5},{5,6},{6,7},{8,9},{9,10},{10,11},{12,13},{... | collective-permute-start | bytes 2359304 | tf_op jit(solution)/shard_map/ppermute | solution.py:184
  75.9 22.5 %collective-permute-start.14 = (bf16[768,512]{1,0:T(8,128)(2,1)S(1)}, bf16[768,512]{1,0:T(8,128)(2,1)S(1)}, u32[]{:S(2)}, u32[]{:S(2)}) collective-permute-start(bf16[768,512]{1,0:T(8,128)(2,1)S(1)} %convolution_convert_fusion.refs_0_.refs_5_), channel_id=1, source_target_pairs={{1,0},{2,1},{3,2},{5,4},{6,5},{7,6},{9,8},{10,9},{11,10},{13,12},{... | collective-permute-start | bytes 2359304 | tf_op jit(solution)/shard_map/ppermute | solution.py:184
  77.2 21.2 %collective-permute-start.15 = (bf16[768,512]{1,0:T(8,128)(2,1)S(1)}, bf16[768,512]{1,0:T(8,128)(2,1)S(1)}, u32[]{:S(2)}, u32[]{:S(2)}) collective-permute-start(bf16[768,512]{1,0:T(8,128)(2,1)S(1)} %convolution_convert_fusion.refs_0_.refs_5_), channel_id=1, source_target_pairs={{2,5},{5,2},{10,13},{13,10},{18,21},{21,18},{26,29},{29,26}} | collective-permute-start | bytes 2359304 | tf_op jit(solution)/shard_map/ppermute | solution.py:380
  81.8 39.7 %collective-permute-start.21 = (bf16[768,768]{1,0:T(8,128)(2,1)S(1)}, bf16[768,768]{1,0:T(8,128)(2,1)S(1)}, u32[]{:S(2)}, u32[]{:S(2)}) collective-permute-start(bf16[768,768]{1,0:T(8,128)(2,1)S(1)} %shard_map.87), channel_id=1, source_target_pairs={{0,8},{8,0},{16,24},{24,16},{1,9},{9,1},{17,25},{25,17},{2,10},{10... | collective-permute-start | bytes 3538952 | tf_op jit(solution)/shard_map/ppermute | solution.py:255
  96.2 1.1 collective-permute-start.17
  97.3 1.1 collective-permute-start.18
  98.5 25.5 %collective-permute-start.19 = (bf16[768,512]{1,0:T(8,128)(2,1)S(1)}, bf16[768,512]{1,0:T(8,128)(2,1)S(1)}, u32[]{:S(2)}, u32[]{:S(2)}) collective-permute-start(bf16[768,512]{1,0:T(8,128)(2,1)S(1)} %collective-permute-done.13.refs_1_.refs_6_), channel_id=1, source_target_pairs={{1,2},{2,3},{5,6},{6,7},{9,10},{10,11},{13,14},{14,15},{17,18},{18... | collective-permute-start | bytes 2359304 | tf_op jit(solution)/shard_map/ppermute | solution.py:184
  99.2 29.1 %collective-permute-start.20 = (bf16[768,512]{1,0:T(8,128)(2,1)S(1)}, bf16[768,512]{1,0:T(8,128)(2,1)S(1)}, u32[]{:S(2)}, u32[]{:S(2)}) collective-permute-start(bf16[768,512]{1,0:T(8,128)(2,1)S(1)} %collective-permute-done.14.refs_2_.refs_7_), channel_id=1, source_target_pairs={{1,0},{2,1},{5,4},{6,5},{9,8},{10,9},{13,12},{14,13},{17,16},{18,1... | collective-permute-start | bytes 2359304 | tf_op jit(solution)/shard_map/ppermute | solution.py:184
  105.0 41.8 %collective-permute-start.30 = (bf16[768,768]{1,0:T(8,128)(2,1)S(1)}, bf16[768,768]{1,0:T(8,128)(2,1)S(1)}, u32[]{:S(2)}, u32[]{:S(2)}) collective-permute-start(bf16[768,768]{1,0:T(8,128)(2,1)S(1)} %shard_map.93), channel_id=1, source_target_pairs={{0,8},{8,0},{16,24},{24,16},{1,9},{9,1},{17,25},{25,17},{2,10},{10... | collective-permute-start | bytes 3538952 | tf_op jit(solution)/shard_map/ppermute | solution.py:255
  121.5 1.1 collective-permute-start.22
  122.6 1.1 collective-permute-start.23
  123.7 5.3 %collective-permute-start.24 = (s32[48]{0:T(128)S(1)}, s32[48]{0:T(128)S(1)}, u32[]{:S(2)}, u32[]{:S(2)}) collective-permute-start(s32[48]{0:T(128)S(1)} %collective-permute-done.23), channel_id=1, source_target_pairs={{0,4},{4,0},{1,5},{5,1},{2,6},{6,2},{3,7},{7,3},{8,12},{12,8},{9,1... | collective-permute-start | bytes 584 | tf_op jit(solution)/shard_map/ppermute | solution.py:193
  129.0 2.4 collective-permute-start.25
  136.8 35.4 %collective-permute-start.26 = (bf16[768,768]{1,0:T(8,128)(2,1)}, bf16[768,768]{1,0:T(8,128)(2,1)}, u32[]{:S(2)}, u32[]{:S(2)}) collective-permute-start(bf16[768,768]{1,0:T(8,128)(2,1)} %shard_map.89), channel_id=1, source_target_pairs={{0,8},{8,0},{16,24},{24,16},{1,9},{9,1},{17,25},{25,17},{2,10},{10... | collective-permute-start | bytes 3538952 | tf_op jit(solution)/shard_map/ppermute | solution.py:255
  146.8 1.1 collective-permute-start.31
  161.5 61.1 %collective-permute-start.34 = (bf16[576,2048]{1,0:T(8,128)(2,1)}, bf16[576,2048]{1,0:T(8,128)(2,1)S(1)}, u32[]{:S(2)}, u32[]{:S(2)}) collective-permute-start(bf16[576,2048]{1,0:T(8,128)(2,1)} %shard_map.98), channel_id=1, source_target_pairs={{0,8},{8,0},{16,24},{24,16},{1,9},{9,1},{17,25},{25,17},{2,10},{10... | collective-permute-start | bytes 7077896 | tf_op jit(solution)/shard_map/ppermute | solution.py:255
  164.3 38.1 %collective-permute-start.32 = (bf16[1536,512]{1,0:T(8,128)(2,1)S(1)}, bf16[1536,512]{1,0:T(8,128)(2,1)S(1)}, u32[]{:S(2)}, u32[]{:S(2)}) collective-permute-start(bf16[1536,512]{1,0:T(8,128)(2,1)S(1)} %shard_map.94), channel_id=1, source_target_pairs={{2,3},{1,0},{6,7},{5,4},{10,11},{9,8},{14,15},{13,12},{18,19},{17,... | collective-permute-start | bytes 4718600 | tf_op jit(solution)/shard_map/ppermute | solution.py:429
  172.1 2.0 collective-permute-start.27
  174.1 2.0 collective-permute-start.28
  181.0 94.9 %collective-permute-start.29 = (bf16[192,3072]{1,0:T(8,128)(2,1)}, bf16[192,3072]{1,0:T(8,128)(2,1)}, u32[]{:S(2)}, u32[]{:S(2)}) collective-permute-start(bf16[192,3072]{1,0:T(8,128)(2,1)} %shard_map.92), channel_id=1, source_target_pairs={{0,8},{8,0},{16,24},{24,16},{1,9},{9,1},{17,25},{25,17},{2,10},{10... | collective-permute-start | bytes 3538952 | tf_op jit(solution)/shard_map/ppermute | solution.py:255
  227.9 68.0 %collective-permute-start.35 = (bf16[256,3072]{1,0:T(8,128)(2,1)}, bf16[256,3072]{1,0:T(8,128)(2,1)}, u32[]{:S(2)}, u32[]{:S(2)}) collective-permute-start(bf16[256,3072]{1,0:T(8,128)(2,1)} %shard_map.99), channel_id=1, source_target_pairs={{0,8},{8,0},{16,24},{24,16},{1,9},{9,1},{17,25},{25,17},{2,10},{10... | collective-permute-start | bytes 4718600 | tf_op jit(solution)/shard_map/ppermute | solution.py:255
  233.9 48.0 %collective-permute-start.36 = (bf16[576,512]{1,0:T(8,128)(2,1)}, bf16[576,512]{1,0:T(8,128)(2,1)}, u32[]{:S(2)}, u32[]{:S(2)}) collective-permute-start(bf16[576,512]{1,0:T(8,128)(2,1)} %reshape.76.refs_0_), channel_id=1, source_target_pairs={{0,1},{1,2},{2,3},{4,5},{5,6},{6,7},{8,9},{9,10},{10,11},{12,13},{... | collective-permute-start | bytes 1769480 | tf_op jit(solution)/shard_map/ppermute | solution.py:184
  238.2 43.7 %collective-permute-start.37 = (bf16[576,512]{1,0:T(8,128)(2,1)}, bf16[576,512]{1,0:T(8,128)(2,1)}, u32[]{:S(2)}, u32[]{:S(2)}) collective-permute-start(bf16[576,512]{1,0:T(8,128)(2,1)} %reshape.76.refs_0_), channel_id=1, source_target_pairs={{1,0},{2,1},{3,2},{5,4},{6,5},{7,6},{9,8},{10,9},{11,10},{13,12},{... | collective-permute-start | bytes 1769480 | tf_op jit(solution)/shard_map/ppermute | solution.py:184
  280.8 37.6 %collective-permute-start.33 = (bf16[256,3072]{1,0:T(8,128)(2,1)}, bf16[256,3072]{1,0:T(8,128)(2,1)}, u32[]{:S(2)}, u32[]{:S(2)}) collective-permute-start(bf16[256,3072]{1,0:T(8,128)(2,1)} %shard_map.97), channel_id=1, source_target_pairs={{0,8},{8,0},{16,24},{24,16},{1,9},{9,1},{17,25},{25,17},{2,10},{10... | collective-permute-start | bytes 4718600 | tf_op jit(solution)/shard_map/ppermute | solution.py:255
  306.1 66.0 %collective-permute-start.44 = (bf16[576,2048]{1,0:T(8,128)(2,1)}, bf16[576,2048]{1,0:T(8,128)(2,1)}, u32[]{:S(2)}, u32[]{:S(2)}) collective-permute-start(bf16[576,2048]{1,0:T(8,128)(2,1)} %shard_map.106), channel_id=1, source_target_pairs={{0,8},{8,0},{16,24},{24,16},{1,9},{9,1},{17,25},{25,17},{2,10},{10... | collective-permute-start | bytes 7077896 | tf_op jit(solution)/shard_map/ppermute | solution.py:255
  307.8 16.1 %collective-permute-start.39 = (bf16[576,512]{1,0:T(8,128)(2,1)}, bf16[576,512]{1,0:T(8,128)(2,1)}, u32[]{:S(2)}, u32[]{:S(2)}) collective-permute-start(bf16[576,512]{1,0:T(8,128)(2,1)} %collective-permute-done.36.refs_1_), channel_id=1, source_target_pairs={{1,2},{2,3},{5,6},{6,7},{9,10},{10,11},{13,14},{14,15},{17,18},{18... | collective-permute-start | bytes 1769480 | tf_op jit(solution)/shard_map/ppermute | solution.py:184
  309.4 16.5 %collective-permute-start.40 = (bf16[576,512]{1,0:T(8,128)(2,1)}, bf16[576,512]{1,0:T(8,128)(2,1)}, u32[]{:S(2)}, u32[]{:S(2)}) collective-permute-start(bf16[576,512]{1,0:T(8,128)(2,1)} %collective-permute-done.37.refs_2_), channel_id=1, source_target_pairs={{1,0},{2,1},{5,4},{6,5},{9,8},{10,9},{13,12},{14,13},{17,16},{18,1... | collective-permute-start | bytes 1769480 | tf_op jit(solution)/shard_map/ppermute | solution.py:184
  323.4 79.3 %collective-permute-start.38 = (bf16[256,3072]{1,0:T(8,128)(2,1)}, bf16[256,3072]{1,0:T(8,128)(2,1)}, u32[]{:S(2)}, u32[]{:S(2)}) collective-permute-start(bf16[256,3072]{1,0:T(8,128)(2,1)} %shard_map.101), channel_id=1, source_target_pairs={{0,8},{8,0},{16,24},{24,16},{1,9},{9,1},{17,25},{25,17},{2,10},{10... | collective-permute-start | bytes 4718600 | tf_op jit(solution)/shard_map/ppermute | solution.py:255
  327.9 13.0 %collective-permute-start.41 = (bf16[576,512]{1,0:T(8,128)(2,1)}, bf16[576,512]{1,0:T(8,128)(2,1)}, u32[]{:S(2)}, u32[]{:S(2)}) collective-permute-start(bf16[576,512]{1,0:T(8,128)(2,1)} %broadcast_select_fusion), channel_id=1, source_target_pairs={{2,3},{1,0},{6,7},{5,4},{10,11},{9,8},{14,15},{13,12},{18,19},{17,... | collective-permute-start | bytes 1769480 | tf_op jit(solution)/shard_map/ppermute | solution.py:449
  332.0 5.1 %collective-permute-start.42 = (bf16[512,512]{1,0:T(8,128)(2,1)}, bf16[512,512]{1,0:T(8,128)(2,1)}, u32[]{:S(2)}, u32[]{:S(2)}) collective-permute-start(bf16[512,512]{1,0:T(8,128)(2,1)} %get-tuple-element.110.refs_0_), channel_id=1, source_target_pairs={{0,4},{4,0},{1,5},{5,1},{2,6},{6,2},{3,7},{7,3},{8,12},{12,8},{9,1... | collective-permute-start | bytes 1572872 | tf_op jit(solution)/shard_map/ppermute | solution.py:193
  332.1 5.0 %collective-permute-start.43 = (bf16[512,512]{1,0:T(8,128)(2,1)}, bf16[512,512]{1,0:T(8,128)(2,1)}, u32[]{:S(2)}, u32[]{:S(2)}) collective-permute-start(bf16[512,512]{1,0:T(8,128)(2,1)} %get-tuple-element.111.refs_1_), channel_id=1, source_target_pairs={{0,4},{4,0},{1,5},{5,1},{2,6},{6,2},{3,7},{7,3},{8,12},{12,8},{9,1... | collective-permute-start | bytes 1572872 | tf_op jit(solution)/shard_map/ppermute | solution.py:193
  375.9 43.5 %collective-permute-start.46 = (bf16[128,3072]{1,0:T(8,128)(2,1)S(1)}, bf16[128,3072]{1,0:T(8,128)(2,1)S(1)}, u32[]{:S(2)}, u32[]{:S(2)}) collective-permute-start(bf16[128,3072]{1,0:T(8,128)(2,1)S(1)} %shard_map.113), channel_id=1, source_target_pairs={{0,8},{8,0},{16,24},{24,16},{1,9},{9,1},{17,25},{25,17},{2,10},{10... | collective-permute-start | bytes 2359304 | tf_op jit(solution)/shard_map/ppermute | solution.py:255
  406.3 17.9 %collective-permute-start.45 = (bf16[64,3072]{1,0:T(8,128)(2,1)S(1)}, bf16[64,3072]{1,0:T(8,128)(2,1)S(1)}, u32[]{:S(2)}, u32[]{:S(2)}) collective-permute-start(bf16[64,3072]{1,0:T(8,128)(2,1)S(1)} %shard_map.112), channel_id=1, source_target_pairs={{0,8},{8,0},{16,24},{24,16},{1,9},{9,1},{17,25},{25,17},{2,10},{10... | collective-permute-start | bytes 1179656 | tf_op jit(solution)/shard_map/ppermute | solution.py:255
  (34 other events, 437.4 us)

commit v4 on v3

--- a/solution.py
+++ b/solution.py
@@ -174,6 +174,70 @@
         compiler_params=pltpu.CompilerParams(vmem_limit_bytes=VMEM_LIMIT),
         cost_estimate=SMALL,
     )(targets, places, *(piece for piece, _ in pieces), base)
+
+
+def add_ahead_kernel(blocks, steps, target_ref, place_ref, piece_ref, base_ref, out_ref, held_ref):
+    held_ref[...] = base_ref[...]
+    out_ref[...] = base_ref[...]
+
+    @pl.when(pl.program_id(0) < steps)
+    def _():
+        for block in range(blocks):
+            here = pl.ds(block * BLK, BLK)
+            arrived = piece_ref[:, pl.ds(pl.multiple_of(place_ref[1, block] * BLK, BLK), BLK)]
+            out_ref[:, here] = base_ref[:, here] + arrived.astype(jnp.float32)
+
+
+def add_ahead(base, targets, places, piece, step, first):
+    parts = BLK // step
+    steps = piece.shape[0] // step
+    cols = base.shape[1]
+    row = pl.BlockSpec((step, cols), lambda i, targets, places: (
+        jnp.where(i < steps, targets[0] * parts + i, targets[1] * parts + first // step), 0
+    ))
+    return pl.pallas_call(
+        functools.partial(add_ahead_kernel, cols // BLK, steps),
+        grid_spec=pltpu.PrefetchScalarGridSpec(
+            num_scalar_prefetch=2,
+            grid=(steps + 1,),
+            in_specs=[pl.BlockSpec((step, cols), lambda i, *_: (jnp.minimum(i, steps - 1), 0)), row],
+            out_specs=[row, pl.BlockSpec((step, cols), lambda i, *_: (0, 0))],
+        ),
+        out_shape=[
+            jax.ShapeDtypeStruct(base.shape, jnp.float32), jax.ShapeDtypeStruct((step, cols), jnp.float32)
+        ],
+        input_output_aliases={3: 0},
+        compiler_params=pltpu.CompilerParams(vmem_limit_bytes=VMEM_LIMIT),
+        cost_estimate=SMALL,
+    )(targets, places, piece, base)
+
+
+def add_held_kernel(blocks, target_ref, place_ref, piece_ref, held_ref, base_ref, out_ref):
+    for block in range(blocks):
+        here = pl.ds(block * BLK, BLK)
+        arrived = piece_ref[:, pl.ds(pl.multiple_of(place_ref[1, block] * BLK, BLK), BLK)]
+        out_ref[:, here] = held_ref[:, here] + arrived.astype(jnp.float32)
+
+
+def add_held(base, target, places, piece, held, first):
+    rows, cols = piece.shape
+    step = rows // 2
+    parts = BLK // step
+    skip = first // step
+    part = pl.BlockSpec((step, cols), lambda i, *_: (i, 0))
+    return pl.pallas_call(
+        functools.partial(add_held_kernel, cols // BLK),
+        grid_spec=pltpu.PrefetchScalarGridSpec(
+            num_scalar_prefetch=2,
+            grid=(2,),
+            in_specs=[part, part, pl.BlockSpec(memory_space=pl.ANY)],
+            out_specs=pl.BlockSpec((step, cols), lambda i, target, places: (target[0] * parts + skip + i, 0)),
+        ),
+        out_shape=jax.ShapeDtypeStruct(base.shape, jnp.float32),
+        input_output_aliases={4: 0},
+        compiler_params=pltpu.CompilerParams(vmem_limit_bytes=VMEM_LIMIT),
+        cost_estimate=SMALL,
+    )(target, places, piece, held, base)
 
 
 def take_block(table, first, count):
@@ -522,9 +586,9 @@
     out = add_cut(out, kept_outer, 8, cut)
     at_i, arrived[9], out = after((at, arrived[9], out))
     whole_row(at_i, False, 3 * BLK + STEP, small, row_side, outer_row(3 * BLK + STEP))
-    out = add_whole(out, kept_outer + 2, 9)
+    out, held = add_ahead(out, take_block(landed, kept_outer + 2, 2), places_w, arrived[9], small, STEP)
     out = add_whole(out, kept_outer + 3, 10, STEP)
-    out = add_whole(out, kept_outer + 3, 11, small, small // 2, STEP)
+    out = add_held(out, take_block(landed, kept_outer + 3, 1), places_w, arrived[11], held, STEP)
     factor = jnp.concatenate([factor_a, factor_b], axis=0)
     return factor[None], out[None]
 

time: 430 us -> 429 us (level)
    pallas_call x0 -> x2, Pallas kernels: none -> 8.96 us  [the longest x1 6.79 us: add_ahead(): pl.pallas_call(functools.partial(add_ahead_kernel, cols // BLK, steps), g...]
    pallas_call x9 -> x7, Pallas kernels: 58.3 us -> 50.6 us  [add_rows(): pl.pallas_call(functools.partial(add_kernel, cols // BLK, len(pieces)), g...]
    ppermute x15, waiting for transfers between devices: 96.1 us -> 91.8 us  [from_sibling(): return lax.ppermute(block, 'front', route)]
where the time goes in v4:
time: 429 us; the launch traced here: 426 us
  Pallas kernels  198 us (46%)
  waiting for transfers between devices  149 us (35%)
  starting transfers between devices  50.9 us (12%)
  local copies, waits for them, and re-layouts  12.9 us (3%)
  other arithmetic  12.5 us (3%)
    ppermute x15, waiting for transfers between devices, from_sibling(): return lax.ppermute(block, 'front', route)  91.8 us
    pallas_call x13, Pallas kernels, updated_rows(): pl.pallas_call(functools.partial(update_kernel, unit, col_unit), grid_spe...  74.6 us
    pallas_call x7, Pallas kernels, add_rows(): pl.pallas_call(functools.partial(add_kernel, cols // BLK, len(pieces)), g...  50.6 us
    pallas_call x1, Pallas kernels, kept_rows(): pl.pallas_call(functools.partial(base_kernel, cols // BLK), grid_spec=plt...  34.3 us
    pallas_call x14, Pallas kernels, assembled(): pl.pallas_call(functools.partial(assemble_kernel, plan, len(sources)), gr...  22.9 us
    ppermute x15, starting transfers between devices, from_sibling(): return lax.ppermute(block, 'front', route)  22.1 us
    ppermute x1, waiting for transfers between devices, shards(): far = lax.ppermute(last_hop, 'col', FAR)  19.3 us
    ppermute x6, waiting for transfers between devices, hop(): lax.ppermute(down_block, 'col', down)  18.9 us
  transfers between devices with their start and end apart: 47, of which 29 were waited for; matrix products, arithmetic and copies ran while one was open for 5% of the time, Pallas kernels for 45%

profile of v4, /device:TPU:0, one launch (start us, length us, event | category | flops | bytes accessed | tf_op | source)
XLA Modules:
  0.0 426.4 jit_solution(8818429571359691884)
XLA Ops:
  2.5 3.0 collective-permute-start.4
  7.5 4.4 %collective-permute-start.2 = (bf16[768,512]{1,0:T(8,128)(2,1)S(1)}, bf16[768,512]{1,0:T(8,128)(2,1)}, u32[]{:S(2)}, u32[]{:S(2)}) collective-permute-start(bf16[768,512]{1,0:T(8,128)(2,1)S(1)} %convolution_convert_fusion.1.refs_0_), channel_id=1, source_target_pairs={{0,1},{1,2},{2,3},{4,5},{5,6},{6,7},{8,9},{9,10},{10,11},{12,13},{... | collective-permute-start | bytes 2359304 | tf_op jit(solution)/shard_map/ppermute | solution.py:248
  13.1 2.7 shard_map.79
  18.0 5.8 %collective-permute-done.4 = bf16[384,1024]{1,0:T(8,128)(2,1)S(1)} collective-permute-done((bf16[384,1024]{1,0:T(8,128)(2,1)S(1)}, bf16[384,1024]{1,0:T(8,128)(2,1)S(1)}, u32[]{:S(2)}, u32[]{:S(2)}) %collective-permute-start.4) | collective-permute-done | bytes 786464 | tf_op jit(solution)/shard_map/ppermute | solution.py:319
  23.9 3.6 collective-permute-done.2.refs_1_
  27.5 5.1 %collective-permute-done.3.refs_2_ = bf16[768,512]{1,0:T(8,128)(2,1)} collective-permute-done((bf16[768,512]{1,0:T(8,128)(2,1)S(1)}, bf16[768,512]{1,0:T(8,128)(2,1)}, u32[]{:S(2)}, u32[]{:S(2)}) %collective-permute-start.3) | collective-permute-done | bytes 786464 | tf_op jit(solution)/shard_map/ppermute | solution.py:248
  41.7 7.6 %collective-permute-done.1 = bf16[576,1024]{1,0:T(8,128)(2,1)} collective-permute-done((bf16[576,1024]{1,0:T(8,128)(2,1)}, bf16[576,1024]{1,0:T(8,128)(2,1)}, u32[]{:S(2)}, u32[]{:S(2)}) %collective-permute-start.1) | collective-permute-done | bytes 1179680 | tf_op jit(solution)/shard_map/ppermute | solution.py:319
  52.1 7.4 %collective-permute-done.8.refs_4_.refs_1_ = bf16[768,512]{1,0:T(8,128)(2,1)S(1)} collective-permute-done((bf16[768,512]{1,0:T(8,128)(2,1)}, bf16[768,512]{1,0:T(8,128)(2,1)S(1)}, u32[]{:S(2)}, u32[]{:S(2)}) %collective-permute-start.8) | collective-permute-done | bytes 786464 | tf_op jit(solution)/shard_map/ppermute | solution.py:248
  60.1 3.8 shard_map.83
  67.9 3.0 collective-permute-done
  72.0 3.9 collective-permute-start.13
  77.9 3.8 shard_map.87
  83.5 12.7 %collective-permute-done.16.refs_0_ = bf16[768,768]{1,0:T(8,128)(2,1)S(1)} collective-permute-done((bf16[768,768]{1,0:T(8,128)(2,1)S(1)}, bf16[768,768]{1,0:T(8,128)(2,1)S(1)}, u32[]{:S(2)}, u32[]{:S(2)}) %collective-permute-start.16) | collective-permute-done | bytes 1179680 | tf_op jit(solution)/shard_map/ppermute | solution.py:319
  101.2 3.8 shard_map.93
  107.1 14.4 %collective-permute-done.21.refs_1_ = bf16[768,768]{1,0:T(8,128)(2,1)S(1)} collective-permute-done((bf16[768,768]{1,0:T(8,128)(2,1)S(1)}, bf16[768,768]{1,0:T(8,128)(2,1)S(1)}, u32[]{:S(2)}, u32[]{:S(2)}) %collective-permute-start.21) | collective-permute-done | bytes 1179680 | tf_op jit(solution)/shard_map/ppermute | solution.py:319
  123.9 4.3 %collective-permute-done.20.refs_4_.refs_3_.refs_9_ = bf16[768,512]{1,0:T(8,128)(2,1)S(1)} collective-permute-done((bf16[768,512]{1,0:T(8,128)(2,1)S(1)}, bf16[768,512]{1,0:T(8,128)(2,1)S(1)}, u32[]{:S(2)}, u32[]{:S(2)}) %collective-permute-start.20) | collective-permute-done | bytes 786464 | tf_op jit(solution)/shard_map/ppermute | solution.py:248
  132.0 4.8 %shard_map.89 = bf16[768,768]{1,0:T(8,128)(2,1)} custom-call(s32[3]{0:T(128)S(1)} %pad_add_fusion.1.at_ref, bf16[6144,3072]{1,0:T(8,128)(2,1)} %bitcast.47, bf16[768,512]{1,0:T(8,128)(2,1)S(1)} %shard_map.80.factor_ref, bf16[768,512]{1,0:T(8,128)(2,1)S(1)} %shard_map.88.col_ref.refs_3_), custom_call_target="tpu_custom_call" | custom-call | flops 1 | bytes 1 | tf_op jit(solution)/shard_map/pallas_call | solution.py:36
  138.4 8.3 %collective-permute-done.30.refs_2_ = bf16[768,768]{1,0:T(8,128)(2,1)S(1)} collective-permute-done((bf16[768,768]{1,0:T(8,128)(2,1)S(1)}, bf16[768,768]{1,0:T(8,128)(2,1)S(1)}, u32[]{:S(2)}, u32[]{:S(2)}) %collective-permute-start.30) | collective-permute-done | bytes 1179680 | tf_op jit(solution)/shard_map/ppermute | solution.py:319
  147.9 2.5 shard_map.91.col_ref
  150.4 11.1 %shard_map.98 = bf16[576,2048]{1,0:T(8,128)(2,1)} custom-call(s32[3]{0:T(128)S(1)} %pad_add_fusion.1.at_ref, bf16[6144,3072]{1,0:T(8,128)(2,1)} %bitcast.48, bf16[768,512]{1,0:T(8,128)(2,1)S(1)} %get-tuple-element.88.factor_ref, bf16[3072,512]{1,0:T(8,128)(2,1)} %shard_map.91.col_ref), custom_call_target="tpu_custom_call" | custom-call | flops 1 | bytes 1 | tf_op jit(solution)/shard_map/pallas_call | solution.py:36
  165.6 6.5 %collective-permute-done.26.refs_3_ = bf16[768,768]{1,0:T(8,128)(2,1)} collective-permute-done((bf16[768,768]{1,0:T(8,128)(2,1)}, bf16[768,768]{1,0:T(8,128)(2,1)}, u32[]{:S(2)}, u32[]{:S(2)}) %collective-permute-start.26) | collective-permute-done | bytes 1179680 | tf_op jit(solution)/shard_map/ppermute | solution.py:319
  176.2 4.8 %shard_map.92 = bf16[192,3072]{1,0:T(8,128)(2,1)} custom-call(s32[3]{0:T(128)S(1)} %pad_add_fusion.1.at_ref, bf16[6144,3072]{1,0:T(8,128)(2,1)} %bitcast.49, bf16[576,512]{1,0:T(8,128)(2,1)S(1)} %collective-permute-done.28.factor_ref, bf16[3072,512]{1,0:T(8,128)(2,1)S(1)} %copy-done), custom_call_target="tpu_custom_call" | custom-call | flops 1 | bytes 1 | tf_op jit(solution)/shard_map/pallas_call | solution.py:36
  183.1 19.3 %collective-permute-done.32.refs_10_ = bf16[1536,512]{1,0:T(8,128)(2,1)S(1)} collective-permute-done((bf16[1536,512]{1,0:T(8,128)(2,1)S(1)}, bf16[1536,512]{1,0:T(8,128)(2,1)S(1)}, u32[]{:S(2)}, u32[]{:S(2)}) %collective-permute-start.32) | collective-permute-done | bytes 1572896 | tf_op jit(solution)/shard_map/ppermute | solution.py:493
  203.5 5.5 %shard_map.95.factor_ref = bf16[6144,512]{1,0:T(8,128)(2,1)} custom-call(s32[3]{0:T(128)S(1)} %pad_add_fusion.1.at_ref, bf16[768,512]{1,0:T(8,128)(2,1)S(1)} %copy-done.2, bf16[768,512]{1,0:T(8,128)(2,1)} %collective-permute-done.2.refs_1_, bf16[768,512]{1,0:T(8,128)(2,1)} %collective-permute-done.3.refs_2_, bf16[768,512]{1,0:T(8,128)(2,1)S(1)} %copy-done.6, ...), custom_call_target="tpu_custom_call" | custom-call | flops 1 | bytes 1 | tf_op jit(solution)/shard_map/pallas_call | solution.py:96
  209.1 13.5 %collective-permute-done.34.refs_1_ = bf16[576,2048]{1,0:T(8,128)(2,1)S(1)} collective-permute-done((bf16[576,2048]{1,0:T(8,128)(2,1)}, bf16[576,2048]{1,0:T(8,128)(2,1)S(1)}, u32[]{:S(2)}, u32[]{:S(2)}) %collective-permute-start.34) | collective-permute-done | bytes 2359328 | tf_op jit(solution)/shard_map/ppermute | solution.py:319
  222.6 5.3 %shard_map.99 = bf16[256,3072]{1,0:T(8,128)(2,1)} custom-call(s32[3]{0:T(128)S(1)} %pad_add_fusion.1.at_ref, bf16[6144,3072]{1,0:T(8,128)(2,1)} %bitcast.50, bf16[6144,512]{1,0:T(8,128)(2,1)} %shard_map.95.factor_ref, bf16[3072,512]{1,0:T(8,128)(2,1)S(1)} %copy-done), custom_call_target="tpu_custom_call" | custom-call | flops 1 | bytes 1 | tf_op jit(solution)/shard_map/pallas_call | solution.py:36
  233.9 4.3 %collective-permute-start.36 = (bf16[576,512]{1,0:T(8,128)(2,1)}, bf16[576,512]{1,0:T(8,128)(2,1)}, u32[]{:S(2)}, u32[]{:S(2)}) collective-permute-start(bf16[576,512]{1,0:T(8,128)(2,1)} %reshape.76.refs_0_), channel_id=1, source_target_pairs={{0,1},{1,2},{2,3},{4,5},{5,6},{6,7},{8,9},{9,10},{10,11},{12,13},{... | collective-permute-start | bytes 1769480 | tf_op jit(solution)/shard_map/ppermute | solution.py:248
  241.6 34.3 %shard_map.96.refs_4_ = f32[3072,3072]{1,0:T(8,128)} custom-call(s32[12]{0:T(128)S(1)} %iota.48.target_ref, s32[12]{0:T(128)S(1)} %get-tuple-element.148.own_ref, s32[12]{0:T(128)S(1)} %get-tuple-element.147.place_ref, bf16[6144,3072]{1,0:T(8,128)(2,1)} %bitcast.51, bf16[6144,512]{1,0:T(8,128)(2,1)} %shard_map.95.factor_ref, bf16[3072,512]{1,0:T(8,128)(2,1)S(1)} %copy-done, ...), custom_call_target="tpu_custom_call" | custom-call | flops 1 | bytes 1 | tf_op jit(solution)/shard_map/pallas_call | solution.py:125
  276.0 5.0 %shard_map.97 = bf16[256,3072]{1,0:T(8,128)(2,1)} custom-call(s32[3]{0:T(128)S(1)} %pad_add_fusion.1.at_ref, bf16[6144,3072]{1,0:T(8,128)(2,1)} %bitcast.52, bf16[6144,512]{1,0:T(8,128)(2,1)} %shard_map.95.factor_ref, bf16[3072,512]{1,0:T(8,128)(2,1)S(1)} %copy-done), custom_call_target="tpu_custom_call" | custom-call | flops 1 | bytes 1 | tf_op jit(solution)/shard_map/pallas_call | solution.py:36
  285.7 10.1 %shard_map.100.refs_2_ = f32[3072,3072]{1,0:T(8,128)} custom-call(s32[3]{0:T(128)S(1)} %get-tuple-element.145.target_ref, s32[5,12]{1,0:T(8,128)S(1)} %stack.50.place_ref, bf16[768,768]{1,0:T(8,128)(2,1)S(1)} %copy-done.17, bf16[768,768]{1,0:T(8,128)(2,1)S(1)} %copy-done.19, bf16[768,768]{1,0:T(8,128)(2,1)S(1)} %copy-done.21, ...), custom_call_target="tpu_custom_call", output_to_operand_aliasing={{}: (6, {})} | custom-call | flops 1 | bytes 1 | tf_op jit(solution)/shard_map/pallas_call | solution.py:167
  295.8 10.2 %shard_map.106 = bf16[576,2048]{1,0:T(8,128)(2,1)} custom-call(s32[3]{0:T(128)S(1)} %pad_add_fusion.1.at_ref, bf16[6144,3072]{1,0:T(8,128)(2,1)} %bitcast.53, bf16[6144,512]{1,0:T(8,128)(2,1)} %shard_map.95.factor_ref, bf16[3072,512]{1,0:T(8,128)(2,1)S(1)} %copy-done), custom_call_target="tpu_custom_call" | custom-call | flops 1 | bytes 1 | tf_op jit(solution)/shard_map/pallas_call | solution.py:36
  310.8 7.8 %collective-permute-done.33.refs_0_ = bf16[256,3072]{1,0:T(8,128)(2,1)} collective-permute-done((bf16[256,3072]{1,0:T(8,128)(2,1)}, bf16[256,3072]{1,0:T(8,128)(2,1)}, u32[]{:S(2)}, u32[]{:S(2)}) %collective-permute-start.33) | collective-permute-done | bytes 1572896 | tf_op jit(solution)/shard_map/ppermute | solution.py:319
  318.6 5.0 %shard_map.101 = bf16[256,3072]{1,0:T(8,128)(2,1)} custom-call(s32[3]{0:T(128)S(1)} %pad_add_fusion.1.at_ref, bf16[6144,3072]{1,0:T(8,128)(2,1)} %bitcast.54, bf16[6144,512]{1,0:T(8,128)(2,1)} %shard_map.95.factor_ref, bf16[3072,512]{1,0:T(8,128)(2,1)S(1)} %copy-done), custom_call_target="tpu_custom_call" | custom-call | flops 1 | bytes 1 | tf_op jit(solution)/shard_map/pallas_call | solution.py:36
  329.3 2.6 shard_map.103
  333.9 3.1 pad_maximum_fusion.front_ref
  342.6 8.8 %shard_map.105.refs_0_ = bf16[1152,1024]{1,0:T(8,128)(2,1)S(1)} custom-call(s32[3]{0:T(128)S(1)} %pad_add_fusion.1.at_ref, bf16[1152,1024]{1,0:T(8,128)(2,1)} %pad_maximum_fusion.front_ref, bf16[1152,512]{1,0:T(8,128)(2,1)S(1)} %shard_map.102.factor_ref, bf16[1024,512]{1,0:T(8,128)(2,1)S(1)} %shard_map.104.col_ref), custom_call_target="tpu_custom_call" | custom-call | flops 1 | bytes 1 | tf_op jit(solution)/shard_map/pallas_call | solution.py:36
  351.4 10.3 %shard_map.107.refs_1_ = f32[3072,3072]{1,0:T(8,128)} custom-call(s32[3]{0:T(128)S(1)} %get-tuple-element.143.target_ref, s32[3,12]{1,0:T(4,128)S(1)} %pad_add_fusion.place_ref, bf16[1152,1024]{1,0:T(8,128)(2,1)S(1)} %shard_map.105.refs_0_, bf16[576,2048]{1,0:T(8,128)(2,1)S(1)} %copy-done.15, ...), custom_call_target="tpu_custom_call", output_to_operand_aliasing={{}: (4, {})} | custom-call | flops 1 | bytes 1 | tf_op jit(solution)/shard_map/pallas_call | solution.py:167
  361.7 5.5 %shard_map.108.refs_1_ = f32[3072,3072]{1,0:T(8,128)} custom-call(s32[1]{0:T(128)} %bitcast.21.target_ref, s32[2,12]{1,0:T(2,128)S(1)} %stack.47.place_ref, bf16[192,3072]{1,0:T(8,128)(2,1)} %collective-permute-done.29.refs_0_, f32[3072,3072]{1,0:T(8,128)} %shard_map.107.refs_1_), custom_call_target="tpu_custom_call", output_to_operand_aliasing={{}: (3, {})} | custom-call | flops 1 | bytes 1 | tf_op jit(solution)/shard_map/pallas_call | solution.py:167
  367.2 4.9 %shard_map.109.refs_1_ = f32[3072,3072]{1,0:T(8,128)} custom-call(s32[1]{0:T(128)} %bitcast.20.target_ref, s32[2,12]{1,0:T(2,128)S(1)} %stack.47.place_ref, bf16[256,3072]{1,0:T(8,128)(2,1)} %collective-permute-done.35.refs_0_, f32[3072,3072]{1,0:T(8,128)} %shard_map.108.refs_1_), custom_call_target="tpu_custom_call", output_to_operand_aliasing={{}: (3, {})} | custom-call | flops 1 | bytes 1 | tf_op jit(solution)/shard_map/pallas_call | solution.py:167
  372.1 4.7 %shard_map.114 = bf16[128,3072]{1,0:T(8,128)(2,1)} custom-call(s32[3]{0:T(128)S(1)} %pad_add_fusion.1.at_ref, bf16[6144,3072]{1,0:T(8,128)(2,1)} %bitcast.55, bf16[6144,512]{1,0:T(8,128)(2,1)} %shard_map.95.factor_ref, bf16[3072,512]{1,0:T(8,128)(2,1)S(1)} %copy-done), custom_call_target="tpu_custom_call" | custom-call | flops 1 | bytes 1 | tf_op jit(solution)/shard_map/pallas_call | solution.py:36
  378.9 5.0 %shard_map.110.refs_2_ = f32[3072,3072]{1,0:T(8,128)} custom-call(s32[1]{0:T(128)} %bitcast.23.target_ref, s32[2,12]{1,0:T(2,128)S(1)} %stack.47.place_ref, bf16[256,3072]{1,0:T(8,128)(2,1)} %collective-permute-done.33.refs_0_, f32[3072,3072]{1,0:T(8,128)} %shard_map.109.refs_1_), custom_call_target="tpu_custom_call", output_to_operand_aliasing={{}: (3, {})} | custom-call | flops 1 | bytes 1 | tf_op jit(solution)/shard_map/pallas_call | solution.py:167
  383.8 10.7 %shard_map.111.base_ref = f32[3072,3072]{1,0:T(8,128)} custom-call(s32[3]{0:T(128)S(1)} %get-tuple-element.144.target_ref, s32[3,12]{1,0:T(4,128)S(1)} %pad_add_fusion.place_ref, bf16[1152,1024]{1,0:T(8,128)(2,1)S(1)} %shard_map.105.refs_0_, bf16[576,2048]{1,0:T(8,128)(2,1)} %collective-permute-done.44.refs_1_, ...), custom_call_target="tpu_custom_call", output_to_operand_aliasing={{}: (4, {})} | custom-call | flops 1 | bytes 1 | tf_op jit(solution)/shard_map/pallas_call | solution.py:167
  394.6 8.3 %collective-permute-done.38.piece_ref = bf16[256,3072]{1,0:T(8,128)(2,1)} collective-permute-done((bf16[256,3072]{1,0:T(8,128)(2,1)}, bf16[256,3072]{1,0:T(8,128)(2,1)}, u32[]{:S(2)}, u32[]{:S(2)}) %collective-permute-start.38) | collective-permute-done | bytes 1572896 | tf_op jit(solution)/shard_map/ppermute | solution.py:319
  402.8 3.5 shard_map.112
  406.6 2.6 maximum_bitcast_fusion
  409.3 6.8 %shard_map.113 = (f32[3072,3072]{1,0:T(8,128)}, f32[64,3072]{1,0:T(8,128)S(1)}) custom-call(s32[2]{0:T(128)S(1)} %fusion.22.target_ref, s32[2,12]{1,0:T(2,128)S(1)} %stack.47.place_ref, bf16[256,3072]{1,0:T(8,128)(2,1)} %collective-permute-done.38.piece_ref, f32[3072,3072]{1,0:T(8,128)} %shard_map.111.base_ref), custom_call_target="tpu_custom_call", output_to_operand_aliasing={{0}: (3, {})} | custom-call | flops 1 | bytes 1 | tf_op jit(solution)/shard_map/pallas_call | solution.py:198
  416.1 3.5 collective-permute-done.46.refs_0_
  419.7 4.2 shard_map.115.base_ref
  (191 shorter events, 92.8 us)
Async XLA Ops:
  2.5 21.4 %collective-permute-start.4 = (bf16[384,1024]{1,0:T(8,128)(2,1)S(1)}, bf16[384,1024]{1,0:T(8,128)(2,1)S(1)}, u32[]{:S(2)}, u32[]{:S(2)}) collective-permute-start(bf16[384,1024]{1,0:T(8,128)(2,1)S(1)} %shard_map.77), channel_id=1, source_target_pairs={{0,8},{8,0},{16,24},{24,16},{1,9},{9,1},{17,25},{25,17},{2,10},{10... | collective-permute-start | bytes 2359304 | tf_op jit(solution)/shard_map/ppermute | solution.py:319
  7.5 20.0 %collective-permute-start.2 = (bf16[768,512]{1,0:T(8,128)(2,1)S(1)}, bf16[768,512]{1,0:T(8,128)(2,1)}, u32[]{:S(2)}, u32[]{:S(2)}) collective-permute-start(bf16[768,512]{1,0:T(8,128)(2,1)S(1)} %convolution_convert_fusion.1.refs_0_), channel_id=1, source_target_pairs={{0,1},{1,2},{2,3},{4,5},{5,6},{6,7},{8,9},{9,10},{10,11},{12,13},{... | collective-permute-start | bytes 2359304 | tf_op jit(solution)/shard_map/ppermute | solution.py:248
  11.9 20.7 %collective-permute-start.3 = (bf16[768,512]{1,0:T(8,128)(2,1)S(1)}, bf16[768,512]{1,0:T(8,128)(2,1)}, u32[]{:S(2)}, u32[]{:S(2)}) collective-permute-start(bf16[768,512]{1,0:T(8,128)(2,1)S(1)} %convolution_convert_fusion.1.refs_0_), channel_id=1, source_target_pairs={{1,0},{2,1},{3,2},{5,4},{6,5},{7,6},{9,8},{10,9},{11,10},{13,12},{... | collective-permute-start | bytes 2359304 | tf_op jit(solution)/shard_map/ppermute | solution.py:248
  15.8 33.4 %collective-permute-start.1 = (bf16[576,1024]{1,0:T(8,128)(2,1)}, bf16[576,1024]{1,0:T(8,128)(2,1)}, u32[]{:S(2)}, u32[]{:S(2)}) collective-permute-start(bf16[576,1024]{1,0:T(8,128)(2,1)} %shard_map.79), channel_id=1, source_target_pairs={{0,8},{8,0},{16,24},{24,16},{1,9},{9,1},{17,25},{25,17},{2,10},{10... | collective-permute-start | bytes 3538952 | tf_op jit(solution)/shard_map/ppermute | solution.py:319
  23.9 10.3 %collective-permute-start.5 = (s32[48]{0:T(128)S(1)}, s32[48]{0:T(128)S(1)}, u32[]{:S(2)}, u32[]{:S(2)}) collective-permute-start(s32[48]{0:T(128)S(1)} %bitcast.63), channel_id=1, source_target_pairs={{0,4},{4,0},{1,5},{5,1},{2,6},{6,2},{3,7},{7,3},{8,12},{12,8},{9,1... | collective-permute-start | bytes 584 | tf_op jit(solution)/shard_map/ppermute | solution.py:257
  34.1 16.3 %collective-permute-start.9 = (bf16[768,512]{1,0:T(8,128)(2,1)}, bf16[768,512]{1,0:T(8,128)(2,1)}, u32[]{:S(2)}, u32[]{:S(2)}) collective-permute-start(bf16[768,512]{1,0:T(8,128)(2,1)} %shard_map.81.refs_0_), channel_id=1, source_target_pairs={{0,4},{4,0},{1,5},{5,1},{2,6},{6,2},{3,7},{7,3},{8,12},{12,8},{9,1... | collective-permute-start | bytes 2359304 | tf_op jit(solution)/shard_map/ppermute | solution.py:257
  34.2 17.9 %collective-permute-start.7 = (bf16[768,512]{1,0:T(8,128)(2,1)}, bf16[768,512]{1,0:T(8,128)(2,1)S(1)}, u32[]{:S(2)}, u32[]{:S(2)}) collective-permute-start(bf16[768,512]{1,0:T(8,128)(2,1)} %collective-permute-done.2.refs_1_), channel_id=1, source_target_pairs={{1,2},{2,3},{5,6},{6,7},{9,10},{10,11},{13,14},{14,15},{17,18},{18... | collective-permute-start | bytes 2359304 | tf_op jit(solution)/shard_map/ppermute | solution.py:248
  34.9 24.6 %collective-permute-start.8 = (bf16[768,512]{1,0:T(8,128)(2,1)}, bf16[768,512]{1,0:T(8,128)(2,1)S(1)}, u32[]{:S(2)}, u32[]{:S(2)}) collective-permute-start(bf16[768,512]{1,0:T(8,128)(2,1)} %collective-permute-done.3.refs_2_), channel_id=1, source_target_pairs={{1,0},{2,1},{5,4},{6,5},{9,8},{10,9},{13,12},{14,13},{17,16},{18,1... | collective-permute-start | bytes 2359304 | tf_op jit(solution)/shard_map/ppermute | solution.py:248
  36.9 91.4 %copy-start.3 = (bf16[768,512]{1,0:T(8,128)(2,1)}, bf16[768,512]{1,0:T(8,128)(2,1)S(1)}, u32[]{:S(2)}) copy-start(bf16[768,512]{1,0:T(8,128)(2,1)S(1)} %convolution_convert_fusion.refs_0_.refs_5_) | copy-start | bytes 2359300
  41.1 29.8 %collective-permute-start = (bf16[496,1024]{1,0:T(8,128)(2,1)S(1)}, bf16[496,1024]{1,0:T(8,128)(2,1)S(1)}, u32[]{:S(2)}, u32[]{:S(2)}) collective-permute-start(bf16[496,1024]{1,0:T(8,128)(2,1)S(1)} %pad_maximum_fusion.1), channel_id=1, source_target_pairs={{0,8},{8,0},{16,24},{24,16},{1,9},{9,1},{17,25},{25,17},{2,10},{10... | collective-permute-start | bytes 3047432 | tf_op jit(solution)/shard_map/ppermute | solution.py:319
  49.3 1.1 collective-permute-start.6
  65.7 5.2 %collective-permute-start.10 = (bf16[768,512]{1,0:T(8,128)(2,1)S(1)}, bf16[768,512]{1,0:T(8,128)(2,1)S(1)}, u32[]{:S(2)}, u32[]{:S(2)}) collective-permute-start(bf16[768,512]{1,0:T(8,128)(2,1)S(1)} %shard_map.84.refs_0_), channel_id=1, source_target_pairs={{0,4},{4,0},{1,5},{5,1},{2,6},{6,2},{3,7},{7,3},{8,12},{12,8},{9,1... | collective-permute-start | bytes 2359304 | tf_op jit(solution)/shard_map/ppermute | solution.py:257
  65.8 5.8 %collective-permute-start.12 = (bf16[768,512]{1,0:T(8,128)(2,1)S(1)}, bf16[768,512]{1,0:T(8,128)(2,1)S(1)}, u32[]{:S(2)}, u32[]{:S(2)}) collective-permute-start(bf16[768,512]{1,0:T(8,128)(2,1)S(1)} %convolution_convert_fusion.refs_0_.refs_5_), channel_id=1, source_target_pairs={{0,4},{4,0},{1,5},{5,1},{2,6},{6,2},{3,7},{7,3},{8,12},{12,8},{9,1... | collective-permute-start | bytes 2359304 | tf_op jit(solution)/shard_map/ppermute | solution.py:257
  66.3 29.9 %collective-permute-start.16 = (bf16[768,768]{1,0:T(8,128)(2,1)S(1)}, bf16[768,768]{1,0:T(8,128)(2,1)S(1)}, u32[]{:S(2)}, u32[]{:S(2)}) collective-permute-start(bf16[768,768]{1,0:T(8,128)(2,1)S(1)} %shard_map.83), channel_id=1, source_target_pairs={{0,8},{8,0},{16,24},{24,16},{1,9},{9,1},{17,25},{25,17},{2,10},{10... | collective-permute-start | bytes 3538952 | tf_op jit(solution)/shard_map/ppermute | solution.py:319
  70.9 1.1 collective-permute-start.11
  72.0 26.4 %collective-permute-start.13 = (bf16[768,512]{1,0:T(8,128)(2,1)S(1)}, bf16[768,512]{1,0:T(8,128)(2,1)S(1)}, u32[]{:S(2)}, u32[]{:S(2)}) collective-permute-start(bf16[768,512]{1,0:T(8,128)(2,1)S(1)} %convolution_convert_fusion.refs_0_.refs_5_), channel_id=1, source_target_pairs={{0,1},{1,2},{2,3},{4,5},{5,6},{6,7},{8,9},{9,10},{10,11},{12,13},{... | collective-permute-start | bytes 2359304 | tf_op jit(solution)/shard_map/ppermute | solution.py:248
  75.9 22.5 %collective-permute-start.14 = (bf16[768,512]{1,0:T(8,128)(2,1)S(1)}, bf16[768,512]{1,0:T(8,128)(2,1)S(1)}, u32[]{:S(2)}, u32[]{:S(2)}) collective-permute-start(bf16[768,512]{1,0:T(8,128)(2,1)S(1)} %convolution_convert_fusion.refs_0_.refs_5_), channel_id=1, source_target_pairs={{1,0},{2,1},{3,2},{5,4},{6,5},{7,6},{9,8},{10,9},{11,10},{13,12},{... | collective-permute-start | bytes 2359304 | tf_op jit(solution)/shard_map/ppermute | solution.py:248
  77.2 21.2 %collective-permute-start.15 = (bf16[768,512]{1,0:T(8,128)(2,1)S(1)}, bf16[768,512]{1,0:T(8,128)(2,1)S(1)}, u32[]{:S(2)}, u32[]{:S(2)}) collective-permute-start(bf16[768,512]{1,0:T(8,128)(2,1)S(1)} %convolution_convert_fusion.refs_0_.refs_5_), channel_id=1, source_target_pairs={{2,5},{5,2},{10,13},{13,10},{18,21},{21,18},{26,29},{29,26}} | collective-permute-start | bytes 2359304 | tf_op jit(solution)/shard_map/ppermute | solution.py:444
  81.8 39.7 %collective-permute-start.21 = (bf16[768,768]{1,0:T(8,128)(2,1)S(1)}, bf16[768,768]{1,0:T(8,128)(2,1)S(1)}, u32[]{:S(2)}, u32[]{:S(2)}) collective-permute-start(bf16[768,768]{1,0:T(8,128)(2,1)S(1)} %shard_map.87), channel_id=1, source_target_pairs={{0,8},{8,0},{16,24},{24,16},{1,9},{9,1},{17,25},{25,17},{2,10},{10... | collective-permute-start | bytes 3538952 | tf_op jit(solution)/shard_map/ppermute | solution.py:319
  96.2 1.1 collective-permute-start.17
  97.3 1.1 collective-permute-start.18
  98.5 25.5 %collective-permute-start.19 = (bf16[768,512]{1,0:T(8,128)(2,1)S(1)}, bf16[768,512]{1,0:T(8,128)(2,1)S(1)}, u32[]{:S(2)}, u32[]{:S(2)}) collective-permute-start(bf16[768,512]{1,0:T(8,128)(2,1)S(1)} %collective-permute-done.13.refs_1_.refs_6_), channel_id=1, source_target_pairs={{1,2},{2,3},{5,6},{6,7},{9,10},{10,11},{13,14},{14,15},{17,18},{18... | collective-permute-start | bytes 2359304 | tf_op jit(solution)/shard_map/ppermute | solution.py:248
  99.2 29.1 %collective-permute-start.20 = (bf16[768,512]{1,0:T(8,128)(2,1)S(1)}, bf16[768,512]{1,0:T(8,128)(2,1)S(1)}, u32[]{:S(2)}, u32[]{:S(2)}) collective-permute-start(bf16[768,512]{1,0:T(8,128)(2,1)S(1)} %collective-permute-done.14.refs_2_.refs_7_), channel_id=1, source_target_pairs={{1,0},{2,1},{5,4},{6,5},{9,8},{10,9},{13,12},{14,13},{17,16},{18,1... | collective-permute-start | bytes 2359304 | tf_op jit(solution)/shard_map/ppermute | solution.py:248
  105.0 41.8 %collective-permute-start.30 = (bf16[768,768]{1,0:T(8,128)(2,1)S(1)}, bf16[768,768]{1,0:T(8,128)(2,1)S(1)}, u32[]{:S(2)}, u32[]{:S(2)}) collective-permute-start(bf16[768,768]{1,0:T(8,128)(2,1)S(1)} %shard_map.93), channel_id=1, source_target_pairs={{0,8},{8,0},{16,24},{24,16},{1,9},{9,1},{17,25},{25,17},{2,10},{10... | collective-permute-start | bytes 3538952 | tf_op jit(solution)/shard_map/ppermute | solution.py:319
  121.5 1.1 collective-permute-start.22
  122.6 1.1 collective-permute-start.23
  123.7 5.3 %collective-permute-start.24 = (s32[48]{0:T(128)S(1)}, s32[48]{0:T(128)S(1)}, u32[]{:S(2)}, u32[]{:S(2)}) collective-permute-start(s32[48]{0:T(128)S(1)} %collective-permute-done.23), channel_id=1, source_target_pairs={{0,4},{4,0},{1,5},{5,1},{2,6},{6,2},{3,7},{7,3},{8,12},{12,8},{9,1... | collective-permute-start | bytes 584 | tf_op jit(solution)/shard_map/ppermute | solution.py:257
  129.0 2.4 collective-permute-start.25
  136.8 35.4 %collective-permute-start.26 = (bf16[768,768]{1,0:T(8,128)(2,1)}, bf16[768,768]{1,0:T(8,128)(2,1)}, u32[]{:S(2)}, u32[]{:S(2)}) collective-permute-start(bf16[768,768]{1,0:T(8,128)(2,1)} %shard_map.89), channel_id=1, source_target_pairs={{0,8},{8,0},{16,24},{24,16},{1,9},{9,1},{17,25},{25,17},{2,10},{10... | collective-permute-start | bytes 3538952 | tf_op jit(solution)/shard_map/ppermute | solution.py:319
  146.8 1.1 collective-permute-start.31
  161.5 61.1 %collective-permute-start.34 = (bf16[576,2048]{1,0:T(8,128)(2,1)}, bf16[576,2048]{1,0:T(8,128)(2,1)S(1)}, u32[]{:S(2)}, u32[]{:S(2)}) collective-permute-start(bf16[576,2048]{1,0:T(8,128)(2,1)} %shard_map.98), channel_id=1, source_target_pairs={{0,8},{8,0},{16,24},{24,16},{1,9},{9,1},{17,25},{25,17},{2,10},{10... | collective-permute-start | bytes 7077896 | tf_op jit(solution)/shard_map/ppermute | solution.py:319
  164.3 38.1 %collective-permute-start.32 = (bf16[1536,512]{1,0:T(8,128)(2,1)S(1)}, bf16[1536,512]{1,0:T(8,128)(2,1)S(1)}, u32[]{:S(2)}, u32[]{:S(2)}) collective-permute-start(bf16[1536,512]{1,0:T(8,128)(2,1)S(1)} %shard_map.94), channel_id=1, source_target_pairs={{2,3},{1,0},{6,7},{5,4},{10,11},{9,8},{14,15},{13,12},{18,19},{17,... | collective-permute-start | bytes 4718600 | tf_op jit(solution)/shard_map/ppermute | solution.py:493
  172.1 2.0 collective-permute-start.27
  174.1 2.0 collective-permute-start.28
  181.0 94.9 %collective-permute-start.29 = (bf16[192,3072]{1,0:T(8,128)(2,1)}, bf16[192,3072]{1,0:T(8,128)(2,1)}, u32[]{:S(2)}, u32[]{:S(2)}) collective-permute-start(bf16[192,3072]{1,0:T(8,128)(2,1)} %shard_map.92), channel_id=1, source_target_pairs={{0,8},{8,0},{16,24},{24,16},{1,9},{9,1},{17,25},{25,17},{2,10},{10... | collective-permute-start | bytes 3538952 | tf_op jit(solution)/shard_map/ppermute | solution.py:319
  227.9 67.9 %collective-permute-start.35 = (bf16[256,3072]{1,0:T(8,128)(2,1)}, bf16[256,3072]{1,0:T(8,128)(2,1)}, u32[]{:S(2)}, u32[]{:S(2)}) collective-permute-start(bf16[256,3072]{1,0:T(8,128)(2,1)} %shard_map.99), channel_id=1, source_target_pairs={{0,8},{8,0},{16,24},{24,16},{1,9},{9,1},{17,25},{25,17},{2,10},{10... | collective-permute-start | bytes 4718600 | tf_op jit(solution)/shard_map/ppermute | solution.py:319
  233.9 48.0 %collective-permute-start.36 = (bf16[576,512]{1,0:T(8,128)(2,1)}, bf16[576,512]{1,0:T(8,128)(2,1)}, u32[]{:S(2)}, u32[]{:S(2)}) collective-permute-start(bf16[576,512]{1,0:T(8,128)(2,1)} %reshape.76.refs_0_), channel_id=1, source_target_pairs={{0,1},{1,2},{2,3},{4,5},{5,6},{6,7},{8,9},{9,10},{10,11},{12,13},{... | collective-permute-start | bytes 1769480 | tf_op jit(solution)/shard_map/ppermute | solution.py:248
  238.2 43.6 %collective-permute-start.37 = (bf16[576,512]{1,0:T(8,128)(2,1)}, bf16[576,512]{1,0:T(8,128)(2,1)}, u32[]{:S(2)}, u32[]{:S(2)}) collective-permute-start(bf16[576,512]{1,0:T(8,128)(2,1)} %reshape.76.refs_0_), channel_id=1, source_target_pairs={{1,0},{2,1},{3,2},{5,4},{6,5},{7,6},{9,8},{10,9},{11,10},{13,12},{... | collective-permute-start | bytes 1769480 | tf_op jit(solution)/shard_map/ppermute | solution.py:248
  280.9 37.6 %collective-permute-start.33 = (bf16[256,3072]{1,0:T(8,128)(2,1)}, bf16[256,3072]{1,0:T(8,128)(2,1)}, u32[]{:S(2)}, u32[]{:S(2)}) collective-permute-start(bf16[256,3072]{1,0:T(8,128)(2,1)} %shard_map.97), channel_id=1, source_target_pairs={{0,8},{8,0},{16,24},{24,16},{1,9},{9,1},{17,25},{25,17},{2,10},{10... | collective-permute-start | bytes 4718600 | tf_op jit(solution)/shard_map/ppermute | solution.py:319
  306.0 66.0 %collective-permute-start.44 = (bf16[576,2048]{1,0:T(8,128)(2,1)}, bf16[576,2048]{1,0:T(8,128)(2,1)}, u32[]{:S(2)}, u32[]{:S(2)}) collective-permute-start(bf16[576,2048]{1,0:T(8,128)(2,1)} %shard_map.106), channel_id=1, source_target_pairs={{0,8},{8,0},{16,24},{24,16},{1,9},{9,1},{17,25},{25,17},{2,10},{10... | collective-permute-start | bytes 7077896 | tf_op jit(solution)/shard_map/ppermute | solution.py:319
  307.8 15.9 %collective-permute-start.39 = (bf16[576,512]{1,0:T(8,128)(2,1)}, bf16[576,512]{1,0:T(8,128)(2,1)}, u32[]{:S(2)}, u32[]{:S(2)}) collective-permute-start(bf16[576,512]{1,0:T(8,128)(2,1)} %collective-permute-done.36.refs_1_), channel_id=1, source_target_pairs={{1,2},{2,3},{5,6},{6,7},{9,10},{10,11},{13,14},{14,15},{17,18},{18... | collective-permute-start | bytes 1769480 | tf_op jit(solution)/shard_map/ppermute | solution.py:248
  309.5 16.4 %collective-permute-start.40 = (bf16[576,512]{1,0:T(8,128)(2,1)}, bf16[576,512]{1,0:T(8,128)(2,1)}, u32[]{:S(2)}, u32[]{:S(2)}) collective-permute-start(bf16[576,512]{1,0:T(8,128)(2,1)} %collective-permute-done.37.refs_2_), channel_id=1, source_target_pairs={{1,0},{2,1},{5,4},{6,5},{9,8},{10,9},{13,12},{14,13},{17,16},{18,1... | collective-permute-start | bytes 1769480 | tf_op jit(solution)/shard_map/ppermute | solution.py:248
  323.5 79.3 %collective-permute-start.38 = (bf16[256,3072]{1,0:T(8,128)(2,1)}, bf16[256,3072]{1,0:T(8,128)(2,1)}, u32[]{:S(2)}, u32[]{:S(2)}) collective-permute-start(bf16[256,3072]{1,0:T(8,128)(2,1)} %shard_map.101), channel_id=1, source_target_pairs={{0,8},{8,0},{16,24},{24,16},{1,9},{9,1},{17,25},{25,17},{2,10},{10... | collective-permute-start | bytes 4718600 | tf_op jit(solution)/shard_map/ppermute | solution.py:319
  327.8 13.0 %collective-permute-start.41 = (bf16[576,512]{1,0:T(8,128)(2,1)}, bf16[576,512]{1,0:T(8,128)(2,1)}, u32[]{:S(2)}, u32[]{:S(2)}) collective-permute-start(bf16[576,512]{1,0:T(8,128)(2,1)} %broadcast_select_fusion), channel_id=1, source_target_pairs={{2,3},{1,0},{6,7},{5,4},{10,11},{9,8},{14,15},{13,12},{18,19},{17,... | collective-permute-start | bytes 1769480 | tf_op jit(solution)/shard_map/ppermute | solution.py:513
  331.9 5.1 %collective-permute-start.42 = (bf16[512,512]{1,0:T(8,128)(2,1)}, bf16[512,512]{1,0:T(8,128)(2,1)}, u32[]{:S(2)}, u32[]{:S(2)}) collective-permute-start(bf16[512,512]{1,0:T(8,128)(2,1)} %get-tuple-element.112.refs_0_), channel_id=1, source_target_pairs={{0,4},{4,0},{1,5},{5,1},{2,6},{6,2},{3,7},{7,3},{8,12},{12,8},{9,1... | collective-permute-start | bytes 1572872 | tf_op jit(solution)/shard_map/ppermute | solution.py:257
  332.0 5.0 %collective-permute-start.43 = (bf16[512,512]{1,0:T(8,128)(2,1)}, bf16[512,512]{1,0:T(8,128)(2,1)}, u32[]{:S(2)}, u32[]{:S(2)}) collective-permute-start(bf16[512,512]{1,0:T(8,128)(2,1)} %get-tuple-element.113.refs_1_), channel_id=1, source_target_pairs={{0,4},{4,0},{1,5},{5,1},{2,6},{6,2},{3,7},{7,3},{8,12},{12,8},{9,1... | collective-permute-start | bytes 1572872 | tf_op jit(solution)/shard_map/ppermute | solution.py:257
  376.8 42.9 %collective-permute-start.46 = (bf16[128,3072]{1,0:T(8,128)(2,1)}, bf16[128,3072]{1,0:T(8,128)(2,1)}, u32[]{:S(2)}, u32[]{:S(2)}) collective-permute-start(bf16[128,3072]{1,0:T(8,128)(2,1)} %shard_map.114), channel_id=1, source_target_pairs={{0,8},{8,0},{16,24},{24,16},{1,9},{9,1},{17,25},{25,17},{2,10},{10... | collective-permute-start | bytes 2359304 | tf_op jit(solution)/shard_map/ppermute | solution.py:319
  406.4 17.8 %collective-permute-start.45 = (bf16[64,3072]{1,0:T(8,128)(2,1)S(1)}, bf16[64,3072]{1,0:T(8,128)(2,1)S(1)}, u32[]{:S(2)}, u32[]{:S(2)}) collective-permute-start(bf16[64,3072]{1,0:T(8,128)(2,1)S(1)} %shard_map.112), channel_id=1, source_target_pairs={{0,8},{8,0},{16,24},{24,16},{1,9},{9,1},{17,25},{25,17},{2,10},{10... | collective-permute-start | bytes 1179656 | tf_op jit(solution)/shard_map/ppermute | solution.py:319
  (34 other events, 465.0 us)

commit v5 on v4

--- a/solution.py
+++ b/solution.py
@@ -11,7 +11,7 @@
 NT = (((1,), (1,)), ((), ()))
 VMEM_LIMIT = 48 * 1024 * 1024
 STEP = 128
-MAP_ROWS = 16
+MAP_ROWS = 8
 
 
 def block_inverse(mapping):

time: 429 us -> 429 us (level)
  no operation moved by 1% of the time
where the time goes in v5:
time: 429 us; the launch traced here: 426 us
  Pallas kernels  198 us (46%)
  waiting for transfers between devices  149 us (35%)
  starting transfers between devices  50.3 us (12%)
  local copies, waits for them, and re-layouts  12.9 us (3%)
  other arithmetic  12.5 us (3%)
    ppermute x15, waiting for transfers between devices, from_sibling(): return lax.ppermute(block, 'front', route)  91.9 us
    pallas_call x13, Pallas kernels, updated_rows(): pl.pallas_call(functools.partial(update_kernel, unit, col_unit), grid_spe...  74.6 us
    pallas_call x7, Pallas kernels, add_rows(): pl.pallas_call(functools.partial(add_kernel, cols // BLK, len(pieces)), g...  50.7 us
    pallas_call x1, Pallas kernels, kept_rows(): pl.pallas_call(functools.partial(base_kernel, cols // BLK), grid_spec=plt...  34.4 us
    pallas_call x14, Pallas kernels, assembled(): pl.pallas_call(functools.partial(assemble_kernel, plan, len(sources)), gr...  22.9 us
    ppermute x15, starting transfers between devices, from_sibling(): return lax.ppermute(block, 'front', route)  21.1 us
    ppermute x1, waiting for transfers between devices, shards(): far = lax.ppermute(last_hop, 'col', FAR)  19.3 us
    ppermute x6, waiting for transfers between devices, hop(): lax.ppermute(down_block, 'col', down)  19.1 us
  transfers between devices with their start and end apart: 47, of which 29 were waited for; matrix products, arithmetic and copies ran while one was open for 5% of the time, Pallas kernels for 45%

profile of v5, /device:TPU:0, one launch (start us, length us, event | category | flops | bytes accessed | tf_op | source)
XLA Modules:
  0.0 426.1 jit_solution(14559855122981262428)
XLA Ops:
  2.5 3.0 collective-permute-start.4
  7.5 4.4 %collective-permute-start.2 = (bf16[768,512]{1,0:T(8,128)(2,1)S(1)}, bf16[768,512]{1,0:T(8,128)(2,1)}, u32[]{:S(2)}, u32[]{:S(2)}) collective-permute-start(bf16[768,512]{1,0:T(8,128)(2,1)S(1)} %convolution_convert_fusion.1.refs_0_), channel_id=1, source_target_pairs={{0,1},{1,2},{2,3},{4,5},{5,6},{6,7},{8,9},{9,10},{10,11},{12,13},{... | collective-permute-start | bytes 2359304 | tf_op jit(solution)/shard_map/ppermute | solution.py:248
  13.1 2.7 shard_map.79
  18.0 5.8 %collective-permute-done.4 = bf16[384,1024]{1,0:T(8,128)(2,1)S(1)} collective-permute-done((bf16[384,1024]{1,0:T(8,128)(2,1)S(1)}, bf16[384,1024]{1,0:T(8,128)(2,1)S(1)}, u32[]{:S(2)}, u32[]{:S(2)}) %collective-permute-start.4) | collective-permute-done | bytes 786464 | tf_op jit(solution)/shard_map/ppermute | solution.py:319
  23.9 3.6 collective-permute-done.2.refs_1_
  27.5 5.1 %collective-permute-done.3.refs_2_ = bf16[768,512]{1,0:T(8,128)(2,1)} collective-permute-done((bf16[768,512]{1,0:T(8,128)(2,1)S(1)}, bf16[768,512]{1,0:T(8,128)(2,1)}, u32[]{:S(2)}, u32[]{:S(2)}) %collective-permute-start.3) | collective-permute-done | bytes 786464 | tf_op jit(solution)/shard_map/ppermute | solution.py:248
  41.7 7.6 %collective-permute-done.1 = bf16[576,1024]{1,0:T(8,128)(2,1)} collective-permute-done((bf16[576,1024]{1,0:T(8,128)(2,1)}, bf16[576,1024]{1,0:T(8,128)(2,1)}, u32[]{:S(2)}, u32[]{:S(2)}) %collective-permute-start.1) | collective-permute-done | bytes 1179680 | tf_op jit(solution)/shard_map/ppermute | solution.py:319
  52.1 7.4 %collective-permute-done.8.refs_4_.refs_1_ = bf16[768,512]{1,0:T(8,128)(2,1)S(1)} collective-permute-done((bf16[768,512]{1,0:T(8,128)(2,1)}, bf16[768,512]{1,0:T(8,128)(2,1)S(1)}, u32[]{:S(2)}, u32[]{:S(2)}) %collective-permute-start.8) | collective-permute-done | bytes 786464 | tf_op jit(solution)/shard_map/ppermute | solution.py:248
  60.1 3.8 shard_map.83
  67.9 2.6 collective-permute-done
  71.6 3.9 collective-permute-start.13
  77.5 3.8 shard_map.87
  83.2 12.6 %collective-permute-done.16.refs_0_ = bf16[768,768]{1,0:T(8,128)(2,1)S(1)} collective-permute-done((bf16[768,768]{1,0:T(8,128)(2,1)S(1)}, bf16[768,768]{1,0:T(8,128)(2,1)S(1)}, u32[]{:S(2)}, u32[]{:S(2)}) %collective-permute-start.16) | collective-permute-done | bytes 1179680 | tf_op jit(solution)/shard_map/ppermute | solution.py:319
  100.7 3.8 shard_map.93
  106.5 14.6 %collective-permute-done.21.refs_1_ = bf16[768,768]{1,0:T(8,128)(2,1)S(1)} collective-permute-done((bf16[768,768]{1,0:T(8,128)(2,1)S(1)}, bf16[768,768]{1,0:T(8,128)(2,1)S(1)}, u32[]{:S(2)}, u32[]{:S(2)}) %collective-permute-start.21) | collective-permute-done | bytes 1179680 | tf_op jit(solution)/shard_map/ppermute | solution.py:319
  123.5 4.4 %collective-permute-done.20.refs_4_.refs_3_.refs_9_ = bf16[768,512]{1,0:T(8,128)(2,1)S(1)} collective-permute-done((bf16[768,512]{1,0:T(8,128)(2,1)S(1)}, bf16[768,512]{1,0:T(8,128)(2,1)S(1)}, u32[]{:S(2)}, u32[]{:S(2)}) %collective-permute-start.20) | collective-permute-done | bytes 786464 | tf_op jit(solution)/shard_map/ppermute | solution.py:248
  131.7 4.8 %shard_map.89 = bf16[768,768]{1,0:T(8,128)(2,1)} custom-call(s32[3]{0:T(128)S(1)} %pad_add_fusion.1.at_ref, bf16[6144,3072]{1,0:T(8,128)(2,1)} %bitcast.47, bf16[768,512]{1,0:T(8,128)(2,1)S(1)} %shard_map.80.factor_ref, bf16[768,512]{1,0:T(8,128)(2,1)S(1)} %shard_map.88.col_ref.refs_3_), custom_call_target="tpu_custom_call" | custom-call | flops 1 | bytes 1 | tf_op jit(solution)/shard_map/pallas_call | solution.py:36
  138.1 8.2 %collective-permute-done.30.refs_2_ = bf16[768,768]{1,0:T(8,128)(2,1)S(1)} collective-permute-done((bf16[768,768]{1,0:T(8,128)(2,1)S(1)}, bf16[768,768]{1,0:T(8,128)(2,1)S(1)}, u32[]{:S(2)}, u32[]{:S(2)}) %collective-permute-start.30) | collective-permute-done | bytes 1179680 | tf_op jit(solution)/shard_map/ppermute | solution.py:319
  147.4 2.5 shard_map.91.col_ref
  150.0 11.1 %shard_map.98 = bf16[576,2048]{1,0:T(8,128)(2,1)} custom-call(s32[3]{0:T(128)S(1)} %pad_add_fusion.1.at_ref, bf16[6144,3072]{1,0:T(8,128)(2,1)} %bitcast.48, bf16[768,512]{1,0:T(8,128)(2,1)S(1)} %get-tuple-element.88.factor_ref, bf16[3072,512]{1,0:T(8,128)(2,1)} %shard_map.91.col_ref), custom_call_target="tpu_custom_call" | custom-call | flops 1 | bytes 1 | tf_op jit(solution)/shard_map/pallas_call | solution.py:36
  165.0 6.7 %collective-permute-done.26.refs_3_ = bf16[768,768]{1,0:T(8,128)(2,1)} collective-permute-done((bf16[768,768]{1,0:T(8,128)(2,1)}, bf16[768,768]{1,0:T(8,128)(2,1)}, u32[]{:S(2)}, u32[]{:S(2)}) %collective-permute-start.26) | collective-permute-done | bytes 1179680 | tf_op jit(solution)/shard_map/ppermute | solution.py:319
  175.7 4.8 %shard_map.92 = bf16[192,3072]{1,0:T(8,128)(2,1)} custom-call(s32[3]{0:T(128)S(1)} %pad_add_fusion.1.at_ref, bf16[6144,3072]{1,0:T(8,128)(2,1)} %bitcast.49, bf16[576,512]{1,0:T(8,128)(2,1)S(1)} %collective-permute-done.28.factor_ref, bf16[3072,512]{1,0:T(8,128)(2,1)S(1)} %copy-done), custom_call_target="tpu_custom_call" | custom-call | flops 1 | bytes 1 | tf_op jit(solution)/shard_map/pallas_call | solution.py:36
  182.4 19.3 %collective-permute-done.32.refs_10_ = bf16[1536,512]{1,0:T(8,128)(2,1)S(1)} collective-permute-done((bf16[1536,512]{1,0:T(8,128)(2,1)S(1)}, bf16[1536,512]{1,0:T(8,128)(2,1)S(1)}, u32[]{:S(2)}, u32[]{:S(2)}) %collective-permute-start.32) | collective-permute-done | bytes 1572896 | tf_op jit(solution)/shard_map/ppermute | solution.py:493
  202.9 5.5 %shard_map.95.factor_ref = bf16[6144,512]{1,0:T(8,128)(2,1)} custom-call(s32[3]{0:T(128)S(1)} %pad_add_fusion.1.at_ref, bf16[768,512]{1,0:T(8,128)(2,1)S(1)} %copy-done.2, bf16[768,512]{1,0:T(8,128)(2,1)} %collective-permute-done.2.refs_1_, bf16[768,512]{1,0:T(8,128)(2,1)} %collective-permute-done.3.refs_2_, bf16[768,512]{1,0:T(8,128)(2,1)S(1)} %copy-done.6, ...), custom_call_target="tpu_custom_call" | custom-call | flops 1 | bytes 1 | tf_op jit(solution)/shard_map/pallas_call | solution.py:96
  208.4 13.7 %collective-permute-done.34.refs_1_ = bf16[576,2048]{1,0:T(8,128)(2,1)S(1)} collective-permute-done((bf16[576,2048]{1,0:T(8,128)(2,1)}, bf16[576,2048]{1,0:T(8,128)(2,1)S(1)}, u32[]{:S(2)}, u32[]{:S(2)}) %collective-permute-start.34) | collective-permute-done | bytes 2359328 | tf_op jit(solution)/shard_map/ppermute | solution.py:319
  222.1 5.3 %shard_map.99 = bf16[256,3072]{1,0:T(8,128)(2,1)} custom-call(s32[3]{0:T(128)S(1)} %pad_add_fusion.1.at_ref, bf16[6144,3072]{1,0:T(8,128)(2,1)} %bitcast.50, bf16[6144,512]{1,0:T(8,128)(2,1)} %shard_map.95.factor_ref, bf16[3072,512]{1,0:T(8,128)(2,1)S(1)} %copy-done), custom_call_target="tpu_custom_call" | custom-call | flops 1 | bytes 1 | tf_op jit(solution)/shard_map/pallas_call | solution.py:36
  233.3 4.6 %collective-permute-start.36 = (bf16[576,512]{1,0:T(8,128)(2,1)}, bf16[576,512]{1,0:T(8,128)(2,1)}, u32[]{:S(2)}, u32[]{:S(2)}) collective-permute-start(bf16[576,512]{1,0:T(8,128)(2,1)} %reshape.76.refs_0_), channel_id=1, source_target_pairs={{0,1},{1,2},{2,3},{4,5},{5,6},{6,7},{8,9},{9,10},{10,11},{12,13},{... | collective-permute-start | bytes 1769480 | tf_op jit(solution)/shard_map/ppermute | solution.py:248
  241.3 34.4 %shard_map.96.refs_4_ = f32[3072,3072]{1,0:T(8,128)} custom-call(s32[12]{0:T(128)S(1)} %iota.48.target_ref, s32[12]{0:T(128)S(1)} %get-tuple-element.148.own_ref, s32[12]{0:T(128)S(1)} %get-tuple-element.147.place_ref, bf16[6144,3072]{1,0:T(8,128)(2,1)} %bitcast.51, bf16[6144,512]{1,0:T(8,128)(2,1)} %shard_map.95.factor_ref, bf16[3072,512]{1,0:T(8,128)(2,1)S(1)} %copy-done, ...), custom_call_target="tpu_custom_call" | custom-call | flops 1 | bytes 1 | tf_op jit(solution)/shard_map/pallas_call | solution.py:125
  275.7 5.0 %shard_map.97 = bf16[256,3072]{1,0:T(8,128)(2,1)} custom-call(s32[3]{0:T(128)S(1)} %pad_add_fusion.1.at_ref, bf16[6144,3072]{1,0:T(8,128)(2,1)} %bitcast.52, bf16[6144,512]{1,0:T(8,128)(2,1)} %shard_map.95.factor_ref, bf16[3072,512]{1,0:T(8,128)(2,1)S(1)} %copy-done), custom_call_target="tpu_custom_call" | custom-call | flops 1 | bytes 1 | tf_op jit(solution)/shard_map/pallas_call | solution.py:36
  285.3 10.1 %shard_map.100.refs_2_ = f32[3072,3072]{1,0:T(8,128)} custom-call(s32[3]{0:T(128)S(1)} %get-tuple-element.145.target_ref, s32[5,12]{1,0:T(8,128)S(1)} %stack.50.place_ref, bf16[768,768]{1,0:T(8,128)(2,1)S(1)} %copy-done.17, bf16[768,768]{1,0:T(8,128)(2,1)S(1)} %copy-done.19, bf16[768,768]{1,0:T(8,128)(2,1)S(1)} %copy-done.21, ...), custom_call_target="tpu_custom_call", output_to_operand_aliasing={{}: (6, {})} | custom-call | flops 1 | bytes 1 | tf_op jit(solution)/shard_map/pallas_call | solution.py:167
  295.5 10.2 %shard_map.106 = bf16[576,2048]{1,0:T(8,128)(2,1)} custom-call(s32[3]{0:T(128)S(1)} %pad_add_fusion.1.at_ref, bf16[6144,3072]{1,0:T(8,128)(2,1)} %bitcast.53, bf16[6144,512]{1,0:T(8,128)(2,1)} %shard_map.95.factor_ref, bf16[3072,512]{1,0:T(8,128)(2,1)S(1)} %copy-done), custom_call_target="tpu_custom_call" | custom-call | flops 1 | bytes 1 | tf_op jit(solution)/shard_map/pallas_call | solution.py:36
  310.5 7.8 %collective-permute-done.33.refs_0_ = bf16[256,3072]{1,0:T(8,128)(2,1)} collective-permute-done((bf16[256,3072]{1,0:T(8,128)(2,1)}, bf16[256,3072]{1,0:T(8,128)(2,1)}, u32[]{:S(2)}, u32[]{:S(2)}) %collective-permute-start.33) | collective-permute-done | bytes 1572896 | tf_op jit(solution)/shard_map/ppermute | solution.py:319
  318.3 5.0 %shard_map.101 = bf16[256,3072]{1,0:T(8,128)(2,1)} custom-call(s32[3]{0:T(128)S(1)} %pad_add_fusion.1.at_ref, bf16[6144,3072]{1,0:T(8,128)(2,1)} %bitcast.54, bf16[6144,512]{1,0:T(8,128)(2,1)} %shard_map.95.factor_ref, bf16[3072,512]{1,0:T(8,128)(2,1)S(1)} %copy-done), custom_call_target="tpu_custom_call" | custom-call | flops 1 | bytes 1 | tf_op jit(solution)/shard_map/pallas_call | solution.py:36
  329.0 2.6 shard_map.103
  333.6 3.1 pad_maximum_fusion.front_ref
  342.3 8.8 %shard_map.105.refs_0_ = bf16[1152,1024]{1,0:T(8,128)(2,1)S(1)} custom-call(s32[3]{0:T(128)S(1)} %pad_add_fusion.1.at_ref, bf16[1152,1024]{1,0:T(8,128)(2,1)} %pad_maximum_fusion.front_ref, bf16[1152,512]{1,0:T(8,128)(2,1)S(1)} %shard_map.102.factor_ref, bf16[1024,512]{1,0:T(8,128)(2,1)S(1)} %shard_map.104.col_ref), custom_call_target="tpu_custom_call" | custom-call | flops 1 | bytes 1 | tf_op jit(solution)/shard_map/pallas_call | solution.py:36
  351.1 10.3 %shard_map.107.refs_1_ = f32[3072,3072]{1,0:T(8,128)} custom-call(s32[3]{0:T(128)S(1)} %get-tuple-element.143.target_ref, s32[3,12]{1,0:T(4,128)S(1)} %pad_add_fusion.place_ref, bf16[1152,1024]{1,0:T(8,128)(2,1)S(1)} %shard_map.105.refs_0_, bf16[576,2048]{1,0:T(8,128)(2,1)S(1)} %copy-done.15, ...), custom_call_target="tpu_custom_call", output_to_operand_aliasing={{}: (4, {})} | custom-call | flops 1 | bytes 1 | tf_op jit(solution)/shard_map/pallas_call | solution.py:167
  361.5 5.5 %shard_map.108.refs_1_ = f32[3072,3072]{1,0:T(8,128)} custom-call(s32[1]{0:T(128)} %bitcast.21.target_ref, s32[2,12]{1,0:T(2,128)S(1)} %stack.47.place_ref, bf16[192,3072]{1,0:T(8,128)(2,1)} %collective-permute-done.29.refs_0_, f32[3072,3072]{1,0:T(8,128)} %shard_map.107.refs_1_), custom_call_target="tpu_custom_call", output_to_operand_aliasing={{}: (3, {})} | custom-call | flops 1 | bytes 1 | tf_op jit(solution)/shard_map/pallas_call | solution.py:167
  366.9 4.9 %shard_map.109.refs_1_ = f32[3072,3072]{1,0:T(8,128)} custom-call(s32[1]{0:T(128)} %bitcast.20.target_ref, s32[2,12]{1,0:T(2,128)S(1)} %stack.47.place_ref, bf16[256,3072]{1,0:T(8,128)(2,1)} %collective-permute-done.35.refs_0_, f32[3072,3072]{1,0:T(8,128)} %shard_map.108.refs_1_), custom_call_target="tpu_custom_call", output_to_operand_aliasing={{}: (3, {})} | custom-call | flops 1 | bytes 1 | tf_op jit(solution)/shard_map/pallas_call | solution.py:167
  371.8 4.7 %shard_map.114 = bf16[128,3072]{1,0:T(8,128)(2,1)} custom-call(s32[3]{0:T(128)S(1)} %pad_add_fusion.1.at_ref, bf16[6144,3072]{1,0:T(8,128)(2,1)} %bitcast.55, bf16[6144,512]{1,0:T(8,128)(2,1)} %shard_map.95.factor_ref, bf16[3072,512]{1,0:T(8,128)(2,1)S(1)} %copy-done), custom_call_target="tpu_custom_call" | custom-call | flops 1 | bytes 1 | tf_op jit(solution)/shard_map/pallas_call | solution.py:36
  378.4 5.0 %shard_map.110.refs_2_ = f32[3072,3072]{1,0:T(8,128)} custom-call(s32[1]{0:T(128)} %bitcast.23.target_ref, s32[2,12]{1,0:T(2,128)S(1)} %stack.47.place_ref, bf16[256,3072]{1,0:T(8,128)(2,1)} %collective-permute-done.33.refs_0_, f32[3072,3072]{1,0:T(8,128)} %shard_map.109.refs_1_), custom_call_target="tpu_custom_call", output_to_operand_aliasing={{}: (3, {})} | custom-call | flops 1 | bytes 1 | tf_op jit(solution)/shard_map/pallas_call | solution.py:167
  383.4 10.7 %shard_map.111.base_ref = f32[3072,3072]{1,0:T(8,128)} custom-call(s32[3]{0:T(128)S(1)} %get-tuple-element.144.target_ref, s32[3,12]{1,0:T(4,128)S(1)} %pad_add_fusion.place_ref, bf16[1152,1024]{1,0:T(8,128)(2,1)S(1)} %shard_map.105.refs_0_, bf16[576,2048]{1,0:T(8,128)(2,1)} %collective-permute-done.44.refs_1_, ...), custom_call_target="tpu_custom_call", output_to_operand_aliasing={{}: (4, {})} | custom-call | flops 1 | bytes 1 | tf_op jit(solution)/shard_map/pallas_call | solution.py:167
  394.1 8.4 %collective-permute-done.38.piece_ref = bf16[256,3072]{1,0:T(8,128)(2,1)} collective-permute-done((bf16[256,3072]{1,0:T(8,128)(2,1)}, bf16[256,3072]{1,0:T(8,128)(2,1)}, u32[]{:S(2)}, u32[]{:S(2)}) %collective-permute-start.38) | collective-permute-done | bytes 1572896 | tf_op jit(solution)/shard_map/ppermute | solution.py:319
  402.5 3.5 shard_map.112
  406.3 2.6 maximum_bitcast_fusion
  409.0 6.8 %shard_map.113 = (f32[3072,3072]{1,0:T(8,128)}, f32[64,3072]{1,0:T(8,128)S(1)}) custom-call(s32[2]{0:T(128)S(1)} %fusion.22.target_ref, s32[2,12]{1,0:T(2,128)S(1)} %stack.47.place_ref, bf16[256,3072]{1,0:T(8,128)(2,1)} %collective-permute-done.38.piece_ref, f32[3072,3072]{1,0:T(8,128)} %shard_map.111.base_ref), custom_call_target="tpu_custom_call", output_to_operand_aliasing={{0}: (3, {})} | custom-call | flops 1 | bytes 1 | tf_op jit(solution)/shard_map/pallas_call | solution.py:198
  415.8 3.6 collective-permute-done.46.refs_0_
  419.4 4.2 shard_map.115.base_ref
  (191 shorter events, 91.9 us)
Async XLA Ops:
  2.5 21.4 %collective-permute-start.4 = (bf16[384,1024]{1,0:T(8,128)(2,1)S(1)}, bf16[384,1024]{1,0:T(8,128)(2,1)S(1)}, u32[]{:S(2)}, u32[]{:S(2)}) collective-permute-start(bf16[384,1024]{1,0:T(8,128)(2,1)S(1)} %shard_map.77), channel_id=1, source_target_pairs={{0,8},{8,0},{16,24},{24,16},{1,9},{9,1},{17,25},{25,17},{2,10},{10... | collective-permute-start | bytes 2359304 | tf_op jit(solution)/shard_map/ppermute | solution.py:319
  7.5 20.0 %collective-permute-start.2 = (bf16[768,512]{1,0:T(8,128)(2,1)S(1)}, bf16[768,512]{1,0:T(8,128)(2,1)}, u32[]{:S(2)}, u32[]{:S(2)}) collective-permute-start(bf16[768,512]{1,0:T(8,128)(2,1)S(1)} %convolution_convert_fusion.1.refs_0_), channel_id=1, source_target_pairs={{0,1},{1,2},{2,3},{4,5},{5,6},{6,7},{8,9},{9,10},{10,11},{12,13},{... | collective-permute-start | bytes 2359304 | tf_op jit(solution)/shard_map/ppermute | solution.py:248
  11.9 20.7 %collective-permute-start.3 = (bf16[768,512]{1,0:T(8,128)(2,1)S(1)}, bf16[768,512]{1,0:T(8,128)(2,1)}, u32[]{:S(2)}, u32[]{:S(2)}) collective-permute-start(bf16[768,512]{1,0:T(8,128)(2,1)S(1)} %convolution_convert_fusion.1.refs_0_), channel_id=1, source_target_pairs={{1,0},{2,1},{3,2},{5,4},{6,5},{7,6},{9,8},{10,9},{11,10},{13,12},{... | collective-permute-start | bytes 2359304 | tf_op jit(solution)/shard_map/ppermute | solution.py:248
  15.8 33.4 %collective-permute-start.1 = (bf16[576,1024]{1,0:T(8,128)(2,1)}, bf16[576,1024]{1,0:T(8,128)(2,1)}, u32[]{:S(2)}, u32[]{:S(2)}) collective-permute-start(bf16[576,1024]{1,0:T(8,128)(2,1)} %shard_map.79), channel_id=1, source_target_pairs={{0,8},{8,0},{16,24},{24,16},{1,9},{9,1},{17,25},{25,17},{2,10},{10... | collective-permute-start | bytes 3538952 | tf_op jit(solution)/shard_map/ppermute | solution.py:319
  23.9 10.3 %collective-permute-start.5 = (s32[48]{0:T(128)S(1)}, s32[48]{0:T(128)S(1)}, u32[]{:S(2)}, u32[]{:S(2)}) collective-permute-start(s32[48]{0:T(128)S(1)} %bitcast.63), channel_id=1, source_target_pairs={{0,4},{4,0},{1,5},{5,1},{2,6},{6,2},{3,7},{7,3},{8,12},{12,8},{9,1... | collective-permute-start | bytes 584 | tf_op jit(solution)/shard_map/ppermute | solution.py:257
  34.1 16.3 %collective-permute-start.9 = (bf16[768,512]{1,0:T(8,128)(2,1)}, bf16[768,512]{1,0:T(8,128)(2,1)}, u32[]{:S(2)}, u32[]{:S(2)}) collective-permute-start(bf16[768,512]{1,0:T(8,128)(2,1)} %shard_map.81.refs_0_), channel_id=1, source_target_pairs={{0,4},{4,0},{1,5},{5,1},{2,6},{6,2},{3,7},{7,3},{8,12},{12,8},{9,1... | collective-permute-start | bytes 2359304 | tf_op jit(solution)/shard_map/ppermute | solution.py:257
  34.2 17.9 %collective-permute-start.7 = (bf16[768,512]{1,0:T(8,128)(2,1)}, bf16[768,512]{1,0:T(8,128)(2,1)S(1)}, u32[]{:S(2)}, u32[]{:S(2)}) collective-permute-start(bf16[768,512]{1,0:T(8,128)(2,1)} %collective-permute-done.2.refs_1_), channel_id=1, source_target_pairs={{1,2},{2,3},{5,6},{6,7},{9,10},{10,11},{13,14},{14,15},{17,18},{18... | collective-permute-start | bytes 2359304 | tf_op jit(solution)/shard_map/ppermute | solution.py:248
  34.9 24.6 %collective-permute-start.8 = (bf16[768,512]{1,0:T(8,128)(2,1)}, bf16[768,512]{1,0:T(8,128)(2,1)S(1)}, u32[]{:S(2)}, u32[]{:S(2)}) collective-permute-start(bf16[768,512]{1,0:T(8,128)(2,1)} %collective-permute-done.3.refs_2_), channel_id=1, source_target_pairs={{1,0},{2,1},{5,4},{6,5},{9,8},{10,9},{13,12},{14,13},{17,16},{18,1... | collective-permute-start | bytes 2359304 | tf_op jit(solution)/shard_map/ppermute | solution.py:248
  36.9 91.1 %copy-start.3 = (bf16[768,512]{1,0:T(8,128)(2,1)}, bf16[768,512]{1,0:T(8,128)(2,1)S(1)}, u32[]{:S(2)}) copy-start(bf16[768,512]{1,0:T(8,128)(2,1)S(1)} %convolution_convert_fusion.refs_0_.refs_5_) | copy-start | bytes 2359300
  41.1 29.4 %collective-permute-start = (bf16[488,1024]{1,0:T(8,128)(2,1)S(1)}, bf16[488,1024]{1,0:T(8,128)(2,1)S(1)}, u32[]{:S(2)}, u32[]{:S(2)}) collective-permute-start(bf16[488,1024]{1,0:T(8,128)(2,1)S(1)} %pad_maximum_fusion.1), channel_id=1, source_target_pairs={{0,8},{8,0},{16,24},{24,16},{1,9},{9,1},{17,25},{25,17},{2,10},{10... | collective-permute-start | bytes 2998280 | tf_op jit(solution)/shard_map/ppermute | solution.py:319
  49.3 1.1 collective-permute-start.6
  65.7 4.8 %collective-permute-start.10 = (bf16[768,512]{1,0:T(8,128)(2,1)S(1)}, bf16[768,512]{1,0:T(8,128)(2,1)S(1)}, u32[]{:S(2)}, u32[]{:S(2)}) collective-permute-start(bf16[768,512]{1,0:T(8,128)(2,1)S(1)} %shard_map.84.refs_0_), channel_id=1, source_target_pairs={{0,4},{4,0},{1,5},{5,1},{2,6},{6,2},{3,7},{7,3},{8,12},{12,8},{9,1... | collective-permute-start | bytes 2359304 | tf_op jit(solution)/shard_map/ppermute | solution.py:257
  65.8 5.3 %collective-permute-start.12 = (bf16[768,512]{1,0:T(8,128)(2,1)S(1)}, bf16[768,512]{1,0:T(8,128)(2,1)S(1)}, u32[]{:S(2)}, u32[]{:S(2)}) collective-permute-start(bf16[768,512]{1,0:T(8,128)(2,1)S(1)} %convolution_convert_fusion.refs_0_.refs_5_), channel_id=1, source_target_pairs={{0,4},{4,0},{1,5},{5,1},{2,6},{6,2},{3,7},{7,3},{8,12},{12,8},{9,1... | collective-permute-start | bytes 2359304 | tf_op jit(solution)/shard_map/ppermute | solution.py:257
  66.3 29.5 %collective-permute-start.16 = (bf16[768,768]{1,0:T(8,128)(2,1)S(1)}, bf16[768,768]{1,0:T(8,128)(2,1)S(1)}, u32[]{:S(2)}, u32[]{:S(2)}) collective-permute-start(bf16[768,768]{1,0:T(8,128)(2,1)S(1)} %shard_map.83), channel_id=1, source_target_pairs={{0,8},{8,0},{16,24},{24,16},{1,9},{9,1},{17,25},{25,17},{2,10},{10... | collective-permute-start | bytes 3538952 | tf_op jit(solution)/shard_map/ppermute | solution.py:319
  70.5 1.1 collective-permute-start.11
  71.6 26.4 %collective-permute-start.13 = (bf16[768,512]{1,0:T(8,128)(2,1)S(1)}, bf16[768,512]{1,0:T(8,128)(2,1)S(1)}, u32[]{:S(2)}, u32[]{:S(2)}) collective-permute-start(bf16[768,512]{1,0:T(8,128)(2,1)S(1)} %convolution_convert_fusion.refs_0_.refs_5_), channel_id=1, source_target_pairs={{0,1},{1,2},{2,3},{4,5},{5,6},{6,7},{8,9},{9,10},{10,11},{12,13},{... | collective-permute-start | bytes 2359304 | tf_op jit(solution)/shard_map/ppermute | solution.py:248
  75.5 22.5 %collective-permute-start.14 = (bf16[768,512]{1,0:T(8,128)(2,1)S(1)}, bf16[768,512]{1,0:T(8,128)(2,1)S(1)}, u32[]{:S(2)}, u32[]{:S(2)}) collective-permute-start(bf16[768,512]{1,0:T(8,128)(2,1)S(1)} %convolution_convert_fusion.refs_0_.refs_5_), channel_id=1, source_target_pairs={{1,0},{2,1},{3,2},{5,4},{6,5},{7,6},{9,8},{10,9},{11,10},{13,12},{... | collective-permute-start | bytes 2359304 | tf_op jit(solution)/shard_map/ppermute | solution.py:248
  76.8 21.2 %collective-permute-start.15 = (bf16[768,512]{1,0:T(8,128)(2,1)S(1)}, bf16[768,512]{1,0:T(8,128)(2,1)S(1)}, u32[]{:S(2)}, u32[]{:S(2)}) collective-permute-start(bf16[768,512]{1,0:T(8,128)(2,1)S(1)} %convolution_convert_fusion.refs_0_.refs_5_), channel_id=1, source_target_pairs={{2,5},{5,2},{10,13},{13,10},{18,21},{21,18},{26,29},{29,26}} | collective-permute-start | bytes 2359304 | tf_op jit(solution)/shard_map/ppermute | solution.py:444
  81.3 39.7 %collective-permute-start.21 = (bf16[768,768]{1,0:T(8,128)(2,1)S(1)}, bf16[768,768]{1,0:T(8,128)(2,1)S(1)}, u32[]{:S(2)}, u32[]{:S(2)}) collective-permute-start(bf16[768,768]{1,0:T(8,128)(2,1)S(1)} %shard_map.87), channel_id=1, source_target_pairs={{0,8},{8,0},{16,24},{24,16},{1,9},{9,1},{17,25},{25,17},{2,10},{10... | collective-permute-start | bytes 3538952 | tf_op jit(solution)/shard_map/ppermute | solution.py:319
  95.7 1.1 collective-permute-start.17
  96.9 1.1 collective-permute-start.18
  98.0 25.5 %collective-permute-start.19 = (bf16[768,512]{1,0:T(8,128)(2,1)S(1)}, bf16[768,512]{1,0:T(8,128)(2,1)S(1)}, u32[]{:S(2)}, u32[]{:S(2)}) collective-permute-start(bf16[768,512]{1,0:T(8,128)(2,1)S(1)} %collective-permute-done.13.refs_1_.refs_6_), channel_id=1, source_target_pairs={{1,2},{2,3},{5,6},{6,7},{9,10},{10,11},{13,14},{14,15},{17,18},{18... | collective-permute-start | bytes 2359304 | tf_op jit(solution)/shard_map/ppermute | solution.py:248
  98.7 29.2 %collective-permute-start.20 = (bf16[768,512]{1,0:T(8,128)(2,1)S(1)}, bf16[768,512]{1,0:T(8,128)(2,1)S(1)}, u32[]{:S(2)}, u32[]{:S(2)}) collective-permute-start(bf16[768,512]{1,0:T(8,128)(2,1)S(1)} %collective-permute-done.14.refs_2_.refs_7_), channel_id=1, source_target_pairs={{1,0},{2,1},{5,4},{6,5},{9,8},{10,9},{13,12},{14,13},{17,16},{18,1... | collective-permute-start | bytes 2359304 | tf_op jit(solution)/shard_map/ppermute | solution.py:248
  104.5 41.8 %collective-permute-start.30 = (bf16[768,768]{1,0:T(8,128)(2,1)S(1)}, bf16[768,768]{1,0:T(8,128)(2,1)S(1)}, u32[]{:S(2)}, u32[]{:S(2)}) collective-permute-start(bf16[768,768]{1,0:T(8,128)(2,1)S(1)} %shard_map.93), channel_id=1, source_target_pairs={{0,8},{8,0},{16,24},{24,16},{1,9},{9,1},{17,25},{25,17},{2,10},{10... | collective-permute-start | bytes 3538952 | tf_op jit(solution)/shard_map/ppermute | solution.py:319
  121.0 1.1 collective-permute-start.22
  122.1 1.1 collective-permute-start.23
  123.3 5.4 %collective-permute-start.24 = (s32[48]{0:T(128)S(1)}, s32[48]{0:T(128)S(1)}, u32[]{:S(2)}, u32[]{:S(2)}) collective-permute-start(s32[48]{0:T(128)S(1)} %collective-permute-done.23), channel_id=1, source_target_pairs={{0,4},{4,0},{1,5},{5,1},{2,6},{6,2},{3,7},{7,3},{8,12},{12,8},{9,1... | collective-permute-start | bytes 584 | tf_op jit(solution)/shard_map/ppermute | solution.py:257
  128.7 2.4 collective-permute-start.25
  136.4 35.2 %collective-permute-start.26 = (bf16[768,768]{1,0:T(8,128)(2,1)}, bf16[768,768]{1,0:T(8,128)(2,1)}, u32[]{:S(2)}, u32[]{:S(2)}) collective-permute-start(bf16[768,768]{1,0:T(8,128)(2,1)} %shard_map.89), channel_id=1, source_target_pairs={{0,8},{8,0},{16,24},{24,16},{1,9},{9,1},{17,25},{25,17},{2,10},{10... | collective-permute-start | bytes 3538952 | tf_op jit(solution)/shard_map/ppermute | solution.py:319
  146.3 1.1 collective-permute-start.31
  161.1 61.1 %collective-permute-start.34 = (bf16[576,2048]{1,0:T(8,128)(2,1)}, bf16[576,2048]{1,0:T(8,128)(2,1)S(1)}, u32[]{:S(2)}, u32[]{:S(2)}) collective-permute-start(bf16[576,2048]{1,0:T(8,128)(2,1)} %shard_map.98), channel_id=1, source_target_pairs={{0,8},{8,0},{16,24},{24,16},{1,9},{9,1},{17,25},{25,17},{2,10},{10... | collective-permute-start | bytes 7077896 | tf_op jit(solution)/shard_map/ppermute | solution.py:319
  163.6 38.1 %collective-permute-start.32 = (bf16[1536,512]{1,0:T(8,128)(2,1)S(1)}, bf16[1536,512]{1,0:T(8,128)(2,1)S(1)}, u32[]{:S(2)}, u32[]{:S(2)}) collective-permute-start(bf16[1536,512]{1,0:T(8,128)(2,1)S(1)} %shard_map.94), channel_id=1, source_target_pairs={{2,3},{1,0},{6,7},{5,4},{10,11},{9,8},{14,15},{13,12},{18,19},{17,... | collective-permute-start | bytes 4718600 | tf_op jit(solution)/shard_map/ppermute | solution.py:493
  171.7 2.0 collective-permute-start.27
  173.7 2.0 collective-permute-start.28
  180.5 95.1 %collective-permute-start.29 = (bf16[192,3072]{1,0:T(8,128)(2,1)}, bf16[192,3072]{1,0:T(8,128)(2,1)}, u32[]{:S(2)}, u32[]{:S(2)}) collective-permute-start(bf16[192,3072]{1,0:T(8,128)(2,1)} %shard_map.92), channel_id=1, source_target_pairs={{0,8},{8,0},{16,24},{24,16},{1,9},{9,1},{17,25},{25,17},{2,10},{10... | collective-permute-start | bytes 3538952 | tf_op jit(solution)/shard_map/ppermute | solution.py:319
  227.4 68.0 %collective-permute-start.35 = (bf16[256,3072]{1,0:T(8,128)(2,1)}, bf16[256,3072]{1,0:T(8,128)(2,1)}, u32[]{:S(2)}, u32[]{:S(2)}) collective-permute-start(bf16[256,3072]{1,0:T(8,128)(2,1)} %shard_map.99), channel_id=1, source_target_pairs={{0,8},{8,0},{16,24},{24,16},{1,9},{9,1},{17,25},{25,17},{2,10},{10... | collective-permute-start | bytes 4718600 | tf_op jit(solution)/shard_map/ppermute | solution.py:319
  233.3 48.2 %collective-permute-start.36 = (bf16[576,512]{1,0:T(8,128)(2,1)}, bf16[576,512]{1,0:T(8,128)(2,1)}, u32[]{:S(2)}, u32[]{:S(2)}) collective-permute-start(bf16[576,512]{1,0:T(8,128)(2,1)} %reshape.76.refs_0_), channel_id=1, source_target_pairs={{0,1},{1,2},{2,3},{4,5},{5,6},{6,7},{8,9},{9,10},{10,11},{12,13},{... | collective-permute-start | bytes 1769480 | tf_op jit(solution)/shard_map/ppermute | solution.py:248
  237.9 43.6 %collective-permute-start.37 = (bf16[576,512]{1,0:T(8,128)(2,1)}, bf16[576,512]{1,0:T(8,128)(2,1)}, u32[]{:S(2)}, u32[]{:S(2)}) collective-permute-start(bf16[576,512]{1,0:T(8,128)(2,1)} %reshape.76.refs_0_), channel_id=1, source_target_pairs={{1,0},{2,1},{3,2},{5,4},{6,5},{7,6},{9,8},{10,9},{11,10},{13,12},{... | collective-permute-start | bytes 1769480 | tf_op jit(solution)/shard_map/ppermute | solution.py:248
  280.6 37.6 %collective-permute-start.33 = (bf16[256,3072]{1,0:T(8,128)(2,1)}, bf16[256,3072]{1,0:T(8,128)(2,1)}, u32[]{:S(2)}, u32[]{:S(2)}) collective-permute-start(bf16[256,3072]{1,0:T(8,128)(2,1)} %shard_map.97), channel_id=1, source_target_pairs={{0,8},{8,0},{16,24},{24,16},{1,9},{9,1},{17,25},{25,17},{2,10},{10... | collective-permute-start | bytes 4718600 | tf_op jit(solution)/shard_map/ppermute | solution.py:319
  305.7 66.2 %collective-permute-start.44 = (bf16[576,2048]{1,0:T(8,128)(2,1)}, bf16[576,2048]{1,0:T(8,128)(2,1)}, u32[]{:S(2)}, u32[]{:S(2)}) collective-permute-start(bf16[576,2048]{1,0:T(8,128)(2,1)} %shard_map.106), channel_id=1, source_target_pairs={{0,8},{8,0},{16,24},{24,16},{1,9},{9,1},{17,25},{25,17},{2,10},{10... | collective-permute-start | bytes 7077896 | tf_op jit(solution)/shard_map/ppermute | solution.py:319
  307.5 15.9 %collective-permute-start.39 = (bf16[576,512]{1,0:T(8,128)(2,1)}, bf16[576,512]{1,0:T(8,128)(2,1)}, u32[]{:S(2)}, u32[]{:S(2)}) collective-permute-start(bf16[576,512]{1,0:T(8,128)(2,1)} %collective-permute-done.36.refs_1_), channel_id=1, source_target_pairs={{1,2},{2,3},{5,6},{6,7},{9,10},{10,11},{13,14},{14,15},{17,18},{18... | collective-permute-start | bytes 1769480 | tf_op jit(solution)/shard_map/ppermute | solution.py:248
  309.2 16.4 %collective-permute-start.40 = (bf16[576,512]{1,0:T(8,128)(2,1)}, bf16[576,512]{1,0:T(8,128)(2,1)}, u32[]{:S(2)}, u32[]{:S(2)}) collective-permute-start(bf16[576,512]{1,0:T(8,128)(2,1)} %collective-permute-done.37.refs_2_), channel_id=1, source_target_pairs={{1,0},{2,1},{5,4},{6,5},{9,8},{10,9},{13,12},{14,13},{17,16},{18,1... | collective-permute-start | bytes 1769480 | tf_op jit(solution)/shard_map/ppermute | solution.py:248
  323.3 79.3 %collective-permute-start.38 = (bf16[256,3072]{1,0:T(8,128)(2,1)}, bf16[256,3072]{1,0:T(8,128)(2,1)}, u32[]{:S(2)}, u32[]{:S(2)}) collective-permute-start(bf16[256,3072]{1,0:T(8,128)(2,1)} %shard_map.101), channel_id=1, source_target_pairs={{0,8},{8,0},{16,24},{24,16},{1,9},{9,1},{17,25},{25,17},{2,10},{10... | collective-permute-start | bytes 4718600 | tf_op jit(solution)/shard_map/ppermute | solution.py:319
  327.5 13.1 %collective-permute-start.41 = (bf16[576,512]{1,0:T(8,128)(2,1)}, bf16[576,512]{1,0:T(8,128)(2,1)}, u32[]{:S(2)}, u32[]{:S(2)}) collective-permute-start(bf16[576,512]{1,0:T(8,128)(2,1)} %broadcast_select_fusion), channel_id=1, source_target_pairs={{2,3},{1,0},{6,7},{5,4},{10,11},{9,8},{14,15},{13,12},{18,19},{17,... | collective-permute-start | bytes 1769480 | tf_op jit(solution)/shard_map/ppermute | solution.py:513
  331.6 5.1 %collective-permute-start.42 = (bf16[512,512]{1,0:T(8,128)(2,1)}, bf16[512,512]{1,0:T(8,128)(2,1)}, u32[]{:S(2)}, u32[]{:S(2)}) collective-permute-start(bf16[512,512]{1,0:T(8,128)(2,1)} %get-tuple-element.112.refs_0_), channel_id=1, source_target_pairs={{0,4},{4,0},{1,5},{5,1},{2,6},{6,2},{3,7},{7,3},{8,12},{12,8},{9,1... | collective-permute-start | bytes 1572872 | tf_op jit(solution)/shard_map/ppermute | solution.py:257
  331.7 5.0 %collective-permute-start.43 = (bf16[512,512]{1,0:T(8,128)(2,1)}, bf16[512,512]{1,0:T(8,128)(2,1)}, u32[]{:S(2)}, u32[]{:S(2)}) collective-permute-start(bf16[512,512]{1,0:T(8,128)(2,1)} %get-tuple-element.113.refs_1_), channel_id=1, source_target_pairs={{0,4},{4,0},{1,5},{5,1},{2,6},{6,2},{3,7},{7,3},{8,12},{12,8},{9,1... | collective-permute-start | bytes 1572872 | tf_op jit(solution)/shard_map/ppermute | solution.py:257
  376.6 42.8 %collective-permute-start.46 = (bf16[128,3072]{1,0:T(8,128)(2,1)}, bf16[128,3072]{1,0:T(8,128)(2,1)}, u32[]{:S(2)}, u32[]{:S(2)}) collective-permute-start(bf16[128,3072]{1,0:T(8,128)(2,1)} %shard_map.114), channel_id=1, source_target_pairs={{0,8},{8,0},{16,24},{24,16},{1,9},{9,1},{17,25},{25,17},{2,10},{10... | collective-permute-start | bytes 2359304 | tf_op jit(solution)/shard_map/ppermute | solution.py:319
  406.1 17.8 %collective-permute-start.45 = (bf16[64,3072]{1,0:T(8,128)(2,1)S(1)}, bf16[64,3072]{1,0:T(8,128)(2,1)S(1)}, u32[]{:S(2)}, u32[]{:S(2)}) collective-permute-start(bf16[64,3072]{1,0:T(8,128)(2,1)S(1)} %shard_map.112), channel_id=1, source_target_pairs={{0,8},{8,0},{16,24},{24,16},{1,9},{9,1},{17,25},{25,17},{2,10},{10... | collective-permute-start | bytes 1179656 | tf_op jit(solution)/shard_map/ppermute | solution.py:319
  (34 other events, 464.6 us)
